TPU v7x, 32 devices: a whole 2x2x4 slice. The times are simulated.
32 devices in a mesh: pair: 8 (over z, x), aux: 4 (over y, core).
Axes of the slice: x: 2, y: 2, z: 4, core: 2. Of those that a mesh axis runs over, the one named last changes fastest.
Arguments:
- factor: float32 [131072, 4096], P('pair', 'aux'), may hold values from -0.015625 to 0.015625
- trials: float32 [256, 131072], P('aux', 'pair'), may hold values from -6 to 6
- stored: float32 [384, 131072], P(None, 'pair'), may hold values from -0.015625 to 0.015625
- energy_gaps: float32 [131072], P('pair'), may hold values from 0.35 to 7
Outputs:
- next_trials: float32 [256, 131072], P('aux', 'pair')
- projections: float32 [2, 384, 256], P(None, None, 'aux')
All inputs are finite; a program needn't handle non-finite values.
Results may differ from a plain program's by a relative error of at most 0.0001.
Values sent between devices are 32-bit elements; how exact they have to be, the bound alone decides.
No kernel may reach another device: no remote copies, remote signals or barrier semaphores. Data moves between devices by JAX's collectives and lax.ppermute only.
A program may use at most 192 MiB of HBM per device.

v0:
```python
import jax
import jax.numpy as jnp
from jax import lax
from jax.sharding import PartitionSpec as P

PAIRS = 131072
ROUNDS = 2


def on_device(factor, trials, stored, energy_gaps):
    highest = lax.Precision.HIGHEST
    own_rows = trials
    row_norms = jnp.ones((trials.shape[0],), jnp.float32)
    collected = []
    for turn_index in range(ROUNDS):
        everything, every_norm = (
            lax.all_gather(own_rows, "aux", axis=0, tiled=True),
            lax.all_gather(row_norms, "aux", axis=0, tiled=True),
        )
        true_rows = own_rows / row_norms[:, None]
        partial_value = jnp.dot(
            everything, factor, precision=highest, preferred_element_type=jnp.float32
        )
        partial_value = partial_value / every_norm[:, None]
        fitted = lax.psum(partial_value, "pair")
        spread = lax.dot_general(
            fitted,
            factor,
            (((1,), (1,)), ((), ())),
            precision=highest,
            preferred_element_type=jnp.float32,
        )
        own_response = lax.psum_scatter(4.0 * spread, "aux", scatter_dimension=0, tiled=True)
        response = energy_gaps[None, :] * true_rows + own_response
        local_intersection = lax.dot_general(
            stored,
            response,
            (((1,), (1,)), ((), ())),
            precision=highest,
            preferred_element_type=jnp.float32,
        )
        projection = lax.psum(local_intersection, "pair")
        removed = lax.dot_general(
            projection,
            stored,
            (((0,), (0,)), ((), ())),
            precision=highest,
            preferred_element_type=jnp.float32,
        )
        scaled = (response - removed) / energy_gaps[None, :]
        square_sum = lax.psum(jnp.sum(scaled * scaled, axis=1), "pair")
        row_norms = jnp.sqrt(square_sum / PAIRS + 1e-06)
        if turn_index + 1 < ROUNDS:
            own_rows = scaled
        else:
            own_rows = scaled / row_norms[:, None]
        collected.append(projection)
    return (own_rows, jnp.stack(collected))


def solution(mesh):
    in_specs = (P("pair", "aux"), P("aux", "pair"), P(None, "pair"), P("pair"))
    out_specs = (P("aux", "pair"), P(None, None, "aux"))
    return jax.shard_map(
        on_device, mesh=mesh, in_specs=in_specs, out_specs=out_specs, check_vma=False
    )
```

profile of v0, /device:TPU:0, one launch (start us, length us, event | category | flops | bytes accessed | tf_op | source)
XLA Modules:
  0.0 1157.7 jit_solution(7700355333763849071)
XLA Ops:
  7.2 0.0 all-gather.3.cloned.1.call-start
  7.2 0.7 all-gather.3.cloned.1.call-update
  7.9 0.0 all-reduce.6.cloned.1.call-start
  7.9 110.3 %all-gather.3.cloned.1.call-done = f32[256,16384]{1,0:T(8,128)} async-done(((f32[64,16384]{1,0:T(8,128)}), f32[256,16384]{1,0:T(8,128)}) %all-gather.3.cloned.1.call-update) | async-done | bytes 16777232 | tf_op jit(solution)/shard_map/all_gather | solution.py:17
  118.2 63.1 %fusion.3 = f32[256,1024]{1,0:T(8,128)} fusion(f32[256,16384]{1,0:T(8,128)} %all-gather.3.cloned.1.call-done, f32[16384,1024]{1,0:T(8,128)} %param.4), kind=kOutput, calls=%fused_computation.18 | convolution fusion | flops 51539607552 | bytes 84934656 | tf_op jit(solution)/shard_map/dot_general | solution.py:21
  181.3 0.0 all-reduce.6.cloned.1.call-update
  181.3 0.3 reduce-scatter.3.cloned.1.call-start
  181.6 78.0 %all-reduce.6.cloned.1.call-done = f32[256,1024]{1,0:T(8,128)} async-done(((f32[256,1024]{1,0:T(8,128)}), f32[256,1024]{1,0:T(8,128)}) %all-reduce.6.cloned.1.call-update) | async-done | bytes 1048592 | tf_op jit(solution)/shard_map/psum | solution.py:25
  259.6 61.7 %convolution_multiply_fusion.1 = f32[256,16384]{1,0:T(8,128)} fusion(f32[256,1024]{1,0:T(8,128)} %all-reduce.6.cloned.1.call-done, f32[16384,1024]{1,0:T(8,128)} %param.4), kind=kOutput, calls=%fused_computation.1 | convolution fusion | flops 51543801856 | bytes 84934656 | tf_op jit(solution)/shard_map/dot_general | solution.py:26
  321.3 0.0 copy-start
  321.3 0.0 reduce-scatter.3.cloned.1.call-update
  321.3 0.4 all-reduce.8.cloned.1.call-start
  321.7 125.5 %reduce-scatter.3.cloned.1.call-done = f32[64,16384]{1,0:T(8,128)} async-done(((f32[256,16384]{1,0:T(8,128)}), f32[64,16384]{1,0:T(8,128)}) %reduce-scatter.3.cloned.1.call-update) | async-done | bytes 4194320 | tf_op jit(solution)/shard_map/reduce_scatter | solution.py:33
  447.2 0.0 copy-done
  447.2 28.5 %fusion.1 = f32[384,64]{0,1:T(8,128)} fusion(f32[384,16384]{1,0:T(8,128)} %param.6, f32[64,16384]{1,0:T(8,128)} %reduce-scatter.3.cloned.1.call-done, f32[64,16384]{1,0:T(8,128)} %param.5, f32[16384]{0:T(1024)S(1)} %copy-done), kind=kOutput, calls=%fused_computation.12 | convolution fusion | flops 4833935360 | bytes 33718272 | tf_op jit(solution)/shard_map/dot_general | solution.py:35
  475.6 0.0 all-reduce.8.cloned.1.call-update
  475.7 0.6 all-gather.5.cloned.1.call-start
  476.3 68.9 %all-reduce.8.cloned.1.call-done = f32[384,64]{0,1:T(8,128)} async-done(((f32[384,64]{0,1:T(8,128)}), f32[384,64]{0,1:T(8,128)}) %all-reduce.8.cloned.1.call-update) | async-done | bytes 98320 | tf_op jit(solution)/shard_map/psum | solution.py:42
  545.2 23.9 %multiply_reduce_fusion.1 = (f32[64]{0:T(128)S(1)}, f32[64,16384]{1,0:T(8,128)}, f32[64,16384]{1,0:T(8,128)}) fusion(f32[16384]{0:T(1024)S(1)} %copy-done, f32[384,64]{0,1:T(8,128)} %all-reduce.8.cloned.1.call-done, f32[384,16384]{1,0:T(8,128)} %param.6, f32[64,16384]{1,0:T(8,128)} %reduce-scatter.3.cloned.1.call-done, f32[64,16384]{1,0:T(8,128)} %param.5), kind=kOutput, calls=%fused_computation.7 | convolution fusion | flops 4838129664 | bytes 42107136 | tf_op jit(solution)/shard_map/dot_general | solution.py:43
  569.1 0.0 copy-start.3
  569.1 0.0 all-gather.5.cloned.1.call-update
  569.1 0.0 all-reduce.10.cloned.1.call-start
  569.2 0.6 copy-done.3
  569.8 0.6 dynamic-slice
  571.0 19.5 %psum.44 = f32[64]{0:T(128)S(1)} all-reduce(f32[64]{0:T(128)S(1)} %get-tuple-element.2), channel_id=1, replica_groups=mesh['pair'=8,'aux'=4] {'pair'}, use_global_device_ids=true, to_apply=%region_4.0 | all-reduce | flops 64 | bytes 512 | tf_op jit(solution)/shard_map/psum | solution.py:51
  590.5 0.1 add_sqrt_fusion.1
  590.6 6.3 all-reduce
  596.9 77.5 %all-gather.5.cloned.1.call-done = f32[256,16384]{1,0:T(8,128)} async-done(((f32[64,16384]{1,0:T(8,128)}), f32[256,16384]{1,0:T(8,128)}) %all-gather.5.cloned.1.call-update) | async-done | bytes 16777232 | tf_op jit(solution)/shard_map/all_gather | solution.py:17
  674.4 63.2 %convolution_divide_fusion = f32[256,1024]{1,0:T(8,128)} fusion(f32[256,16384]{1,0:T(8,128)} %all-gather.5.cloned.1.call-done, f32[16384,1024]{1,0:T(8,128)} %param.4, f32[256]{0:T(256)S(1)} %all-reduce), kind=kOutput, calls=%fused_computation.11 | convolution fusion | flops 51539869696 | bytes 84935680 | tf_op jit(solution)/shard_map/dot_general | solution.py:21
  737.6 0.0 all-reduce.10.cloned.1.call-update
  737.6 0.3 reduce-scatter.5.cloned.1.call-start
  737.9 78.0 %all-reduce.10.cloned.1.call-done = f32[256,1024]{1,0:T(8,128)} async-done(((f32[256,1024]{1,0:T(8,128)}), f32[256,1024]{1,0:T(8,128)}) %all-reduce.10.cloned.1.call-update) | async-done | bytes 1048592 | tf_op jit(solution)/shard_map/psum | solution.py:25
  815.9 61.7 %convolution_multiply_fusion = f32[256,16384]{1,0:T(8,128)} fusion(f32[256,1024]{1,0:T(8,128)} %all-reduce.10.cloned.1.call-done, f32[16384,1024]{1,0:T(8,128)} %param.4), kind=kOutput, calls=%fused_computation | convolution fusion | flops 51543801856 | bytes 84934656 | tf_op jit(solution)/shard_map/dot_general | solution.py:26
  877.5 0.0 reduce-scatter.5.cloned.1.call-update
  877.6 0.3 all-reduce.12.cloned.1.call-start
  877.9 125.6 %reduce-scatter.5.cloned.1.call-done = f32[64,16384]{1,0:T(8,128)} async-done(((f32[256,16384]{1,0:T(8,128)}), f32[64,16384]{1,0:T(8,128)}) %reduce-scatter.5.cloned.1.call-update) | async-done | bytes 4194320 | tf_op jit(solution)/shard_map/reduce_scatter | solution.py:33
  1003.4 28.9 %convolution_bitcast_fusion = f32[384,64]{0,1:T(8,128)} fusion(f32[384,16384]{1,0:T(8,128)} %param.6, f32[64,16384]{1,0:T(8,128)} %reduce-scatter.5.cloned.1.call-done, f32[64,16384]{1,0:T(8,128)} %get-tuple-element.6, f32[64]{0:T(128)S(1)} %get-tuple-element.4, f32[16384]{0:T(1024)S(1)} %copy-done), kind=kOutput, calls=%fused_computation.13 | convolution fusion | flops 4836032512 | bytes 33718528 | tf_op jit(solution)/shard_map/dot_general | solution.py:35
  1032.4 0.0 all-reduce.12.cloned.1.call-update
  1032.4 69.6 %all-reduce.12.cloned.1.call-done = f32[384,64]{0,1:T(8,128)} async-done(((f32[384,64]{0,1:T(8,128)}), f32[384,64]{0,1:T(8,128)}) %all-reduce.12.cloned.1.call-update) | async-done | bytes 98320 | tf_op jit(solution)/shard_map/psum | solution.py:42
  1102.0 23.4 %multiply_reduce_fusion = (f32[64]{0:T(128)S(1)}, f32[64,16384]{1,0:T(8,128)}) fusion(f32[16384]{0:T(1024)S(1)} %copy-done, f32[384,64]{0,1:T(8,128)} %all-reduce.12.cloned.1.call-done, f32[384,16384]{1,0:T(8,128)} %param.6, f32[64,16384]{1,0:T(8,128)} %reduce-scatter.5.cloned.1.call-done, f32[64,16384]{1,0:T(8,128)} %get-tuple-element.6, ...), kind=kOutput, calls=%fused_computation.5 | convolution fusion | flops 4840226816 | bytes 37913088 | tf_op jit(solution)/shard_map/dot_general | solution.py:43
  1125.4 19.5 %psum.47 = f32[64]{0:T(128)S(1)} all-reduce(f32[64]{0:T(128)S(1)} %get-tuple-element.7), channel_id=1, replica_groups=mesh['pair'=8,'aux'=4] {'pair'}, use_global_device_ids=true, to_apply=%region_9.0 | all-reduce | flops 64 | bytes 512 | tf_op jit(solution)/shard_map/psum | solution.py:51
  1145.0 0.0 copy-start.1
  1145.0 0.0 copy-start.2
  1145.0 4.9 multiply_divide_fusion
  1149.8 0.0 copy-done.1
  1149.8 0.0 copy-done.2
  1149.8 0.7 pad_maximum_fusion
  (2 shorter events, 0.0 us)
Async XLA Ops:
  7.2 111.1 %all-gather.3.cloned.1.call-start = ((), (), s32[]{:S(2)}) async-start(), calls=%async_computation.2 | async-start | bytes 20971520 | tf_op jit(solution)/shard_map/all_gather | solution.py:17
  7.9 251.7 %all-reduce.6.cloned.1.call-start = ((), (), s32[]{:S(2)}) async-start(), calls=%async_computation.3 | async-start | bytes 2097152 | tf_op jit(solution)/shard_map/psum | solution.py:25
  181.3 265.9 %reduce-scatter.3.cloned.1.call-start = ((), (), s32[]{:S(2)}) async-start(), calls=%async_computation.4 | async-start | bytes 20971520 | tf_op jit(solution)/shard_map/reduce_scatter | solution.py:33
  321.3 125.9 %copy-start = (f32[16384]{0:T(1024)S(1)}, f32[16384]{0:T(1024)}, u32[]{:S(2)}) copy-start(f32[16384]{0:T(1024)} %param.7) | copy-start | bytes 196612
  321.3 223.9 %all-reduce.8.cloned.1.call-start = ((), (), s32[]{:S(2)}) async-start(), calls=%async_computation.5 | async-start | bytes 196608 | tf_op jit(solution)/shard_map/psum | solution.py:42
  475.7 198.7 %all-gather.5.cloned.1.call-start = ((), (), s32[]{:S(2)}) async-start(), calls=%async_computation.6 | async-start | bytes 20971520 | tf_op jit(solution)/shard_map/all_gather | solution.py:17
  569.1 0.7 copy-start.3
  569.1 246.8 %all-reduce.10.cloned.1.call-start = ((), (), s32[]{:S(2)}) async-start(), calls=%async_computation.7 | async-start | bytes 2097152 | tf_op jit(solution)/shard_map/psum | solution.py:25
  737.6 265.8 %reduce-scatter.5.cloned.1.call-start = ((), (), s32[]{:S(2)}) async-start(), calls=%async_computation.8 | async-start | bytes 20971520 | tf_op jit(solution)/shard_map/reduce_scatter | solution.py:33
  877.6 224.4 %all-reduce.12.cloned.1.call-start = ((), (), s32[]{:S(2)}) async-start(), calls=%async_computation.9 | async-start | bytes 196608 | tf_op jit(solution)/shard_map/psum | solution.py:42
  1145.0 4.9 copy-start.1
  1145.0 4.9 copy-start.2
Sparse Core Ops, SparseCore 0:
  9.6 108.6 all-gather.2
  181.4 78.1 all-reduce.5
  321.4 125.7 reduce-scatter.2
  475.8 69.4 all-reduce.7
  569.2 105.0 all-gather.4
  737.8 78.0 all-reduce.9
  877.7 125.7 reduce-scatter.4
  1032.5 69.4 all-reduce.11
where the time goes:
time: 1160 us
  waiting for transfers between devices  734 us (63%)
  matrix products  354 us (31%)
  blocking collectives  45.4 us (4%)
  between operations  15.1 us (1%)
    reduce_scatter x2, waiting for transfers between devices, on_device(): lax.psum_scatter(4.0 * spread, 'aux', scatter_dimension=0, tiled=True)  251 us
    all_gather x2, waiting for transfers between devices, on_device(): lax.all_gather(own_rows, 'aux', axis=0, tiled=True)  188 us
    psum x2, waiting for transfers between devices, on_device(): fitted = lax.psum(partial_value, 'pair')  156 us
    psum x2, waiting for transfers between devices, on_device(): projection = lax.psum(local_intersection, 'pair')  139 us
    dot_general x2, matrix products, on_device(): jnp.dot(everything, factor, precision=highest, preferred_element_type=jnp...  126 us
    dot_general x2, matrix products, on_device(): lax.dot_general(fitted, factor, (((1,), (1,)), ((), ())), precision=highe...  123 us
    dot_general x2, matrix products, on_device(): lax.dot_general(stored, response, (((1,), (1,)), ((), ())), precision=hig...  57.4 us
    dot_general x2, matrix products, on_device(): lax.dot_general(projection, stored, (((0,), (0,)), ((), ())), precision=h...  47.3 us
  transfers between devices with their start and end apart: 8, of which 8 were waited for; matrix products, arithmetic and copies ran while one was open for 0% of the time, Pallas kernels for 0%

commit v1 on v0

v1 whole, which is shorter than its diff:
```python
import functools

import jax
import jax.numpy as jnp
from jax import lax
from jax.experimental import pallas as pl
from jax.experimental.pallas import tpu as pltpu
from jax.sharding import PartitionSpec as P

ROUNDS = 2
PIECES = 4
VMEM = 56 * 1024 * 1024
NN = (((1,), (0,)), ((), ()))
NT = (((1,), (1,)), ((), ()))


def split(x):
    hi = x.astype(jnp.bfloat16)
    lo = (x - hi.astype(jnp.float32)).astype(jnp.bfloat16)
    return hi, lo


def dot(a, b, dims):
    return lax.dot_general(a, b, dims, preferred_element_type=jnp.float32)


def dot3(a_both, b, dims):
    rows = a_both.shape[0] // 2
    b_hi, b_lo = b
    both = dot(a_both, b_hi, dims)
    return both[:rows] + both[rows:] + dot(a_both[:rows], b_lo, dims)


def block_of(size, most):
    block = size
    while block > most and block % 2 == 0:
        block //= 2
    return block


def light():
    return pl.CostEstimate(flops=1, bytes_accessed=1, transcendentals=0)


def pass_over(factor, chunk, columns, fitted=None, parts=None, gaps=None, stored=None, which=None, before=None, after=(), pieces=PIECES, most=2048):
    aux = factor.shape[1]
    block = block_of(columns, most)
    steps = columns // block
    first = chunk * steps
    out_rows = fitted.shape[0] if fitted is not None else 0
    half = out_rows // 2
    piece = half // pieces
    wide = gaps is not None
    own = extra = 0
    if wide:
        own = stored.shape[0] // which[1]
        extra = -(-own // 128) * 128
    parts = parts or []
    rows = sum(p.shape[0] for p in parts)
    after = [a for a in after if a is not None]

    def kernel(*refs):
        refs = list(refs)
        if wide:
            refs.pop(0)
        f_ref = refs.pop(0)
        if half:
            t_ref = refs.pop(0)
        xs = [refs.pop(0) for _ in parts]
        if wide:
            g_ref, s_ref = refs.pop(0), refs.pop(0)
        b_ref = refs.pop(0) if before is not None else None
        for _ in after:
            refs.pop(0)
        if half:
            keep_ref = refs.pop(0)
            send_refs = [refs.pop(0) for _ in range(pieces)]
        o_ref = refs.pop(0) if parts else None
        if half:
            both_ref = refs.pop(0)

        @pl.when(pl.program_id(0) == 0)
        def _():
            if half:
                hi, lo = split(4.0 * t_ref[...])
                both_ref[:out_rows] = hi
                both_ref[out_rows:] = lo
            if parts:
                if b_ref is None:
                    o_ref[...] = jnp.zeros_like(o_ref)
                else:
                    o_ref[...] = b_ref[...]

        factors = split(f_ref[...])
        if half:
            out = dot3(both_ref[...], factors, NT)
            keep_ref[...] = out[:half]
            for i, r in enumerate(send_refs):
                r[...] = out[half + i * piece : half + (i + 1) * piece]
        if parts:
            x = jnp.concatenate([r[...] for r in xs], axis=0) if len(xs) > 1 else xs[0][...]
            o_ref[:, :aux] += dot3(jnp.concatenate(split(x), axis=0), factors, NN)
            if wide:
                both = jnp.concatenate(split(x * g_ref[...]), axis=0)
                o_ref[:, aux : aux + own] += dot3(both, split(s_ref[...]), NT)

    in_specs = [pl.BlockSpec((block, aux), lambda k, *_: (first + k, 0))]
    args = [factor]
    if half:
        in_specs.append(pl.BlockSpec((out_rows, aux), lambda k, *_: (0, 0)))
        args.append(fitted)
    for p in parts:
        offset = first if p.shape[1] != columns else 0
        in_specs.append(pl.BlockSpec((p.shape[0], block), lambda k, *_, offset=offset: (0, offset + k)))
        args.append(p)
    if wide:
        in_specs.append(pl.BlockSpec((1, block), lambda k, *_: (0, first + k)))
        in_specs.append(pl.BlockSpec((own, block), lambda k, a: (a[0], first + k)))
        args += [gaps, stored]
    if before is not None:
        in_specs.append(pl.BlockSpec(before.shape, lambda k, *_: (0, 0)))
        args.append(before)
    for a in after:
        in_specs.append(pl.BlockSpec(memory_space=pl.ANY))
        args.append(a)
    shapes, specs = [], []
    if half:
        for height in [half] + [piece] * pieces:
            shapes.append(jax.ShapeDtypeStruct((height, columns), jnp.float32))
            specs.append(pl.BlockSpec((height, block), lambda k, *_: (0, k)))
    if parts:
        shapes.append(jax.ShapeDtypeStruct((rows, aux + extra), jnp.float32))
        specs.append(pl.BlockSpec((rows, aux + extra), lambda k, *_: (0, 0)))
    if wide:
        args = [which[0]] + args
    out = pl.pallas_call(
        kernel,
        out_shape=tuple(shapes),
        grid_spec=pltpu.PrefetchScalarGridSpec(
            num_scalar_prefetch=1 if wide else 0,
            grid=(steps,),
            in_specs=in_specs,
            out_specs=tuple(specs),
            scratch_shapes=[pltpu.VMEM((2 * out_rows, aux), jnp.bfloat16)] if half else [],
        ),
        compiler_params=pltpu.CompilerParams(vmem_limit_bytes=VMEM),
        cost_estimate=light(),
        name=("spread" if half else "") + ("fit" if parts else ""),
    )(*args)
    if half:
        out = [out[0], list(out[1 : 1 + pieces]), *out[1 + pieces :]]
    return out


def assemble(summed, arrived, olds, old_chunks, projection, stored, gaps, chunk, swap, after=(), most=2048):
    rows, columns = arrived.shape
    total = stored.shape[0]
    block = block_of(columns, most)
    steps = columns // block
    first = chunk * steps
    half = rows // 2
    pieces = PIECES if swap else 1
    piece = rows // pieces

    def kernel(*refs):
        refs = list(refs)
        c_ref, y_ref = refs.pop(0), refs.pop(0)
        xs = [refs.pop(0) for _ in olds]
        p_ref, s_ref, g_ref = refs[:3]
        o_refs, q_ref = refs[-1 - pieces : -1], refs[-1]
        arrival = y_ref[...]
        if swap:
            arrival = jnp.concatenate([arrival[half:], arrival[:half]], axis=0)
        x = jnp.concatenate([r[...] for r in xs], axis=0) if len(xs) > 1 else xs[0][...]
        both = jnp.concatenate(split(p_ref[...]), axis=0)
        removed = dot3(both, split(s_ref[...]), NN)
        new = x + (c_ref[...] + arrival - removed) / g_ref[...]
        for i, r in enumerate(o_refs):
            r[...] = new[i * piece : (i + 1) * piece]

        @pl.when(pl.program_id(0) == 0)
        def _():
            q_ref[...] = jnp.zeros_like(q_ref)

        q_ref[...] += jnp.sum(new * new, axis=1, keepdims=True)

    def old_spec(height, offset):
        return pl.BlockSpec((height, block), lambda k: (0, offset * steps + k))

    in_specs = [
        pl.BlockSpec((rows, block), lambda k: (0, k)),
        pl.BlockSpec((rows, block), lambda k: (0, k)),
    ]
    share = rows // len(olds)
    in_specs += [old_spec(share, c) for c in old_chunks]
    in_specs += [
        pl.BlockSpec((rows, total), lambda k: (0, 0)),
        pl.BlockSpec((total, block), lambda k: (0, first + k)),
        pl.BlockSpec((1, block), lambda k: (0, first + k)),
    ]
    in_specs += [pl.BlockSpec(memory_space=pl.ANY) for _ in after]
    *new, squares = pl.pallas_call(
        kernel,
        out_shape=(
            *[jax.ShapeDtypeStruct((piece, columns), jnp.float32)] * pieces,
            jax.ShapeDtypeStruct((rows, 128), jnp.float32),
        ),
        grid=(steps,),
        in_specs=in_specs,
        out_specs=(
            *[pl.BlockSpec((piece, block), lambda k: (0, k))] * pieces,
            pl.BlockSpec((rows, 128), lambda k: (0, 0)),
        ),
        compiler_params=pltpu.CompilerParams(vmem_limit_bytes=VMEM),
        cost_estimate=light(),
        name="assemble",
    )(summed, arrived, *olds, projection, stored, gaps, *after)
    return new, squares


def swap_with(value, axis, size, distance):
    return lax.ppermute(value, axis, [(i, i ^ distance) for i in range(size)])


def small(kernel, shapes, *args, name="small", scalar=None, after=()):
    out = tuple(jax.ShapeDtypeStruct(x, jnp.float32) for x in shapes)
    specs = [pl.BlockSpec(memory_space=pltpu.VMEM)] * len(args)
    if scalar is not None:
        specs = [pl.BlockSpec(memory_space=pltpu.SMEM)] + specs
        args = (scalar, *args)
    used = len(args)

    def body(*refs):
        kernel(*refs[:used], *refs[used + len(after) :])

    specs += [pl.BlockSpec(memory_space=pl.ANY)] * len(after)
    args = (*args, *after)
    return pl.pallas_call(
        body,
        out_shape=out,
        in_specs=specs,
        out_specs=tuple(pl.BlockSpec(memory_space=pltpu.VMEM) for _ in out),
        compiler_params=pltpu.CompilerParams(vmem_limit_bytes=VMEM // 2),
        cost_estimate=light(),
        name=name,
    )(*args)


def total_of(*values, after=()):
    def kernel(*refs):
        acc = refs[0][...]
        for r in refs[1:-1]:
            acc = acc + r[...]
        refs[-1][...] = acc

    return small(kernel, [values[0].shape], *values, name="total", after=after)[0]


def joined(keep, near, parts, after=(), most=4096):
    rows, columns = keep.shape
    block = block_of(columns, most)
    each = near[0].shape[0]
    height = rows // parts

    def kernel(k_ref, *refs):
        ins, outs = refs[: len(near)], refs[len(near) + len(after) :]
        for i, r in enumerate(ins):
            at = i * each
            outs[at // height][at % height : at % height + each] = k_ref[at : at + each] + r[...]

    return pl.pallas_call(
        kernel,
        out_shape=tuple([jax.ShapeDtypeStruct((height, columns), jnp.float32)] * parts),
        grid=(columns // block,),
        in_specs=[pl.BlockSpec((rows, block), lambda k: (0, k))]
        + [pl.BlockSpec((each, block), lambda k: (0, k))] * len(near)
        + [pl.BlockSpec(memory_space=pl.ANY)] * len(after),
        out_specs=tuple([pl.BlockSpec((height, block), lambda k: (0, k))] * parts),
        compiler_params=pltpu.CompilerParams(vmem_limit_bytes=VMEM),
        cost_estimate=light(),
        name="joined",
    )(keep, *near, *after)


def pair_sum(value, size, columns=None, between=(None, None)):
    rows = value.shape[0]
    columns = columns or value.shape[1]
    block = rows // 4
    me = jnp.reshape(lax.axis_index("pair") % 4, (1,)).astype(jnp.int32)

    def cut(m_ref, v_ref, *out):
        for d, o in enumerate(out):
            o[...] = v_ref[pl.ds(pl.multiple_of((m_ref[0] ^ d) * block, 8), block), :columns]

    def gather(m_ref, *refs):
        for d, r in enumerate(refs[:-1]):
            refs[-1][pl.ds(pl.multiple_of((m_ref[0] ^ d) * block, 8), block), :] = r[...]

    mine, *rest = small(cut, [(block, columns)] * 4, value, scalar=me, name="cut")
    others = [swap_with(r, "pair", size, d) for d, r in enumerate(rest, 1)]
    after = [between[0]([mine])] if between[0] else []
    total = total_of(mine, *others, after=after)
    distance = 4
    while distance < size:
        other = swap_with(total, "pair", size, distance)
        after = [between[1]([total])] if between[1] and distance == 4 else []
        total = total_of(total, other, after=after)
        distance *= 2
    every = [total] + [swap_with(total, "pair", size, d) for d in (1, 2, 3)]
    return small(gather, [(rows, columns)], *every, scalar=me, name="gather")[0]


def small_sum(value, size):
    if size & (size - 1):
        return lax.psum(value, "pair")
    distance = 1
    while distance < size:
        value = value + swap_with(value, "pair", size, distance)
        distance *= 2
    return value


def on_device(n_pair, n_aux, factor, trials, stored, energy_gaps):
    local, aux = factor.shape
    total = stored.shape[0]
    pairs = local * n_pair
    owned = trials.shape[0]
    own_s = total // n_aux
    me = lax.axis_index("aux")
    which = (jnp.reshape(me, (1,)).astype(jnp.int32), n_aux)
    gaps = energy_gaps[None, :]
    chunks = 2
    h = owned // 2
    two = 2 * h
    kc = local // chunks
    aux_swap = functools.partial(swap_with, axis="aux", size=n_aux)
    over = functools.partial(pass_over, factor)
    wide = dict(gaps=gaps, stored=stored, which=which)

    def project(fitted, partial, crossed):
        def part(m_ref, f_ref, p_ref, w_ref, keep_ref, send_ref):
            f = jnp.concatenate(split(4.0 * f_ref[...]), axis=0)
            own = p_ref[:, aux:]
            shape = (own.shape[1], total)
            row = lax.broadcasted_iota(jnp.int32, shape, 0)
            column = lax.broadcasted_iota(jnp.int32, shape, 1)
            here = (column == row + m_ref[0] * own_s) & (row < own_s)
            here = jnp.where(here, 1.0, 0.0).astype(jnp.bfloat16)
            placed = dot(jnp.concatenate(split(own), axis=0), here, NN)
            rows = own.shape[0]
            out = dot3(f, split(w_ref[...]), NT) + placed[:rows] + placed[rows:]
            keep_ref[...] = out[:two]
            send_ref[...] = out[two:]

        def both(k_ref, t_ref, o_ref):
            o_ref[:h] = k_ref[:h] + t_ref[h:]
            o_ref[h:] = k_ref[h:] + t_ref[:h]

        keep, send = small(part, [(two, total)] * 2, fitted, partial, crossed, scalar=which[0], name="project")
        first_part = keep
        keep = total_of(keep, aux_swap(send, distance=1))
        part_sum = small(both, [(two, total)], keep, aux_swap(keep, distance=2), name="both")[0]
        return first_part, part_sum, pair_sum(part_sum, n_pair)

    everyone = []
    for g in range(2):
        per_chunk = []
        for c in range(chunks):
            own = trials[g * h : (g + 1) * h, c * kc : (c + 1) * kc]
            per_chunk.append([own, aux_swap(own, distance=2)])
        everyone.append(per_chunk)

    def near_too(parts, token):
        parts = lax.optimization_barrier((*parts, token))[:2]
        return [*parts, *(aux_swap(p, distance=1) for p in parts)]

    crossed = None
    quarter = local // 4
    for c in range(2):
        (crossed,) = over(c, quarter, parts=[stored], before=crossed, after=[crossed])
    partial = None
    for c in range(chunks):
        everyone[0][c] = near_too(everyone[0][c], crossed)
        (partial,) = over(c, kc, parts=everyone[0][c], before=partial, **wide)
    held = [crossed]

    def more(c):
        def run(after):
            held.extend(over(c, quarter, parts=[stored], before=held[-1], after=after))
            return held[-1]

        return run

    one_part = partial
    one = pair_sum(partial, n_pair, aux, (more(2), more(3)))
    crossed = held[-1]

    def summed(keep, send, after):
        (keep,) = joined(keep, [aux_swap(x, distance=1) for x in send], 1, after)
        return keep, aux_swap(keep, distance=2)

    def new_vectors(g, c, pair, projection, token):
        new, square = assemble(
            *pair, everyone[g][c][:2], (0, 0), projection, stored, gaps, c, True, after=token
        )
        return new + [aux_swap(x, distance=1) for x in new], square[:h]

    begun, aux_sum, first = project(one, one_part, crossed)
    projected = [[None, None], [None, None]]
    projected[0][0] = first[:h]
    partial, sent, token = None, [[], []], [crossed, begun]
    for c in range(chunks):
        everyone[1][c] = near_too(everyone[1][c], crossed)
        keep, send, partial = over(c, kc, fitted=one, parts=everyone[1][c], before=partial, after=token, **wide)
        sent[0].append(summed(keep, send, [aux_sum]))
        token = [sent[0][-1][0]]
    two_part = partial
    two_sum = pair_sum(partial, n_pair, aux)
    current = [[], []]
    squares = [0.0, 0.0]
    begun, aux_sum, second = project(two_sum, two_part, crossed)
    projected[0][1] = second[:h]

    partial, token = None, [two_sum, sent[0][-1][0]]
    for c in range(chunks):
        x, square = new_vectors(0, c, sent[0][c], first, token)
        current[0].append(x)
        squares[0] = squares[0] + square
        keep, send, partial = over(c, kc, fitted=two_sum, parts=x, before=partial, after=[begun], **wide)
        sent[1].append(summed(keep, send, [aux_sum]))
        token = [sent[1][-1][0]]
    one_part = partial
    one = pair_sum(partial, n_pair, aux)
    begun, aux_sum, first = project(one, one_part, crossed)
    first = first[:h]
    projected[1][0] = first

    def last_sum(keep, send, after):
        near = [aux_swap(x, distance=1) for x in send]
        own, far = joined(keep, near, 2, after)
        return own, aux_swap(far, distance=2)

    partial, last = None, [[], []]
    for c in range(chunks):
        x, square = new_vectors(1, c, sent[1][c], second, token)
        current[1].append(x)
        squares[1] = squares[1] + square
        if c == 0:
            keep, send, partial = over(c, kc, fitted=one, parts=x, before=partial, after=[begun], **wide)
            last[0].append(last_sum(keep, send, [aux_sum]))
            keep, send = over(c + 1, kc, fitted=one, after=[last[0][-1][0]])
            last[0].append(last_sum(keep, send, []))
            token = [last[0][-1][0]]
        else:
            (partial,) = over(c, kc, parts=x, before=partial, **wide)
    ends = [[], []]
    norms = [0.0, 0.0]

    def finish(g, c, projection, token):
        new, square = assemble(
            *last[g][c],
            current[g][c][: PIECES // 2],
            (0,) * (PIECES // 2),
            projection,
            stored,
            gaps,
            c,
            False,
            after=token,
        )
        ends[g].append(new[0])
        norms[g] = norms[g] + square
        return new[0]

    two_part = partial
    two_sum = pair_sum(
        partial,
        n_pair,
        aux,
        (lambda after: finish(0, 0, first, after), lambda after: finish(0, 1, first, after)),
    )
    begun, aux_sum, second = project(two_sum, two_part, crossed)
    second = second[:h]
    projected[1][1] = second
    token = [begun]
    for c in range(chunks):
        keep, send = over(c, kc, fitted=two_sum, after=token, pieces=2 * PIECES)
        last[1].append(last_sum(keep, send, [aux_sum]))
        token = [last[1][-1][0]]
    token = []
    for c in range(chunks):
        token = [finish(1, c, second, token)]

    sums = jnp.concatenate([jnp.concatenate(squares, 0), jnp.concatenate(norms, 0)], axis=1)
    sums = small_sum(sums, n_pair)
    norm = jnp.sqrt(sums[:, :1] / pairs + 1e-06)
    scale = norm * jnp.sqrt(sums[:, 128:129] / (norm * norm) / pairs + 1e-06)
    out = jnp.concatenate([jnp.concatenate(e, axis=1) for e in ends], axis=0) / scale
    first_p = jnp.concatenate(projected[0], axis=0)
    second_p = jnp.concatenate(projected[1], axis=0) / norm
    return out, jnp.stack([first_p.T, second_p.T])


def solution(mesh):
    in_specs = (P("pair", "aux"), P("aux", "pair"), P(None, "pair"), P("pair"))
    out_specs = (P("aux", "pair"), P(None, None, "aux"))
    body = functools.partial(on_device, mesh.shape["pair"], mesh.shape["aux"])
    return jax.shard_map(body, mesh=mesh, in_specs=in_specs, out_specs=out_specs, check_vma=False)
```

time: 1160 us -> 695 us (0.60)
  waiting for transfers between devices: 734 us -> 134 us
  Pallas kernels: 0 us -> 391 us
  matrix products: 354 us -> 0 us
  starting transfers between devices: 2 us -> 114 us
  blocking collectives: 45.4 us -> 0 us
  local copies, waits for them, and re-layouts: 1.17 us -> 40.3 us
  between operations: 15.1 us -> 2 us
    pallas_call x0 -> x75, Pallas kernels: none -> 391 us  [the longest x15 290 us: pass_over(): pl.pallas_call(kernel, out_shape=tuple(shapes), grid_spec=pltpu.PrefetchS...]
    dot_general x8 -> x0, matrix products: 354 us -> none  [the longest x2 126 us: on_device(): jnp.dot(everything, factor, precision=highest, preferred_element_type=jnp...]
    psum x4 -> x0, waiting for transfers between devices: 294 us -> none  [the longest x2 156 us: on_device(): fitted = lax.psum(partial_value, 'pair')]
    reduce_scatter x2 -> x0, waiting for transfers between devices: 251 us -> none  [on_device(): lax.psum_scatter(4.0 * spread, 'aux', scatter_dimension=0, tiled=True)]
    all_gather x2 -> x0, waiting for transfers between devices: 188 us -> none  [on_device(): lax.all_gather(own_rows, 'aux', axis=0, tiled=True)]
    ppermute x0 -> x143, waiting for transfers between devices: none -> 134 us  [swap_with(): return lax.ppermute(value, axis, [(i, i ^ distance) for i in range(size)])]
    ppermute x0 -> x143, starting transfers between devices: none -> 114 us  [swap_with(): return lax.ppermute(value, axis, [(i, i ^ distance) for i in range(size)])]
    psum x2 -> x0, blocking collectives: 39 us -> none  [on_device(): square_sum = lax.psum(jnp.sum(scaled * scaled, axis=1), 'pair')]
  transfers between devices with their start and end apart: 8 -> 143, of which waited for: 8 -> 83; matrix products, arithmetic and copies ran while one was open for 0% -> 0% of each run, Pallas kernels for 0% -> 49%
where the time goes in v1:
time: 695 us; the launch traced here: 687 us
  Pallas kernels  391 us (56%)
  waiting for transfers between devices  134 us (19%)
  starting transfers between devices  114 us (16%)
  local copies, waits for them, and re-layouts  40.3 us (6%)
    pallas_call x15, Pallas kernels, pass_over(): pl.pallas_call(kernel, out_shape=tuple(shapes), grid_spec=pltpu.PrefetchS...  290 us
    ppermute x143, waiting for transfers between devices, swap_with(): return lax.ppermute(value, axis, [(i, i ^ distance) for i in range(size)])  134 us
    ppermute x143, starting transfers between devices, swap_with(): return lax.ppermute(value, axis, [(i, i ^ distance) for i in range(size)])  114 us
    pallas_call x8, Pallas kernels, assemble(): pl.pallas_call(kernel, out_shape=(*[jax.ShapeDtypeStruct((piece, columns)...  71.3 us
    unnamed x250, local copies, waits for them, and re-layouts  35.5 us
    pallas_call x8, Pallas kernels, joined(): pl.pallas_call(kernel, out_shape=tuple([jax.ShapeDtypeStruct((height, col...  26.9 us
  transfers between devices with their start and end apart: 143, of which 83 were waited for; matrix products, arithmetic and copies ran while one was open for 0% of the time, Pallas kernels for 49%

profile of v1, /device:TPU:0, one launch (start us, length us, event | category | flops | bytes accessed | tf_op | source)
XLA Modules:
  0.0 687.4 jit_solution(9174994639984399984)
XLA Ops:
  0.6 3.5 fusion.10
  4.2 3.0 collective-permute-start.3
  7.3 15.7 %fit.7.refs_2_.refs_3_ = f32[384,1024]{1,0:T(8,128)} custom-call(f32[16384,1024]{1,0:T(8,128)} %refs_0_.13, f32[384,16384]{1,0:T(8,128)} %refs_5_.15), custom_call_target="tpu_custom_call" | custom-call | flops 1 | bytes 1 | tf_op jit(solution)/shard_map/fit/pallas_call | solution.py:136
  23.0 16.1 %fit.8.refs_2_ = f32[384,1024]{1,0:T(8,128)} custom-call(f32[16384,1024]{1,0:T(8,128)} %refs_0_.13, f32[384,16384]{1,0:T(8,128)} %refs_5_.15, f32[384,1024]{1,0:T(8,128)} %fit.7.refs_2_.refs_3_, f32[384,1024]{1,0:T(8,128)} %fit.7.refs_2_.refs_3_), custom_call_target="tpu_custom_call" | custom-call | flops 1 | bytes 1 | tf_op jit(solution)/shard_map/fit/pallas_call | solution.py:136
  39.6 13.3 %collective-permute-done.refs_3_ = f32[32,8192]{1,0:T(8,128)} collective-permute-done((f32[32,8192]{1,0:T(8,128)S(1)}, f32[32,8192]{1,0:T(8,128)}, u32[]{:S(2)}, u32[]{:S(2)}) %collective-permute-start) | collective-permute-done | bytes 1048608 | tf_op jit(solution)/shard_map/ppermute | solution.py:222
  55.2 16.6 %fit.9.refs_8_ = f32[128,1152]{1,0:T(8,128)} custom-call(s32[1]{0:T(128)} %bitcast.refs_0_, f32[16384,1024]{1,0:T(8,128)} %refs_0_.13, f32[32,8192]{1,0:T(8,128)} %copy-done.45, f32[32,8192]{1,0:T(8,128)} %collective-permute-done.3.refs_3_, f32[32,8192]{1,0:T(8,128)} %collective-permute-done.4.refs_4_, f32[32,8192]{1,0:T(8,128)} %collective-permute-done.5.refs_5_, ...), custom_call_target="tpu_custom_call" | custom-call | flops 1 | bytes 1 | tf_op jit(solution)/shard_map/fit/pallas_call | solution.py:136
  71.8 19.5 %fit.10.refs_1_.refs_2_ = f32[128,1152]{1,0:T(8,128)} custom-call(s32[1]{0:T(128)} %bitcast.refs_0_, f32[16384,1024]{1,0:T(8,128)} %refs_0_.13, f32[32,8192]{1,0:T(8,128)} %copy-done.44, f32[32,8192]{1,0:T(8,128)} %collective-permute-done.refs_3_, f32[32,8192]{1,0:T(8,128)} %collective-permute-done.1.refs_4_, f32[32,8192]{1,0:T(8,128)} %collective-permute-done.2.refs_5_, ...), custom_call_target="tpu_custom_call" | custom-call | flops 1 | bytes 1 | tf_op jit(solution)/shard_map/fit/pallas_call | solution.py:136
  96.6 16.1 %fit.11.refs_4_.refs_2_ = f32[384,1024]{1,0:T(8,128)} custom-call(f32[16384,1024]{1,0:T(8,128)} %refs_0_.13, f32[384,16384]{1,0:T(8,128)} %refs_5_.15, f32[384,1024]{1,0:T(8,128)} %fit.8.refs_2_, f32[32,1024]{1,0:T(8,128)} %copy-done.34), custom_call_target="tpu_custom_call" | custom-call | flops 1 | bytes 1 | tf_op jit(solution)/shard_map/fit/pallas_call | solution.py:136
  114.8 16.2 %fit.12.refs_2_.refs_3_.refs_9_ = f32[384,1024]{1,0:T(8,128)} custom-call(f32[16384,1024]{1,0:T(8,128)} %refs_0_.13, f32[384,16384]{1,0:T(8,128)} %refs_5_.15, f32[384,1024]{1,0:T(8,128)} %fit.11.refs_4_.refs_2_, f32[32,1024]{1,0:T(8,128)} %copy-done.27), custom_call_target="tpu_custom_call" | custom-call | flops 1 | bytes 1 | tf_op jit(solution)/shard_map/fit/pallas_call | solution.py:136
  134.2 6.8 collective-permute-done.9.refs_1_
  150.8 3.5 collective-permute-done.12.refs_4_
  157.9 24.6 %spreadfit.5 = (f32[64,8192]{1,0:T(8,128)}, f32[16,8192]{1,0:T(8,128)}, f32[16,8192]{1,0:T(8,128)}, f32[16,8192]{1,0:T(8,128)}, f32[16,8192]{1,0:T(8,128)}, /*index=5*/f32[128,1152]{1,0:T(8,128)}) custom-call(s32[1]{0:T(128)} %bitcast.refs_0_, f32[16384,1024]{1,0:T(8,128)} %refs_0_.13, f32[128,1024]{1,0:T(8,128)} %copy-done.7, f32[32,8192]{1,0:T(8,128)} %copy-done.43, ...), custom_call_target="tpu_custom_call" | custom-call | flops 1 | bytes 1 | tf_op jit(solution)/shard_map/spreadfit/pallas_call | solution.py:136
  187.8 3.3 joined.8.refs_10_.refs_0_
  197.8 24.2 %spreadfit.6 = (f32[64,8192]{1,0:T(8,128)}, f32[16,8192]{1,0:T(8,128)}, f32[16,8192]{1,0:T(8,128)}, f32[16,8192]{1,0:T(8,128)}, f32[16,8192]{1,0:T(8,128)}, /*index=5*/f32[128,1152]{1,0:T(8,128)}) custom-call(s32[1]{0:T(128)} %bitcast.refs_0_, f32[16384,1024]{1,0:T(8,128)} %refs_0_.13, f32[128,1024]{1,0:T(8,128)} %copy-done.7, ...), custom_call_target="tpu_custom_call" | custom-call | flops 1 | bytes 1 | tf_op jit(solution)/shard_map/spreadfit/pallas_call | solution.py:136
  228.8 3.4 joined.9.refs_8_.refs_0_
  234.3 2.8 collective-permute-start.28
  256.5 2.9 collective-permute-start.43
  261.8 9.4 %assemble.8 = (f32[16,8192]{1,0:T(8,128)}, f32[16,8192]{1,0:T(8,128)}, f32[16,8192]{1,0:T(8,128)}, f32[16,8192]{1,0:T(8,128)}, f32[64,128]{1,0:T(8,128)}) custom-call(f32[64,8192]{1,0:T(8,128)} %joined.8.refs_10_.refs_0_, f32[64,8192]{1,0:T(8,128)} %collective-permute-done.44.refs_1_, f32[32,8192]{1,0:T(8,128)} %copy-done.45, ...), custom_call_target="tpu_custom_call" | custom-call | flops 1 | bytes 1 | tf_op jit(solution)/shard_map/assemble/pallas_call | solution.py:202
  276.6 24.4 %spreadfit.7 = (f32[64,8192]{1,0:T(8,128)}, f32[16,8192]{1,0:T(8,128)}, f32[16,8192]{1,0:T(8,128)}, f32[16,8192]{1,0:T(8,128)}, f32[16,8192]{1,0:T(8,128)}, /*index=5*/f32[128,1152]{1,0:T(8,128)}) custom-call(s32[1]{0:T(128)} %bitcast.refs_0_, f32[16384,1024]{1,0:T(8,128)} %refs_0_.13, f32[128,1024]{1,0:T(8,128)} %copy-done.4, ...), custom_call_target="tpu_custom_call" | custom-call | flops 1 | bytes 1 | tf_op jit(solution)/shard_map/spreadfit/pallas_call | solution.py:136
  306.2 3.3 joined.10.refs_7_.refs_0_
  311.5 9.4 %assemble.9 = (f32[16,8192]{1,0:T(8,128)}, f32[16,8192]{1,0:T(8,128)}, f32[16,8192]{1,0:T(8,128)}, f32[16,8192]{1,0:T(8,128)}, f32[64,128]{1,0:T(8,128)}) custom-call(f32[64,8192]{1,0:T(8,128)} %joined.9.refs_8_.refs_0_, f32[64,8192]{1,0:T(8,128)} %copy-done.50, f32[32,8192]{1,0:T(8,128)} %copy-done.44, f32[32,8192]{1,0:T(8,128)} %collective-permute-done.refs_3_, ...), custom_call_target="tpu_custom_call" | custom-call | flops 1 | bytes 1 | tf_op jit(solution)/shard_map/assemble/pallas_call | solution.py:202
  326.2 24.6 %spreadfit.8 = (f32[64,8192]{1,0:T(8,128)}, f32[16,8192]{1,0:T(8,128)}, f32[16,8192]{1,0:T(8,128)}, f32[16,8192]{1,0:T(8,128)}, f32[16,8192]{1,0:T(8,128)}, /*index=5*/f32[128,1152]{1,0:T(8,128)}) custom-call(s32[1]{0:T(128)} %bitcast.refs_0_, f32[16384,1024]{1,0:T(8,128)} %refs_0_.13, f32[128,1024]{1,0:T(8,128)} %copy-done.4, ...), custom_call_target="tpu_custom_call" | custom-call | flops 1 | bytes 1 | tf_op jit(solution)/shard_map/spreadfit/pallas_call | solution.py:136
  356.0 3.3 joined.11.refs_7_.refs_0_
  377.1 3.3 collective-permute-done.69.refs_3_
  398.1 9.4 %assemble.10 = (f32[16,8192]{1,0:T(8,128)}, f32[16,8192]{1,0:T(8,128)}, f32[16,8192]{1,0:T(8,128)}, f32[16,8192]{1,0:T(8,128)}, f32[64,128]{1,0:T(8,128)}) custom-call(f32[64,8192]{1,0:T(8,128)} %joined.10.refs_7_.refs_0_, f32[64,8192]{1,0:T(8,128)} %copy-done.49, f32[32,8192]{1,0:T(8,128)} %copy-done.43, ...), custom_call_target="tpu_custom_call" | custom-call | flops 1 | bytes 1 | tf_op jit(solution)/shard_map/assemble/pallas_call | solution.py:202
  412.8 24.8 %spreadfit.9 = (f32[64,8192]{1,0:T(8,128)}, f32[16,8192]{1,0:T(8,128)}, f32[16,8192]{1,0:T(8,128)}, f32[16,8192]{1,0:T(8,128)}, f32[16,8192]{1,0:T(8,128)}, /*index=5*/f32[128,1152]{1,0:T(8,128)}) custom-call(s32[1]{0:T(128)} %bitcast.refs_0_, f32[16384,1024]{1,0:T(8,128)} %refs_0_.13, f32[128,1024]{1,0:T(8,128)} %copy-done.5, ...), custom_call_target="tpu_custom_call" | custom-call | flops 1 | bytes 1 | tf_op jit(solution)/shard_map/spreadfit/pallas_call | solution.py:136
  442.8 3.2 joined.12
  446.1 16.5 %spread.3 = (f32[64,8192]{1,0:T(8,128)}, f32[16,8192]{1,0:T(8,128)}, f32[16,8192]{1,0:T(8,128)}, f32[16,8192]{1,0:T(8,128)}, f32[16,8192]{1,0:T(8,128)}) custom-call(f32[16384,1024]{1,0:T(8,128)} %refs_0_.13, f32[128,1024]{1,0:T(8,128)} %copy-done.5, f32[32,8192]{1,0:T(8,128)} %get-tuple-element.214.refs_2_.refs_0_), custom_call_target="tpu_custom_call" | custom-call | flops 1 | bytes 1 | tf_op jit(solution)/shard_map/spread/pallas_call | solution.py:136
  467.8 3.3 joined.13
  472.3 9.5 %assemble.11 = (f32[16,8192]{1,0:T(8,128)}, f32[16,8192]{1,0:T(8,128)}, f32[16,8192]{1,0:T(8,128)}, f32[16,8192]{1,0:T(8,128)}, f32[64,128]{1,0:T(8,128)}) custom-call(f32[64,8192]{1,0:T(8,128)} %joined.11.refs_7_.refs_0_, f32[64,8192]{1,0:T(8,128)} %copy-done.48, f32[32,8192]{1,0:T(8,128)} %get-tuple-element.147.refs_3_.refs_2_, f32[32,8192]{1,0:T(8,128)} %copy-done.46, ...), custom_call_target="tpu_custom_call" | custom-call | flops 1 | bytes 1 | tf_op jit(solution)/shard_map/assemble/pallas_call | solution.py:202
  489.5 3.2 collective-permute-done.91.refs_3_
  502.3 17.3 %fit.13.refs_1_.refs_2_ = f32[128,1152]{1,0:T(8,128)} custom-call(s32[1]{0:T(128)} %bitcast.refs_0_, f32[16384,1024]{1,0:T(8,128)} %refs_0_.13, f32[16,8192]{1,0:T(8,128)} %get-tuple-element.226.refs_2_, f32[16,8192]{1,0:T(8,128)} %get-tuple-element.227.refs_3_, f32[16,8192]{1,0:T(8,128)} %get-tuple-element.228.refs_4_, ...), custom_call_target="tpu_custom_call" | custom-call | flops 1 | bytes 1 | tf_op jit(solution)/shard_map/fit/pallas_call | solution.py:136
  526.4 8.2 %assemble.12 = (f32[32,8192]{1,0:T(8,128)}, f32[32,128]{1,0:T(8,128)}) custom-call(f32[32,8192]{1,0:T(8,128)} %get-tuple-element.214.refs_2_.refs_0_, f32[32,8192]{1,0:T(8,128)} %copy-done.56, f32[16,8192]{1,0:T(8,128)} %get-tuple-element.173.refs_3_.refs_2_, f32[16,8192]{1,0:T(8,128)} %get-tuple-element.174.refs_4_.refs_3_, f32[32,384]{1,0:T(8,128)} %slice.56.refs_4_, ...), custom_call_target="tpu_custom_call" | custom-call | flops 1 | bytes 1 | tf_op jit(solution)/shard_map/assemble/pallas_call | solution.py:202
  539.5 8.2 %assemble.13 = (f32[32,8192]{1,0:T(8,128)}, f32[32,128]{1,0:T(8,128)}) custom-call(f32[32,8192]{1,0:T(8,128)} %get-tuple-element.225.refs_7_.refs_0_, f32[32,8192]{1,0:T(8,128)} %copy-done.55, f32[16,8192]{1,0:T(8,128)} %get-tuple-element.184.refs_3_.refs_2_, f32[16,8192]{1,0:T(8,128)} %get-tuple-element.185.refs_4_.refs_3_, f32[32,384]{1,0:T(8,128)} %slice.56.refs_4_, ...), custom_call_target="tpu_custom_call" | custom-call | flops 1 | bytes 1 | tf_op jit(solution)/shard_map/assemble/pallas_call | solution.py:202
  553.4 2.9 collective-permute-done.110.refs_2_
  559.6 16.5 %spread.4 = (f32[64,8192]{1,0:T(8,128)}, f32[8,8192]{1,0:T(8,128)}, f32[8,8192]{1,0:T(8,128)}, f32[8,8192]{1,0:T(8,128)}, f32[8,8192]{1,0:T(8,128)}, /*index=5*/...) custom-call(f32[16384,1024]{1,0:T(8,128)} %refs_0_.13, f32[128,1024]{1,0:T(8,128)} %copy-done.6, ...), custom_call_target="tpu_custom_call" | custom-call | flops 1 | bytes 1 | tf_op jit(solution)/shard_map/spread/pallas_call | solution.py:136
  579.2 4.3 collective-permute-done.122.refs_1_
  587.1 3.4 joined.14
  590.5 16.6 %spread.5 = (f32[64,8192]{1,0:T(8,128)}, f32[8,8192]{1,0:T(8,128)}, f32[8,8192]{1,0:T(8,128)}, f32[8,8192]{1,0:T(8,128)}, f32[8,8192]{1,0:T(8,128)}, /*index=5*/...) custom-call(f32[16384,1024]{1,0:T(8,128)} %refs_0_.13, f32[128,1024]{1,0:T(8,128)} %copy-done.6, ...), custom_call_target="tpu_custom_call" | custom-call | flops 1 | bytes 1 | tf_op jit(solution)/shard_map/spread/pallas_call | solution.py:136
  612.3 3.6 joined.15
  624.5 3.9 collective-permute-done.127.refs_1_
  637.0 8.2 %assemble.14 = (f32[32,8192]{1,0:T(8,128)}, f32[32,128]{1,0:T(8,128)}) custom-call(f32[32,8192]{1,0:T(8,128)} %get-tuple-element.249.refs_0_.refs_2_, f32[32,8192]{1,0:T(8,128)} %copy-done.57, f32[16,8192]{1,0:T(8,128)} %get-tuple-element.203.refs_3_.refs_2_, f32[16,8192]{1,0:T(8,128)} %get-tuple-element.204.refs_4_.refs_3_, f32[32,384]{1,0:T(8,128)} %slice.57.refs_4_, ...), custom_call_target="tpu_custom_call" | custom-call | flops 1 | bytes 1 | tf_op jit(solution)/shard_map/assemble/pallas_call | solution.py:202
  645.1 12.6 %collective-permute-done.139.refs_1_ = f32[32,8192]{1,0:T(8,128)S(1)} collective-permute-done((f32[32,8192]{1,0:T(8,128)}, f32[32,8192]{1,0:T(8,128)S(1)}, u32[]{:S(2)}, u32[]{:S(2)}) %collective-permute-start.139) | collective-permute-done | bytes 1048608 | tf_op jit(solution)/shard_map/ppermute | solution.py:222
  658.8 9.1 %assemble.15 = (f32[32,8192]{1,0:T(8,128)}, f32[32,128]{1,0:T(8,128)}) custom-call(f32[32,8192]{1,0:T(8,128)} %get-tuple-element.265.refs_0_, f32[32,8192]{1,0:T(8,128)} %copy-done.54, f32[16,8192]{1,0:T(8,128)} %get-tuple-element.226.refs_2_, f32[16,8192]{1,0:T(8,128)} %get-tuple-element.227.refs_3_, f32[32,384]{1,0:T(8,128)} %slice.57.refs_4_, ...), custom_call_target="tpu_custom_call" | custom-call | flops 1 | bytes 1 | tf_op jit(solution)/shard_map/assemble/pallas_call | solution.py:202
  669.8 3.2 collective-permute-done.140
  674.0 3.3 collective-permute-done.141
  678.2 4.4 collective-permute-done.142
  683.5 3.6 maximum_divide_fusion
  (583 shorter events, 217.0 us)
Async XLA Ops:
  4.2 34.9 %collective-permute-start.3 = (f32[32,8192]{1,0:T(8,128)S(1)}, f32[32,8192]{1,0:T(8,128)}, u32[]{:S(2)}, u32[]{:S(2)}) collective-permute-start(f32[32,8192]{1,0:T(8,128)S(1)} %get-tuple-element.141.refs_2_), channel_id=1, source_target_pairs={{0,2},{1,3},{2,0},{3,1},{4,6},{5,7},{6,4},{7,5},{8,10},{9,11},{10,... | collective-permute-start | bytes 3145736 | tf_op jit(solution)/shard_map/ppermute | solution.py:222
  7.2 45.7 %collective-permute-start = (f32[32,8192]{1,0:T(8,128)S(1)}, f32[32,8192]{1,0:T(8,128)}, u32[]{:S(2)}, u32[]{:S(2)}) collective-permute-start(f32[32,8192]{1,0:T(8,128)S(1)} %get-tuple-element.139.refs_2_), channel_id=1, source_target_pairs={{0,2},{1,3},{2,0},{3,1},{4,6},{5,7},{6,4},{7,5},{8,10},{9,11},{10,... | collective-permute-start | bytes 3145736 | tf_op jit(solution)/shard_map/ppermute | solution.py:222
  39.0 16.2 %collective-permute-start.4 = (f32[32,8192]{1,0:T(8,128)S(1)}, f32[32,8192]{1,0:T(8,128)}, u32[]{:S(2)}, u32[]{:S(2)}) collective-permute-start(f32[32,8192]{1,0:T(8,128)S(1)} %get-tuple-element.141.refs_2_), channel_id=1, source_target_pairs={{0,1},{1,0},{2,3},{3,2},{4,5},{5,4},{6,7},{7,6},{8,9},{9,8},{10,11... | collective-permute-start | bytes 3145736 | tf_op jit(solution)/shard_map/ppermute | solution.py:222
  39.1 16.1 %collective-permute-start.5 = (f32[32,8192]{1,0:T(8,128)}, f32[32,8192]{1,0:T(8,128)}, u32[]{:S(2)}, u32[]{:S(2)}) collective-permute-start(f32[32,8192]{1,0:T(8,128)} %collective-permute-done.3.refs_3_), channel_id=1, source_target_pairs={{0,1},{1,0},{2,3},{3,2},{4,5},{5,4},{6,7},{7,6},{8,9},{9,8},{10,11... | collective-permute-start | bytes 3145736 | tf_op jit(solution)/shard_map/ppermute | solution.py:222
  52.9 18.9 %collective-permute-start.1 = (f32[32,8192]{1,0:T(8,128)S(1)}, f32[32,8192]{1,0:T(8,128)}, u32[]{:S(2)}, u32[]{:S(2)}) collective-permute-start(f32[32,8192]{1,0:T(8,128)S(1)} %get-tuple-element.139.refs_2_), channel_id=1, source_target_pairs={{0,1},{1,0},{2,3},{3,2},{4,5},{5,4},{6,7},{7,6},{8,9},{9,8},{10,11... | collective-permute-start | bytes 3145736 | tf_op jit(solution)/shard_map/ppermute | solution.py:222
  52.9 18.9 %collective-permute-start.2 = (f32[32,8192]{1,0:T(8,128)}, f32[32,8192]{1,0:T(8,128)}, u32[]{:S(2)}, u32[]{:S(2)}) collective-permute-start(f32[32,8192]{1,0:T(8,128)} %collective-permute-done.refs_3_), channel_id=1, source_target_pairs={{0,1},{1,0},{2,3},{3,2},{4,5},{5,4},{6,7},{7,6},{8,9},{9,8},{10,11... | collective-permute-start | bytes 3145736 | tf_op jit(solution)/shard_map/ppermute | solution.py:222
  53.5 77.6 %collective-permute-start.16 = (f32[32,8192]{1,0:T(8,128)S(1)}, f32[32,8192]{1,0:T(8,128)}, u32[]{:S(2)}, u32[]{:S(2)}) collective-permute-start(f32[32,8192]{1,0:T(8,128)S(1)} %get-tuple-element.149.refs_3_.refs_2_), channel_id=1, source_target_pairs={{0,2},{1,3},{2,0},{3,1},{4,6},{5,7},{6,4},{7,5},{8,10},{9,11},{10,... | collective-permute-start | bytes 3145736 | tf_op jit(solution)/shard_map/ppermute | solution.py:222
  93.1 19.6 %collective-permute-start.6 = (f32[32,1024]{1,0:T(8,128)S(1)}, f32[32,1024]{1,0:T(8,128)S(1)}, u32[]{:S(2)}, u32[]{:S(2)}) collective-permute-start(f32[32,1024]{1,0:T(8,128)S(1)} %get-tuple-element.144), channel_id=1, source_target_pairs={{0,4},{4,0},{8,12},{12,8},{16,20},{20,16},{24,28},{28,24},{1,5},{5... | collective-permute-start | bytes 393224 | tf_op jit(solution)/shard_map/ppermute | solution.py:222
  94.6 18.1 %collective-permute-start.7 = (f32[32,1024]{1,0:T(8,128)S(1)}, f32[32,1024]{1,0:T(8,128)S(1)}, u32[]{:S(2)}, u32[]{:S(2)}) collective-permute-start(f32[32,1024]{1,0:T(8,128)S(1)} %get-tuple-element.145), channel_id=1, source_target_pairs={{0,8},{4,12},{8,0},{12,4},{16,24},{20,28},{24,16},{28,20},{1,9},{5... | collective-permute-start | bytes 393224 | tf_op jit(solution)/shard_map/ppermute | solution.py:222
  96.2 16.5 %collective-permute-start.8 = (f32[32,1024]{1,0:T(8,128)S(1)}, f32[32,1024]{1,0:T(8,128)S(1)}, u32[]{:S(2)}, u32[]{:S(2)}) collective-permute-start(f32[32,1024]{1,0:T(8,128)S(1)} %get-tuple-element.146), channel_id=1, source_target_pairs={{0,12},{4,8},{8,4},{12,0},{16,28},{20,24},{24,20},{28,16},{1,13},{... | collective-permute-start | bytes 393224 | tf_op jit(solution)/shard_map/ppermute | solution.py:222
  131.1 25.9 %collective-permute-start.17 = (f32[32,8192]{1,0:T(8,128)S(1)}, f32[32,8192]{1,0:T(8,128)S(1)}, u32[]{:S(2)}, u32[]{:S(2)}) collective-permute-start(f32[32,8192]{1,0:T(8,128)S(1)} %get-tuple-element.149.refs_3_.refs_2_), channel_id=1, source_target_pairs={{0,1},{1,0},{2,3},{3,2},{4,5},{5,4},{6,7},{7,6},{8,9},{9,8},{10,11... | collective-permute-start | bytes 3145736 | tf_op jit(solution)/shard_map/ppermute | solution.py:222
  131.1 25.8 %collective-permute-start.18 = (f32[32,8192]{1,0:T(8,128)}, f32[32,8192]{1,0:T(8,128)}, u32[]{:S(2)}, u32[]{:S(2)}) collective-permute-start(f32[32,8192]{1,0:T(8,128)} %collective-permute-done.16.refs_4_.refs_3_), channel_id=1, source_target_pairs={{0,1},{1,0},{2,3},{3,2},{4,5},{5,4},{6,7},{7,6},{8,9},{9,8},{10,11... | collective-permute-start | bytes 3145736 | tf_op jit(solution)/shard_map/ppermute | solution.py:222
  131.6 9.4 %collective-permute-start.9 = (f32[32,1024]{1,0:T(8,128)}, f32[32,1024]{1,0:T(8,128)S(1)}, u32[]{:S(2)}, u32[]{:S(2)}) collective-permute-start(f32[32,1024]{1,0:T(8,128)} %copy-done.27), channel_id=1, source_target_pairs={{0,16},{4,20},{8,24},{12,28},{16,0},{20,4},{24,8},{28,12},{1,17},{... | collective-permute-start | bytes 393224 | tf_op jit(solution)/shard_map/ppermute | solution.py:222
  144.9 47.8 %collective-permute-start.13 = (f32[32,8192]{1,0:T(8,128)S(1)}, f32[32,8192]{1,0:T(8,128)S(1)}, u32[]{:S(2)}, u32[]{:S(2)}) collective-permute-start(f32[32,8192]{1,0:T(8,128)S(1)} %copy-done.42), channel_id=1, source_target_pairs={{0,2},{1,3},{2,0},{3,1},{4,6},{5,7},{6,4},{7,5},{8,10},{9,11},{10,... | collective-permute-start | bytes 3145736 | tf_op jit(solution)/shard_map/ppermute | solution.py:222
  156.4 26.8 %collective-permute-start.24 = (f32[64,384]{1,0:T(8,128)S(1)}, f32[64,384]{1,0:T(8,128)S(1)}, u32[]{:S(2)}, u32[]{:S(2)}) collective-permute-start(f32[64,384]{1,0:T(8,128)S(1)} %total.22.refs_0_), channel_id=1, source_target_pairs={{0,2},{1,3},{2,0},{3,1},{4,6},{5,7},{6,4},{7,5},{8,10},{9,11},{10,... | collective-permute-start | bytes 294920 | tf_op jit(solution)/shard_map/ppermute | solution.py:222
  191.1 70.7 %collective-permute-start.44 = (f32[64,8192]{1,0:T(8,128)}, f32[64,8192]{1,0:T(8,128)}, u32[]{:S(2)}, u32[]{:S(2)}) collective-permute-start(f32[64,8192]{1,0:T(8,128)} %joined.8.refs_10_.refs_0_), channel_id=1, source_target_pairs={{0,2},{1,3},{2,0},{3,1},{4,6},{5,7},{6,4},{7,5},{8,10},{9,11},{10,... | collective-permute-start | bytes 6291464 | tf_op jit(solution)/shard_map/ppermute | solution.py:222
  224.3 8.5 %collective-permute-start.25 = (f32[32,1024]{1,0:T(8,128)S(1)}, f32[32,1024]{1,0:T(8,128)S(1)}, u32[]{:S(2)}, u32[]{:S(2)}) collective-permute-start(f32[32,1024]{1,0:T(8,128)S(1)} %get-tuple-element.161), channel_id=1, source_target_pairs={{0,4},{4,0},{8,12},{12,8},{16,20},{20,16},{24,28},{28,24},{1,5},{5... | collective-permute-start | bytes 393224 | tf_op jit(solution)/shard_map/ppermute | solution.py:222
  225.8 7.0 %collective-permute-start.26 = (f32[32,1024]{1,0:T(8,128)S(1)}, f32[32,1024]{1,0:T(8,128)S(1)}, u32[]{:S(2)}, u32[]{:S(2)}) collective-permute-start(f32[32,1024]{1,0:T(8,128)S(1)} %get-tuple-element.162), channel_id=1, source_target_pairs={{0,8},{4,12},{8,0},{12,4},{16,24},{20,28},{24,16},{28,20},{1,9},{5... | collective-permute-start | bytes 393224 | tf_op jit(solution)/shard_map/ppermute | solution.py:222
  227.1 7.2 %collective-permute-start.27 = (f32[32,1024]{1,0:T(8,128)S(1)}, f32[32,1024]{1,0:T(8,128)S(1)}, u32[]{:S(2)}, u32[]{:S(2)}) collective-permute-start(f32[32,1024]{1,0:T(8,128)S(1)} %get-tuple-element.163), channel_id=1, source_target_pairs={{0,12},{4,8},{8,4},{12,0},{16,28},{20,24},{24,20},{28,16},{1,13},{... | collective-permute-start | bytes 393224 | tf_op jit(solution)/shard_map/ppermute | solution.py:222
  232.2 78.0 %collective-permute-start.36 = (f32[64,8192]{1,0:T(8,128)}, f32[64,8192]{1,0:T(8,128)S(1)}, u32[]{:S(2)}, u32[]{:S(2)}) collective-permute-start(f32[64,8192]{1,0:T(8,128)} %joined.9.refs_8_.refs_0_), channel_id=1, source_target_pairs={{0,2},{1,3},{2,0},{3,1},{4,6},{5,7},{6,4},{7,5},{8,10},{9,11},{10,... | collective-permute-start | bytes 6291464 | tf_op jit(solution)/shard_map/ppermute | solution.py:222
  234.3 11.7 %collective-permute-start.28 = (f32[32,1024]{1,0:T(8,128)S(1)}, f32[32,1024]{1,0:T(8,128)S(1)}, u32[]{:S(2)}, u32[]{:S(2)}) collective-permute-start(f32[32,1024]{1,0:T(8,128)S(1)} %total.23.refs_0_), channel_id=1, source_target_pairs={{0,16},{4,20},{8,24},{12,28},{16,0},{20,4},{24,8},{28,12},{1,17},{... | collective-permute-start | bytes 393224 | tf_op jit(solution)/shard_map/ppermute | solution.py:222
  246.0 7.4 %collective-permute-start.29 = (f32[32,1024]{1,0:T(8,128)S(1)}, f32[32,1024]{1,0:T(8,128)S(1)}, u32[]{:S(2)}, u32[]{:S(2)}) collective-permute-start(f32[32,1024]{1,0:T(8,128)S(1)} %total.24.refs_1_), channel_id=1, source_target_pairs={{0,4},{4,0},{8,12},{12,8},{16,20},{20,16},{24,28},{28,24},{1,5},{5... | collective-permute-start | bytes 393224 | tf_op jit(solution)/shard_map/ppermute | solution.py:222
  247.2 7.2 %collective-permute-start.30 = (f32[32,1024]{1,0:T(8,128)S(1)}, f32[32,1024]{1,0:T(8,128)S(1)}, u32[]{:S(2)}, u32[]{:S(2)}) collective-permute-start(f32[32,1024]{1,0:T(8,128)S(1)} %total.24.refs_1_), channel_id=1, source_target_pairs={{0,8},{4,12},{8,0},{12,4},{16,24},{20,28},{24,16},{28,20},{1,9},{5... | collective-permute-start | bytes 393224 | tf_op jit(solution)/shard_map/ppermute | solution.py:222
  253.4 6.7 collective-permute-start.41
  260.1 11.8 %collective-permute-start.53 = (f32[64,384]{1,0:T(8,128)S(1)}, f32[64,384]{1,0:T(8,128)S(1)}, u32[]{:S(2)}, u32[]{:S(2)}) collective-permute-start(f32[64,384]{1,0:T(8,128)S(1)} %get-tuple-element.183), channel_id=1, source_target_pairs={{0,1},{1,0},{2,3},{3,2},{4,5},{5,4},{6,7},{7,6},{8,9},{9,8},{10,11... | collective-permute-start | bytes 294920 | tf_op jit(solution)/shard_map/ppermute | solution.py:222
  273.4 28.2 %collective-permute-start.54 = (f32[64,384]{1,0:T(8,128)S(1)}, f32[64,384]{1,0:T(8,128)S(1)}, u32[]{:S(2)}, u32[]{:S(2)}) collective-permute-start(f32[64,384]{1,0:T(8,128)S(1)} %total.27.refs_0_), channel_id=1, source_target_pairs={{0,2},{1,3},{2,0},{3,1},{4,6},{5,7},{6,4},{7,5},{8,10},{9,11},{10,... | collective-permute-start | bytes 294920 | tf_op jit(solution)/shard_map/ppermute | solution.py:222
  309.5 87.3 %collective-permute-start.66 = (f32[64,8192]{1,0:T(8,128)}, f32[64,8192]{1,0:T(8,128)S(1)}, u32[]{:S(2)}, u32[]{:S(2)}) collective-permute-start(f32[64,8192]{1,0:T(8,128)} %joined.10.refs_7_.refs_0_), channel_id=1, source_target_pairs={{0,2},{1,3},{2,0},{3,1},{4,6},{5,7},{6,4},{7,5},{8,10},{9,11},{10,... | collective-permute-start | bytes 6291464 | tf_op jit(solution)/shard_map/ppermute | solution.py:222
  359.3 111.7 %collective-permute-start.96 = (f32[64,8192]{1,0:T(8,128)}, f32[64,8192]{1,0:T(8,128)S(1)}, u32[]{:S(2)}, u32[]{:S(2)}) collective-permute-start(f32[64,8192]{1,0:T(8,128)} %joined.11.refs_7_.refs_0_), channel_id=1, source_target_pairs={{0,2},{1,3},{2,0},{3,1},{4,6},{5,7},{6,4},{7,5},{8,10},{9,11},{10,... | collective-permute-start | bytes 6291464 | tf_op jit(solution)/shard_map/ppermute | solution.py:222
  361.9 6.5 collective-permute-start.60
  364.2 6.5 collective-permute-start.61
  370.8 11.7 %collective-permute-start.62 = (f32[32,1024]{1,0:T(8,128)S(1)}, f32[32,1024]{1,0:T(8,128)S(1)}, u32[]{:S(2)}, u32[]{:S(2)}) collective-permute-start(f32[32,1024]{1,0:T(8,128)S(1)} %total.28.refs_0_), channel_id=1, source_target_pairs={{0,16},{4,20},{8,24},{12,28},{16,0},{20,4},{24,8},{28,12},{1,17},{... | collective-permute-start | bytes 393224 | tf_op jit(solution)/shard_map/ppermute | solution.py:222
  393.7 14.5 %collective-permute-start.86 = (f32[64,384]{1,0:T(8,128)S(1)}, f32[64,384]{1,0:T(8,128)S(1)}, u32[]{:S(2)}, u32[]{:S(2)}) collective-permute-start(f32[64,384]{1,0:T(8,128)S(1)} %get-tuple-element.213), channel_id=1, source_target_pairs={{0,1},{1,0},{2,3},{3,2},{4,5},{5,4},{6,7},{7,6},{8,9},{9,8},{10,11... | collective-permute-start | bytes 294920 | tf_op jit(solution)/shard_map/ppermute | solution.py:222
  409.7 28.6 %collective-permute-start.87 = (f32[64,384]{1,0:T(8,128)S(1)}, f32[64,384]{1,0:T(8,128)S(1)}, u32[]{:S(2)}, u32[]{:S(2)}) collective-permute-start(f32[64,384]{1,0:T(8,128)S(1)} %total.32.refs_0_), channel_id=1, source_target_pairs={{0,2},{1,3},{2,0},{3,1},{4,6},{5,7},{6,4},{7,5},{8,10},{9,11},{10,... | collective-permute-start | bytes 294920 | tf_op jit(solution)/shard_map/ppermute | solution.py:222
  481.8 15.7 %collective-permute-start.101 = (f32[16,8192]{1,0:T(8,128)}, f32[16,8192]{1,0:T(8,128)S(1)}, u32[]{:S(2)}, u32[]{:S(2)}) collective-permute-start(f32[16,8192]{1,0:T(8,128)} %get-tuple-element.226.refs_2_), channel_id=1, source_target_pairs={{0,1},{1,0},{2,3},{3,2},{4,5},{5,4},{6,7},{7,6},{8,9},{9,8},{10,11... | collective-permute-start | bytes 1572872 | tf_op jit(solution)/shard_map/ppermute | solution.py:222
  482.1 43.4 %collective-permute-start.88 = (f32[32,8192]{1,0:T(8,128)S(1)}, f32[32,8192]{1,0:T(8,128)S(1)}, u32[]{:S(2)}, u32[]{:S(2)}) collective-permute-start(f32[32,8192]{1,0:T(8,128)S(1)} %copy-done.123), channel_id=1, source_target_pairs={{0,2},{1,3},{2,0},{3,1},{4,6},{5,7},{6,4},{7,5},{8,10},{9,11},{10,... | collective-permute-start | bytes 3145736 | tf_op jit(solution)/shard_map/ppermute | solution.py:222
  482.8 55.7 %collective-permute-start.105 = (f32[32,8192]{1,0:T(8,128)}, f32[32,8192]{1,0:T(8,128)S(1)}, u32[]{:S(2)}, u32[]{:S(2)}) collective-permute-start(f32[32,8192]{1,0:T(8,128)} %get-tuple-element.233), channel_id=1, source_target_pairs={{0,2},{1,3},{2,0},{3,1},{4,6},{5,7},{6,4},{7,5},{8,10},{9,11},{10,... | collective-permute-start | bytes 3145736 | tf_op jit(solution)/shard_map/ppermute | solution.py:222
  498.1 23.2 %collective-permute-start.93 = (f32[16,384]{1,0:T(8,128)S(1)}, f32[16,384]{1,0:T(8,128)S(1)}, u32[]{:S(2)}, u32[]{:S(2)}) collective-permute-start(f32[16,384]{1,0:T(8,128)S(1)} %total.34.refs_1_), channel_id=1, source_target_pairs={{0,4},{4,0},{8,12},{12,8},{16,20},{20,16},{24,28},{28,24},{1,5},{5... | collective-permute-start | bytes 73736 | tf_op jit(solution)/shard_map/ppermute | solution.py:222
  499.7 22.5 %collective-permute-start.94 = (f32[16,384]{1,0:T(8,128)S(1)}, f32[16,384]{1,0:T(8,128)S(1)}, u32[]{:S(2)}, u32[]{:S(2)}) collective-permute-start(f32[16,384]{1,0:T(8,128)S(1)} %total.34.refs_1_), channel_id=1, source_target_pairs={{0,8},{4,12},{8,0},{12,4},{16,24},{20,28},{24,16},{28,20},{1,9},{5... | collective-permute-start | bytes 73736 | tf_op jit(solution)/shard_map/ppermute | solution.py:222
  500.8 22.5 %collective-permute-start.95 = (f32[16,384]{1,0:T(8,128)S(1)}, f32[16,384]{1,0:T(8,128)S(1)}, u32[]{:S(2)}, u32[]{:S(2)}) collective-permute-start(f32[16,384]{1,0:T(8,128)S(1)} %total.34.refs_1_), channel_id=1, source_target_pairs={{0,12},{4,8},{8,4},{12,0},{16,28},{20,24},{24,20},{28,16},{1,13},{... | collective-permute-start | bytes 73736 | tf_op jit(solution)/shard_map/ppermute | solution.py:222
  521.3 13.3 %collective-permute-start.106 = (f32[32,1024]{1,0:T(8,128)S(1)}, f32[32,1024]{1,0:T(8,128)S(1)}, u32[]{:S(2)}, u32[]{:S(2)}) collective-permute-start(f32[32,1024]{1,0:T(8,128)S(1)} %get-tuple-element.234), channel_id=1, source_target_pairs={{0,4},{4,0},{8,12},{12,8},{16,20},{20,16},{24,28},{28,24},{1,5},{5... | collective-permute-start | bytes 393224 | tf_op jit(solution)/shard_map/ppermute | solution.py:222
  522.2 12.4 %collective-permute-start.107 = (f32[32,1024]{1,0:T(8,128)S(1)}, f32[32,1024]{1,0:T(8,128)S(1)}, u32[]{:S(2)}, u32[]{:S(2)}) collective-permute-start(f32[32,1024]{1,0:T(8,128)S(1)} %get-tuple-element.235), channel_id=1, source_target_pairs={{0,8},{4,12},{8,0},{12,4},{16,24},{20,28},{24,16},{28,20},{1,9},{5... | collective-permute-start | bytes 393224 | tf_op jit(solution)/shard_map/ppermute | solution.py:222
  523.3 11.4 %collective-permute-start.108 = (f32[32,1024]{1,0:T(8,128)S(1)}, f32[32,1024]{1,0:T(8,128)S(1)}, u32[]{:S(2)}, u32[]{:S(2)}) collective-permute-start(f32[32,1024]{1,0:T(8,128)S(1)} %get-tuple-element.236), channel_id=1, source_target_pairs={{0,12},{4,8},{8,4},{12,0},{16,28},{20,24},{24,20},{28,16},{1,13},{... | collective-permute-start | bytes 393224 | tf_op jit(solution)/shard_map/ppermute | solution.py:222
  535.9 11.7 %collective-permute-start.109 = (f32[32,1024]{1,0:T(8,128)S(1)}, f32[32,1024]{1,0:T(8,128)S(1)}, u32[]{:S(2)}, u32[]{:S(2)}) collective-permute-start(f32[32,1024]{1,0:T(8,128)S(1)} %total.35.refs_7_.refs_0_), channel_id=1, source_target_pairs={{0,16},{4,20},{8,24},{12,28},{16,0},{20,4},{24,8},{28,12},{1,17},{... | collective-permute-start | bytes 393224 | tf_op jit(solution)/shard_map/ppermute | solution.py:222
  576.1 7.4 %collective-permute-start.113 = (f32[8,8192]{1,0:T(8,128)}, f32[8,8192]{1,0:T(8,128)S(1)}, u32[]{:S(2)}, u32[]{:S(2)}) collective-permute-start(f32[8,8192]{1,0:T(8,128)} %get-tuple-element.240), channel_id=1, source_target_pairs={{0,1},{1,0},{2,3},{3,2},{4,5},{5,4},{6,7},{7,6},{8,9},{9,8},{10,11... | collective-permute-start | bytes 786440 | tf_op jit(solution)/shard_map/ppermute | solution.py:222
  576.2 7.9 %collective-permute-start.114 = (f32[8,8192]{1,0:T(8,128)}, f32[8,8192]{1,0:T(8,128)S(1)}, u32[]{:S(2)}, u32[]{:S(2)}) collective-permute-start(f32[8,8192]{1,0:T(8,128)} %get-tuple-element.241), channel_id=1, source_target_pairs={{0,1},{1,0},{2,3},{3,2},{4,5},{5,4},{6,7},{7,6},{8,9},{9,8},{10,11... | collective-permute-start | bytes 786440 | tf_op jit(solution)/shard_map/ppermute | solution.py:222
  576.7 7.4 %collective-permute-start.115 = (f32[8,8192]{1,0:T(8,128)}, f32[8,8192]{1,0:T(8,128)S(1)}, u32[]{:S(2)}, u32[]{:S(2)}) collective-permute-start(f32[8,8192]{1,0:T(8,128)} %get-tuple-element.242), channel_id=1, source_target_pairs={{0,1},{1,0},{2,3},{3,2},{4,5},{5,4},{6,7},{7,6},{8,9},{9,8},{10,11... | collective-permute-start | bytes 786440 | tf_op jit(solution)/shard_map/ppermute | solution.py:222
  610.0 26.0 %collective-permute-start.123 = (f32[32,8192]{1,0:T(8,128)S(1)}, f32[32,8192]{1,0:T(8,128)S(1)}, u32[]{:S(2)}, u32[]{:S(2)}) collective-permute-start(f32[32,8192]{1,0:T(8,128)S(1)} %copy-done.124), channel_id=1, source_target_pairs={{0,2},{1,3},{2,0},{3,1},{4,6},{5,7},{6,4},{7,5},{8,10},{9,11},{10,... | collective-permute-start | bytes 3145736 | tf_op jit(solution)/shard_map/ppermute | solution.py:222
  615.9 41.9 %collective-permute-start.139 = (f32[32,8192]{1,0:T(8,128)}, f32[32,8192]{1,0:T(8,128)S(1)}, u32[]{:S(2)}, u32[]{:S(2)}) collective-permute-start(f32[32,8192]{1,0:T(8,128)} %get-tuple-element.266), channel_id=1, source_target_pairs={{0,2},{1,3},{2,0},{3,1},{4,6},{5,7},{6,4},{7,5},{8,10},{9,11},{10,... | collective-permute-start | bytes 3145736 | tf_op jit(solution)/shard_map/ppermute | solution.py:222
  (222 other events, 1258.6 us)

commit v2 on v1

--- a/solution.py
+++ b/solution.py
@@ -9,7 +9,7 @@
 
 ROUNDS = 2
 PIECES = 4
-VMEM = 56 * 1024 * 1024
+VMEM = 61 * 1024 * 1024
 NN = (((1,), (0,)), ((), ()))
 NT = (((1,), (1,)), ((), ()))
 
@@ -152,8 +152,13 @@
     return out
 
 
+def whole(refs):
+    return jnp.concatenate([r[...] for r in refs], axis=0) if len(refs) > 1 else refs[0][...]
+
+
 def assemble(summed, arrived, olds, old_chunks, projection, stored, gaps, chunk, swap, after=(), most=2048):
-    rows, columns = arrived.shape
+    rows = sum(a.shape[0] for a in arrived)
+    columns = arrived[0].shape[1]
     total = stored.shape[0]
     block = block_of(columns, most)
     steps = columns // block
@@ -164,17 +169,18 @@
 
     def kernel(*refs):
         refs = list(refs)
-        c_ref, y_ref = refs.pop(0), refs.pop(0)
+        cs = [refs.pop(0) for _ in summed]
+        ys = [refs.pop(0) for _ in arrived]
         xs = [refs.pop(0) for _ in olds]
         p_ref, s_ref, g_ref = refs[:3]
         o_refs, q_ref = refs[-1 - pieces : -1], refs[-1]
-        arrival = y_ref[...]
+        arrival = whole(ys)
         if swap:
             arrival = jnp.concatenate([arrival[half:], arrival[:half]], axis=0)
-        x = jnp.concatenate([r[...] for r in xs], axis=0) if len(xs) > 1 else xs[0][...]
+        x = whole(xs)
         both = jnp.concatenate(split(p_ref[...]), axis=0)
         removed = dot3(both, split(s_ref[...]), NN)
-        new = x + (c_ref[...] + arrival - removed) / g_ref[...]
+        new = x + (whole(cs) + arrival - removed) / g_ref[...]
         for i, r in enumerate(o_refs):
             r[...] = new[i * piece : (i + 1) * piece]
 
@@ -187,10 +193,7 @@
     def old_spec(height, offset):
         return pl.BlockSpec((height, block), lambda k: (0, offset * steps + k))
 
-    in_specs = [
-        pl.BlockSpec((rows, block), lambda k: (0, k)),
-        pl.BlockSpec((rows, block), lambda k: (0, k)),
-    ]
+    in_specs = [pl.BlockSpec((a.shape[0], block), lambda k: (0, k)) for a in (*summed, *arrived)]
     share = rows // len(olds)
     in_specs += [old_spec(share, c) for c in old_chunks]
     in_specs += [
@@ -214,7 +217,7 @@
         compiler_params=pltpu.CompilerParams(vmem_limit_bytes=VMEM),
         cost_estimate=light(),
         name="assemble",
-    )(summed, arrived, *olds, projection, stored, gaps, *after)
+    )(*summed, *arrived, *olds, projection, stored, gaps, *after)
     return new, squares
 
 
@@ -240,7 +243,7 @@
         out_shape=out,
         in_specs=specs,
         out_specs=tuple(pl.BlockSpec(memory_space=pltpu.VMEM) for _ in out),
-        compiler_params=pltpu.CompilerParams(vmem_limit_bytes=VMEM // 2),
+        compiler_params=pltpu.CompilerParams(vmem_limit_bytes=VMEM),
         cost_estimate=light(),
         name=name,
     )(*args)
@@ -282,21 +285,20 @@
     )(keep, *near, *after)
 
 
-def pair_sum(value, size, columns=None, between=(None, None)):
-    rows = value.shape[0]
-    columns = columns or value.shape[1]
+def pair_sum(value, size, between=(None, None), last=None, after=()):
+    rows, columns = value.shape
     block = rows // 4
     me = jnp.reshape(lax.axis_index("pair") % 4, (1,)).astype(jnp.int32)
 
     def cut(m_ref, v_ref, *out):
         for d, o in enumerate(out):
-            o[...] = v_ref[pl.ds(pl.multiple_of((m_ref[0] ^ d) * block, 8), block), :columns]
+            o[...] = v_ref[pl.ds(pl.multiple_of((m_ref[0] ^ d) * block, 8), block), :]
 
     def gather(m_ref, *refs):
         for d, r in enumerate(refs[:-1]):
             refs[-1][pl.ds(pl.multiple_of((m_ref[0] ^ d) * block, 8), block), :] = r[...]
 
-    mine, *rest = small(cut, [(block, columns)] * 4, value, scalar=me, name="cut")
+    mine, *rest = small(cut, [(block, columns)] * 4, value, scalar=me, name="cut", after=after)
     others = [swap_with(r, "pair", size, d) for d, r in enumerate(rest, 1)]
     after = [between[0]([mine])] if between[0] else []
     total = total_of(mine, *others, after=after)
@@ -307,7 +309,8 @@
         total = total_of(total, other, after=after)
         distance *= 2
     every = [total] + [swap_with(total, "pair", size, d) for d in (1, 2, 3)]
-    return small(gather, [(rows, columns)], *every, scalar=me, name="gather")[0]
+    after = [last([total])] if last else []
+    return small(gather, [(rows, columns)], *every, scalar=me, name="gather", after=after)[0]
 
 
 def small_sum(value, size):
@@ -337,10 +340,10 @@
     over = functools.partial(pass_over, factor)
     wide = dict(gaps=gaps, stored=stored, which=which)
 
-    def project(fitted, partial, crossed):
-        def part(m_ref, f_ref, p_ref, w_ref, keep_ref, send_ref):
-            f = jnp.concatenate(split(4.0 * f_ref[...]), axis=0)
-            own = p_ref[:, aux:]
+    def project(fitted):
+        def part(m_ref, f_ref, w_ref, keep_ref, send_ref):
+            f = jnp.concatenate(split(4.0 * f_ref[:, :aux]), axis=0)
+            own = f_ref[:, aux:]
             shape = (own.shape[1], total)
             row = lax.broadcasted_iota(jnp.int32, shape, 0)
             column = lax.broadcasted_iota(jnp.int32, shape, 1)
@@ -356,89 +359,86 @@
             o_ref[:h] = k_ref[:h] + t_ref[h:]
             o_ref[h:] = k_ref[h:] + t_ref[:h]
 
-        keep, send = small(part, [(two, total)] * 2, fitted, partial, crossed, scalar=which[0], name="project")
+        keep, send = small(part, [(two, total)] * 2, fitted, crossed, scalar=which[0], name="project")
         first_part = keep
         keep = total_of(keep, aux_swap(send, distance=1))
         part_sum = small(both, [(two, total)], keep, aux_swap(keep, distance=2), name="both")[0]
-        return first_part, part_sum, pair_sum(part_sum, n_pair)
+        return first_part, part_sum
 
     everyone = []
     for g in range(2):
-        per_chunk = []
-        for c in range(chunks):
-            own = trials[g * h : (g + 1) * h, c * kc : (c + 1) * kc]
-            per_chunk.append([own, aux_swap(own, distance=2)])
-        everyone.append(per_chunk)
+        own = trials[g * h : (g + 1) * h]
+        everyone.append([own, aux_swap(own, distance=2)])
 
     def near_too(parts, token):
         parts = lax.optimization_barrier((*parts, token))[:2]
         return [*parts, *(aux_swap(p, distance=1) for p in parts)]
 
-    crossed = None
-    quarter = local // 4
-    for c in range(2):
-        (crossed,) = over(c, quarter, parts=[stored], before=crossed, after=[crossed])
-    partial = None
-    for c in range(chunks):
-        everyone[0][c] = near_too(everyone[0][c], crossed)
-        (partial,) = over(c, kc, parts=everyone[0][c], before=partial, **wide)
-    held = [crossed]
-
-    def more(c):
+    (crossed,) = over(0, local, parts=[stored])
+    everyone[0] = near_too(everyone[0], crossed)
+    held = [None]
+
+    def first_fit(c):
         def run(after):
-            held.extend(over(c, quarter, parts=[stored], before=held[-1], after=after))
+            held.extend(over(c, kc, parts=everyone[0], before=held[-1], after=after, **wide))
             return held[-1]
 
         return run
 
-    one_part = partial
-    one = pair_sum(partial, n_pair, aux, (more(2), more(3)))
-    crossed = held[-1]
+    begins = []
+
+    def first_way(after):
+        begins.append(pair_sum(held[-1], n_pair, after=after))
+        everyone[1] = near_too(everyone[1], begins[0])
+        begins.append(over(0, kc, fitted=begins[0], parts=everyone[1], **wide))
+        return begins[1][2]
+
+    crossed = pair_sum(crossed, n_pair, (first_fit(0), first_fit(1)), first_way)
+    one = begins[0]
 
     def summed(keep, send, after):
         (keep,) = joined(keep, [aux_swap(x, distance=1) for x in send], 1, after)
-        return keep, aux_swap(keep, distance=2)
+        return [keep], [aux_swap(keep, distance=2)]
 
     def new_vectors(g, c, pair, projection, token):
         new, square = assemble(
-            *pair, everyone[g][c][:2], (0, 0), projection, stored, gaps, c, True, after=token
+            *pair, everyone[g][:2], (c, c), projection, stored, gaps, c, True, after=token
         )
         return new + [aux_swap(x, distance=1) for x in new], square[:h]
 
-    begun, aux_sum, first = project(one, one_part, crossed)
+    begun, first = project(one)
     projected = [[None, None], [None, None]]
     projected[0][0] = first[:h]
-    partial, sent, token = None, [[], []], [crossed, begun]
-    for c in range(chunks):
-        everyone[1][c] = near_too(everyone[1][c], crossed)
-        keep, send, partial = over(c, kc, fitted=one, parts=everyone[1][c], before=partial, after=token, **wide)
-        sent[0].append(summed(keep, send, [aux_sum]))
-        token = [sent[0][-1][0]]
-    two_part = partial
-    two_sum = pair_sum(partial, n_pair, aux)
+    keep, send, partial = begins[1]
+    sent = [[summed(keep, send, [first])], []]
+    for c in range(1, chunks):
+        keep, send, partial = over(
+            c, kc, fitted=one, parts=everyone[1], before=partial, after=[sent[0][-1][0][0]], **wide
+        )
+        sent[0].append(summed(keep, send, []))
+    two_sum = pair_sum(partial, n_pair)
     current = [[], []]
     squares = [0.0, 0.0]
-    begun, aux_sum, second = project(two_sum, two_part, crossed)
+    begun, second = project(two_sum)
     projected[0][1] = second[:h]
 
-    partial, token = None, [two_sum, sent[0][-1][0]]
+    partial, token = None, [two_sum, sent[0][-1][0][0]]
     for c in range(chunks):
         x, square = new_vectors(0, c, sent[0][c], first, token)
         current[0].append(x)
         squares[0] = squares[0] + square
         keep, send, partial = over(c, kc, fitted=two_sum, parts=x, before=partial, after=[begun], **wide)
-        sent[1].append(summed(keep, send, [aux_sum]))
-        token = [sent[1][-1][0]]
-    one_part = partial
-    one = pair_sum(partial, n_pair, aux)
-    begun, aux_sum, first = project(one, one_part, crossed)
-    first = first[:h]
+        sent[1].append(summed(keep, send, [second]))
+        token = [sent[1][-1][0][0]]
+    one = pair_sum(partial, n_pair)
+    begun, aux_sum = project(one)
+    first = aux_sum[:h]
     projected[1][0] = first
 
-    def last_sum(keep, send, after):
+    def last_sum(keep, send, after, split_in=1):
         near = [aux_swap(x, distance=1) for x in send]
-        own, far = joined(keep, near, 2, after)
-        return own, aux_swap(far, distance=2)
+        out = joined(keep, near, 2 * split_in, after)
+        return out[:split_in], [aux_swap(x, distance=2) for x in out[split_in:]]
 
     partial, last = None, [[], []]
     for c in range(chunks):
@@ -448,9 +448,9 @@
         if c == 0:
             keep, send, partial = over(c, kc, fitted=one, parts=x, before=partial, after=[begun], **wide)
             last[0].append(last_sum(keep, send, [aux_sum]))
-            keep, send = over(c + 1, kc, fitted=one, after=[last[0][-1][0]])
+            keep, send = over(c + 1, kc, fitted=one, after=[last[0][-1][0][0]])
             last[0].append(last_sum(keep, send, []))
-            token = [last[0][-1][0]]
+            token = [last[0][-1][0][0]]
         else:
             (partial,) = over(c, kc, parts=x, before=partial, **wide)
     ends = [[], []]
@@ -472,21 +472,19 @@
         norms[g] = norms[g] + square
         return new[0]
 
-    two_part = partial
     two_sum = pair_sum(
         partial,
         n_pair,
-        aux,
         (lambda after: finish(0, 0, first, after), lambda after: finish(0, 1, first, after)),
     )
-    begun, aux_sum, second = project(two_sum, two_part, crossed)
-    second = second[:h]
+    begun, aux_sum = project(two_sum)
+    second = aux_sum[:h]
     projected[1][1] = second
     token = [begun]
     for c in range(chunks):
-        keep, send = over(c, kc, fitted=two_sum, after=token, pieces=2 * PIECES)
+        keep, send = over(c, kc, fitted=two_sum, after=token)
         last[1].append(last_sum(keep, send, [aux_sum]))
-        token = [last[1][-1][0]]
+        token = [last[1][-1][0][0]]
     token = []
     for c in range(chunks):
         token = [finish(1, c, second, token)]

time: 695 us -> 692 us (level)
  Pallas kernels: 391 us -> 429 us
  starting transfers between devices: 114 us -> 87.2 us
  waiting for transfers between devices: 134 us -> 125 us
    pallas_call x44 -> x32, Pallas kernels: 3.34 us -> 63.3 us  [small(): pl.pallas_call(body, out_shape=out, in_specs=specs, out_specs=tuple((pl.B...]
    ppermute x143 -> x108, starting transfers between devices: 114 us -> 87.2 us  [swap_with(): return lax.ppermute(value, axis, [(i, i ^ distance) for i in range(size)])]
    pallas_call x15 -> x12, Pallas kernels: 290 us -> 268 us  [pass_over(): pl.pallas_call(kernel, out_shape=tuple(shapes), grid_spec=pltpu.PrefetchS...]
    ppermute x143 -> x108, waiting for transfers between devices: 134 us -> 125 us  [swap_with(): return lax.ppermute(value, axis, [(i, i ^ distance) for i in range(size)])]
    unnamed x250 -> x194, local copies, waits for them, and re-layouts: 35.5 us -> 28.7 us
  transfers between devices with their start and end apart: 143 -> 108, of which waited for: 83 -> 53; matrix products, arithmetic and copies ran while one was open for 0% -> 0% of each run, Pallas kernels for 49% -> 53%
where the time goes in v2:
time: 692 us; the launch traced here: 683 us
  Pallas kernels  429 us (62%)
  waiting for transfers between devices  125 us (18%)
  starting transfers between devices  87.2 us (13%)
  local copies, waits for them, and re-layouts  33.7 us (5%)
    pallas_call x12, Pallas kernels, pass_over(): pl.pallas_call(kernel, out_shape=tuple(shapes), grid_spec=pltpu.PrefetchS...  268 us
    ppermute x108, waiting for transfers between devices, swap_with(): return lax.ppermute(value, axis, [(i, i ^ distance) for i in range(size)])  125 us
    ppermute x108, starting transfers between devices, swap_with(): return lax.ppermute(value, axis, [(i, i ^ distance) for i in range(size)])  87.2 us
    pallas_call x8, Pallas kernels, assemble(): pl.pallas_call(kernel, out_shape=(*[jax.ShapeDtypeStruct((piece, columns)...  71.2 us
    pallas_call x32, Pallas kernels, small(): pl.pallas_call(body, out_shape=out, in_specs=specs, out_specs=tuple((pl.B...  63.3 us
    unnamed x194, local copies, waits for them, and re-layouts  28.7 us
    pallas_call x8, Pallas kernels, joined(): pl.pallas_call(kernel, out_shape=tuple([jax.ShapeDtypeStruct((height, col...  26.5 us
  transfers between devices with their start and end apart: 108, of which 53 were waited for; matrix products, arithmetic and copies ran while one was open for 0% of the time, Pallas kernels for 53%

profile of v2, /device:TPU:0, one launch (start us, length us, event | category | flops | bytes accessed | tf_op | source)
XLA Modules:
  0.0 682.6 jit_solution(2828406115769088240)
XLA Ops:
  0.6 3.8 fusion.10
  4.5 3.0 collective-permute-start
  7.4 46.1 %fit.4.refs_1_ = f32[384,1024]{1,0:T(8,128)} custom-call(f32[16384,1024]{1,0:T(8,128)} %refs_0_.7, f32[384,16384]{1,0:T(8,128)} %refs_5_.15), custom_call_target="tpu_custom_call" | custom-call | flops 1 | bytes 1 | tf_op jit(solution)/shard_map/fit/pallas_call | solution.py:136
  61.8 16.6 %fit.5.refs_4_.refs_8_ = f32[128,1152]{1,0:T(8,128)} custom-call(s32[1]{0:T(128)} %bitcast.refs_0_, f32[16384,1024]{1,0:T(8,128)} %refs_0_.7, f32[32,16384]{1,0:T(8,128)} %get-tuple-element.115.refs_2_, f32[32,16384]{1,0:T(8,128)} %collective-permute-done.refs_3_, f32[32,16384]{1,0:T(8,128)} %collective-permute-done.1.refs_4_, ...), custom_call_target="tpu_custom_call" | custom-call | flops 1 | bytes 1 | tf_op jit(solution)/shard_map/fit/pallas_call | solution.py:136
  84.1 16.9 %fit.6.refs_2_.refs_1_ = f32[128,1152]{1,0:T(8,128)} custom-call(s32[1]{0:T(128)} %bitcast.refs_0_, f32[16384,1024]{1,0:T(8,128)} %refs_0_.7, f32[32,16384]{1,0:T(8,128)} %get-tuple-element.115.refs_2_, f32[32,16384]{1,0:T(8,128)} %collective-permute-done.refs_3_, f32[32,16384]{1,0:T(8,128)} %collective-permute-done.1.refs_4_, ...), custom_call_target="tpu_custom_call" | custom-call | flops 1 | bytes 1 | tf_op jit(solution)/shard_map/fit/pallas_call | solution.py:136
  121.2 6.7 collective-permute-done.10.refs_1_
  150.5 24.3 %spreadfit.5 = (f32[64,8192]{1,0:T(8,128)}, f32[16,8192]{1,0:T(8,128)}, f32[16,8192]{1,0:T(8,128)}, f32[16,8192]{1,0:T(8,128)}, f32[16,8192]{1,0:T(8,128)}, /*index=5*/f32[128,1152]{1,0:T(8,128)}) custom-call(s32[1]{0:T(128)} %bitcast.refs_0_, f32[16384,1024]{1,0:T(8,128)} %refs_0_.7, f32[128,1152]{1,0:T(8,128)} %gather.5.refs_2_.refs_1_, ...), custom_call_target="tpu_custom_call" | custom-call | flops 1 | bytes 1 | tf_op jit(solution)/shard_map/spreadfit/pallas_call | solution.py:136
  178.7 2.9 project.4
  187.0 3.5 collective-permute-done.25.refs_1_
  194.0 3.2 joined.8.refs_10_.refs_0_
  198.9 24.2 %spreadfit.6 = (f32[64,8192]{1,0:T(8,128)}, f32[16,8192]{1,0:T(8,128)}, f32[16,8192]{1,0:T(8,128)}, f32[16,8192]{1,0:T(8,128)}, f32[16,8192]{1,0:T(8,128)}, /*index=5*/f32[128,1152]{1,0:T(8,128)}) custom-call(s32[1]{0:T(128)} %bitcast.refs_0_, f32[16384,1024]{1,0:T(8,128)} %refs_0_.7, f32[128,1152]{1,0:T(8,128)} %gather.5.refs_2_.refs_1_, ...), custom_call_target="tpu_custom_call" | custom-call | flops 1 | bytes 1 | tf_op jit(solution)/shard_map/spreadfit/pallas_call | solution.py:136
  230.4 3.6 joined.9.refs_8_.refs_0_
  241.4 6.8 collective-permute-done.29.refs_1_
  262.7 2.9 project.5
  265.6 9.4 %assemble.8 = (f32[16,8192]{1,0:T(8,128)}, f32[16,8192]{1,0:T(8,128)}, f32[16,8192]{1,0:T(8,128)}, f32[16,8192]{1,0:T(8,128)}, f32[64,128]{1,0:T(8,128)}) custom-call(f32[64,8192]{1,0:T(8,128)} %joined.8.refs_10_.refs_0_, f32[64,8192]{1,0:T(8,128)} %collective-permute-done.38.refs_1_, f32[32,16384]{1,0:T(8,128)} %get-tuple-element.115.refs_2_, ...), custom_call_target="tpu_custom_call" | custom-call | flops 1 | bytes 1 | tf_op jit(solution)/shard_map/assemble/pallas_call | solution.py:205
  279.7 24.2 %spreadfit.7 = (f32[64,8192]{1,0:T(8,128)}, f32[16,8192]{1,0:T(8,128)}, f32[16,8192]{1,0:T(8,128)}, f32[16,8192]{1,0:T(8,128)}, f32[16,8192]{1,0:T(8,128)}, /*index=5*/f32[128,1152]{1,0:T(8,128)}) custom-call(s32[1]{0:T(128)} %bitcast.refs_0_, f32[16384,1024]{1,0:T(8,128)} %refs_0_.7, f32[128,1152]{1,0:T(8,128)} %gather.7.refs_7_.refs_1_.refs_2_, ...), custom_call_target="tpu_custom_call" | custom-call | flops 1 | bytes 1 | tf_op jit(solution)/shard_map/spreadfit/pallas_call | solution.py:136
  308.5 3.2 joined.10.refs_7_.refs_0_
  313.8 9.4 %assemble.9 = (f32[16,8192]{1,0:T(8,128)}, f32[16,8192]{1,0:T(8,128)}, f32[16,8192]{1,0:T(8,128)}, f32[16,8192]{1,0:T(8,128)}, f32[64,128]{1,0:T(8,128)}) custom-call(f32[64,8192]{1,0:T(8,128)} %joined.9.refs_8_.refs_0_, f32[64,8192]{1,0:T(8,128)} %copy-done.7, f32[32,16384]{1,0:T(8,128)} %get-tuple-element.115.refs_2_, ...), custom_call_target="tpu_custom_call" | custom-call | flops 1 | bytes 1 | tf_op jit(solution)/shard_map/assemble/pallas_call | solution.py:205
  328.4 24.6 %spreadfit.8 = (f32[64,8192]{1,0:T(8,128)}, f32[16,8192]{1,0:T(8,128)}, f32[16,8192]{1,0:T(8,128)}, f32[16,8192]{1,0:T(8,128)}, f32[16,8192]{1,0:T(8,128)}, /*index=5*/f32[128,1152]{1,0:T(8,128)}) custom-call(s32[1]{0:T(128)} %bitcast.refs_0_, f32[16384,1024]{1,0:T(8,128)} %refs_0_.7, f32[128,1152]{1,0:T(8,128)} %gather.7.refs_7_.refs_1_.refs_2_, ...), custom_call_target="tpu_custom_call" | custom-call | flops 1 | bytes 1 | tf_op jit(solution)/shard_map/spreadfit/pallas_call | solution.py:136
  360.3 3.3 joined.11.refs_7_.refs_0_
  371.7 6.4 collective-permute-done.56.refs_1_
  383.8 3.1 collective-permute-done.57.refs_2_
  392.4 2.9 project.6
  395.3 9.4 %assemble.10 = (f32[16,8192]{1,0:T(8,128)}, f32[16,8192]{1,0:T(8,128)}, f32[16,8192]{1,0:T(8,128)}, f32[16,8192]{1,0:T(8,128)}, f32[64,128]{1,0:T(8,128)}) custom-call(f32[64,8192]{1,0:T(8,128)} %joined.10.refs_7_.refs_0_, f32[64,8192]{1,0:T(8,128)} %collective-permute-done.60.refs_1_, f32[32,16384]{1,0:T(8,128)} %copy-done, ...), custom_call_target="tpu_custom_call" | custom-call | flops 1 | bytes 1 | tf_op jit(solution)/shard_map/assemble/pallas_call | solution.py:205
  409.4 24.4 %spreadfit.9 = (f32[64,8192]{1,0:T(8,128)}, f32[16,8192]{1,0:T(8,128)}, f32[16,8192]{1,0:T(8,128)}, f32[16,8192]{1,0:T(8,128)}, f32[16,8192]{1,0:T(8,128)}, /*index=5*/f32[128,1152]{1,0:T(8,128)}) custom-call(s32[1]{0:T(128)} %bitcast.refs_0_, f32[16384,1024]{1,0:T(8,128)} %refs_0_.7, f32[128,1152]{1,0:T(8,128)} %gather.8.refs_1_.refs_2_, ...), custom_call_target="tpu_custom_call" | custom-call | flops 1 | bytes 1 | tf_op jit(solution)/shard_map/spreadfit/pallas_call | solution.py:136
  438.4 3.3 joined.12
  441.7 16.5 %spread.3 = (f32[64,8192]{1,0:T(8,128)}, f32[16,8192]{1,0:T(8,128)}, f32[16,8192]{1,0:T(8,128)}, f32[16,8192]{1,0:T(8,128)}, f32[16,8192]{1,0:T(8,128)}) custom-call(f32[16384,1024]{1,0:T(8,128)} %refs_0_.7, f32[128,1152]{1,0:T(8,128)} %gather.8.refs_1_.refs_2_, f32[32,8192]{1,0:T(8,128)} %get-tuple-element.182.refs_2_.refs_0_), custom_call_target="tpu_custom_call" | custom-call | flops 1 | bytes 1 | tf_op jit(solution)/shard_map/spread/pallas_call | solution.py:136
  462.7 3.2 joined.13
  467.2 9.4 %assemble.11 = (f32[16,8192]{1,0:T(8,128)}, f32[16,8192]{1,0:T(8,128)}, f32[16,8192]{1,0:T(8,128)}, f32[16,8192]{1,0:T(8,128)}, f32[64,128]{1,0:T(8,128)}) custom-call(f32[64,8192]{1,0:T(8,128)} %joined.11.refs_7_.refs_0_, f32[64,8192]{1,0:T(8,128)} %copy-done.6, f32[32,16384]{1,0:T(8,128)} %copy-done, f32[32,16384]{1,0:T(8,128)} %collective-permute-done.14.refs_4_.refs_3_, ...), custom_call_target="tpu_custom_call" | custom-call | flops 1 | bytes 1 | tf_op jit(solution)/shard_map/assemble/pallas_call | solution.py:205
  483.6 17.1 %fit.7.refs_1_ = f32[128,1152]{1,0:T(8,128)} custom-call(s32[1]{0:T(128)} %bitcast.refs_0_, f32[16384,1024]{1,0:T(8,128)} %refs_0_.7, f32[16,8192]{1,0:T(8,128)} %get-tuple-element.190.refs_2_, f32[16,8192]{1,0:T(8,128)} %get-tuple-element.191.refs_3_, f32[16,8192]{1,0:T(8,128)} %get-tuple-element.192.refs_4_, f32[16,8192]{1,0:T(8,128)} %get-tuple-element.193.refs_5_, ...), custom_call_target="tpu_custom_call" | custom-call | flops 1 | bytes 1 | tf_op jit(solution)/shard_map/fit/pallas_call | solution.py:136
  507.6 8.2 %assemble.12 = (f32[32,8192]{1,0:T(8,128)}, f32[32,128]{1,0:T(8,128)}) custom-call(f32[32,8192]{1,0:T(8,128)} %get-tuple-element.182.refs_2_.refs_0_, f32[32,8192]{1,0:T(8,128)} %copy-done.10, f32[16,8192]{1,0:T(8,128)} %get-tuple-element.145.refs_3_.refs_2_, f32[16,8192]{1,0:T(8,128)} %get-tuple-element.146.refs_4_.refs_3_, f32[32,384]{1,0:T(8,128)} %slice.48.refs_4_, ...), custom_call_target="tpu_custom_call" | custom-call | flops 1 | bytes 1 | tf_op jit(solution)/shard_map/assemble/pallas_call | solution.py:205
  518.4 3.0 collective-permute-start.89
  521.3 3.6 collective-permute-done.85.refs_1_
  525.9 8.2 %assemble.13 = (f32[32,8192]{1,0:T(8,128)}, f32[32,128]{1,0:T(8,128)}) custom-call(f32[32,8192]{1,0:T(8,128)} %get-tuple-element.189.refs_7_.refs_0_, f32[32,8192]{1,0:T(8,128)} %copy-done.9, f32[16,8192]{1,0:T(8,128)} %get-tuple-element.156.refs_3_.refs_2_, f32[16,8192]{1,0:T(8,128)} %get-tuple-element.157.refs_4_.refs_3_, f32[32,384]{1,0:T(8,128)} %slice.48.refs_4_, ...), custom_call_target="tpu_custom_call" | custom-call | flops 1 | bytes 1 | tf_op jit(solution)/shard_map/assemble/pallas_call | solution.py:205
  548.7 2.9 project.7
  551.6 16.8 %spread.4 = (f32[64,8192]{1,0:T(8,128)}, f32[16,8192]{1,0:T(8,128)}, f32[16,8192]{1,0:T(8,128)}, f32[16,8192]{1,0:T(8,128)}, f32[16,8192]{1,0:T(8,128)}) custom-call(f32[16384,1024]{1,0:T(8,128)} %refs_0_.7, f32[128,1152]{1,0:T(8,128)} %gather.9.refs_1_, f32[64,384]{1,0:T(8,128)} %get-tuple-element.202.refs_2_.refs_0_), custom_call_target="tpu_custom_call" | custom-call | flops 1 | bytes 1 | tf_op jit(solution)/shard_map/spread/pallas_call | solution.py:136
  574.9 3.7 collective-permute-done.98.refs_1_
  582.3 3.3 joined.14
  585.6 16.5 %spread.5 = (f32[64,8192]{1,0:T(8,128)}, f32[16,8192]{1,0:T(8,128)}, f32[16,8192]{1,0:T(8,128)}, f32[16,8192]{1,0:T(8,128)}, f32[16,8192]{1,0:T(8,128)}) custom-call(f32[16384,1024]{1,0:T(8,128)} %refs_0_.7, f32[128,1152]{1,0:T(8,128)} %gather.9.refs_1_, f32[32,8192]{1,0:T(8,128)} %get-tuple-element.209.refs_0_.refs_2_), custom_call_target="tpu_custom_call" | custom-call | flops 1 | bytes 1 | tf_op jit(solution)/shard_map/spread/pallas_call | solution.py:136
  607.4 3.3 joined.15
  612.8 16.6 %collective-permute-done.99.refs_1_ = f32[32,8192]{1,0:T(8,128)S(1)} collective-permute-done((f32[32,8192]{1,0:T(8,128)}, f32[32,8192]{1,0:T(8,128)S(1)}, u32[]{:S(2)}, u32[]{:S(2)}) %collective-permute-start.99) | collective-permute-done | bytes 1048608 | tf_op jit(solution)/shard_map/ppermute | solution.py:225
  630.4 8.2 %assemble.14 = (f32[32,8192]{1,0:T(8,128)}, f32[32,128]{1,0:T(8,128)}) custom-call(f32[32,8192]{1,0:T(8,128)} %get-tuple-element.209.refs_0_.refs_2_, f32[32,8192]{1,0:T(8,128)} %copy-done.12, f32[16,8192]{1,0:T(8,128)} %get-tuple-element.171.refs_3_.refs_2_, f32[16,8192]{1,0:T(8,128)} %get-tuple-element.172.refs_4_.refs_3_, f32[32,384]{1,0:T(8,128)} %slice.49.refs_4_, ...), custom_call_target="tpu_custom_call" | custom-call | flops 1 | bytes 1 | tf_op jit(solution)/shard_map/assemble/pallas_call | solution.py:205
  638.6 12.4 %collective-permute-done.104.refs_1_ = f32[32,8192]{1,0:T(8,128)S(1)} collective-permute-done((f32[32,8192]{1,0:T(8,128)}, f32[32,8192]{1,0:T(8,128)S(1)}, u32[]{:S(2)}, u32[]{:S(2)}) %collective-permute-start.104) | collective-permute-done | bytes 1048608 | tf_op jit(solution)/shard_map/ppermute | solution.py:225
  652.0 9.1 %assemble.15 = (f32[32,8192]{1,0:T(8,128)}, f32[32,128]{1,0:T(8,128)}) custom-call(f32[32,8192]{1,0:T(8,128)} %get-tuple-element.217.refs_0_, f32[32,8192]{1,0:T(8,128)} %copy-done.11, f32[16,8192]{1,0:T(8,128)} %get-tuple-element.190.refs_2_, f32[16,8192]{1,0:T(8,128)} %get-tuple-element.191.refs_3_, f32[32,384]{1,0:T(8,128)} %slice.49.refs_4_, ...), custom_call_target="tpu_custom_call" | custom-call | flops 1 | bytes 1 | tf_op jit(solution)/shard_map/assemble/pallas_call | solution.py:205
  663.0 3.3 collective-permute-done.105
  670.6 4.0 collective-permute-start.107
  674.6 2.9 collective-permute-done.107
  678.5 3.7 maximum_divide_fusion
  (442 shorter events, 216.9 us)
Async XLA Ops:
  4.5 49.1 %collective-permute-start = (f32[32,16384]{1,0:T(8,128)}, f32[32,16384]{1,0:T(8,128)}, u32[]{:S(2)}, u32[]{:S(2)}) collective-permute-start(f32[32,16384]{1,0:T(8,128)} %get-tuple-element.115.refs_2_), channel_id=1, source_target_pairs={{0,2},{1,3},{2,0},{3,1},{4,6},{5,7},{6,4},{7,5},{8,10},{9,11},{10,... | collective-permute-start | bytes 6291464 | tf_op jit(solution)/shard_map/ppermute | solution.py:225
  53.5 7.8 %collective-permute-start.1 = (f32[32,16384]{1,0:T(8,128)}, f32[32,16384]{1,0:T(8,128)}, u32[]{:S(2)}, u32[]{:S(2)}) collective-permute-start(f32[32,16384]{1,0:T(8,128)} %get-tuple-element.115.refs_2_), channel_id=1, source_target_pairs={{0,1},{1,0},{2,3},{3,2},{4,5},{5,4},{6,7},{7,6},{8,9},{9,8},{10,11... | collective-permute-start | bytes 6291464 | tf_op jit(solution)/shard_map/ppermute | solution.py:225
  53.6 8.2 %collective-permute-start.2 = (f32[32,16384]{1,0:T(8,128)}, f32[32,16384]{1,0:T(8,128)}, u32[]{:S(2)}, u32[]{:S(2)}) collective-permute-start(f32[32,16384]{1,0:T(8,128)} %collective-permute-done.refs_3_), channel_id=1, source_target_pairs={{0,1},{1,0},{2,3},{3,2},{4,5},{5,4},{6,7},{7,6},{8,9},{9,8},{10,11... | collective-permute-start | bytes 6291464 | tf_op jit(solution)/shard_map/ppermute | solution.py:225
  54.1 88.7 %collective-permute-start.14 = (f32[32,16384]{1,0:T(8,128)S(1)}, f32[32,16384]{1,0:T(8,128)}, u32[]{:S(2)}, u32[]{:S(2)}) collective-permute-start(f32[32,16384]{1,0:T(8,128)S(1)} %get-tuple-element.125.refs_3_.refs_2_), channel_id=1, source_target_pairs={{0,2},{1,3},{2,0},{3,1},{4,6},{5,7},{6,4},{7,5},{8,10},{9,11},{10,... | collective-permute-start | bytes 6291464 | tf_op jit(solution)/shard_map/ppermute | solution.py:225
  58.3 20.1 %collective-permute-start.3 = (f32[96,1024]{1,0:T(8,128)}, f32[96,1024]{1,0:T(8,128)S(1)}, u32[]{:S(2)}, u32[]{:S(2)}) collective-permute-start(f32[96,1024]{1,0:T(8,128)} %get-tuple-element.118), channel_id=1, source_target_pairs={{0,4},{4,0},{8,12},{12,8},{16,20},{20,16},{24,28},{28,24},{1,5},{5... | collective-permute-start | bytes 1179656 | tf_op jit(solution)/shard_map/ppermute | solution.py:225
  59.8 18.6 %collective-permute-start.4 = (f32[96,1024]{1,0:T(8,128)}, f32[96,1024]{1,0:T(8,128)S(1)}, u32[]{:S(2)}, u32[]{:S(2)}) collective-permute-start(f32[96,1024]{1,0:T(8,128)} %get-tuple-element.119), channel_id=1, source_target_pairs={{0,8},{4,12},{8,0},{12,4},{16,24},{20,28},{24,16},{28,20},{1,9},{5... | collective-permute-start | bytes 1179656 | tf_op jit(solution)/shard_map/ppermute | solution.py:225
  61.4 17.6 %collective-permute-start.5 = (f32[96,1024]{1,0:T(8,128)}, f32[96,1024]{1,0:T(8,128)}, u32[]{:S(2)}, u32[]{:S(2)}) collective-permute-start(f32[96,1024]{1,0:T(8,128)} %get-tuple-element.120), channel_id=1, source_target_pairs={{0,12},{4,8},{8,4},{12,0},{16,28},{20,24},{24,20},{28,16},{1,13},{... | collective-permute-start | bytes 1179656 | tf_op jit(solution)/shard_map/ppermute | solution.py:225
  81.5 20.0 %collective-permute-start.6 = (f32[96,1024]{1,0:T(8,128)}, f32[96,1024]{1,0:T(8,128)S(1)}, u32[]{:S(2)}, u32[]{:S(2)}) collective-permute-start(f32[96,1024]{1,0:T(8,128)} %total.14.refs_9_.refs_0_), channel_id=1, source_target_pairs={{0,16},{4,20},{8,24},{12,28},{16,0},{20,4},{24,8},{28,12},{1,17},{... | collective-permute-start | bytes 1179656 | tf_op jit(solution)/shard_map/ppermute | solution.py:225
  118.5 9.4 %collective-permute-start.10 = (f32[32,1152]{1,0:T(8,128)}, f32[32,1152]{1,0:T(8,128)S(1)}, u32[]{:S(2)}, u32[]{:S(2)}) collective-permute-start(f32[32,1152]{1,0:T(8,128)} %total.16.refs_0_), channel_id=1, source_target_pairs={{0,16},{4,20},{8,24},{12,28},{16,0},{20,4},{24,8},{28,12},{1,17},{... | collective-permute-start | bytes 442376 | tf_op jit(solution)/shard_map/ppermute | solution.py:225
  132.3 7.7 %collective-permute-start.13 = (f32[32,1152]{1,0:T(8,128)}, f32[32,1152]{1,0:T(8,128)S(1)}, u32[]{:S(2)}, u32[]{:S(2)}) collective-permute-start(f32[32,1152]{1,0:T(8,128)} %total.17.refs_1_), channel_id=1, source_target_pairs={{0,12},{4,8},{8,4},{12,0},{16,28},{20,24},{24,20},{28,16},{1,13},{... | collective-permute-start | bytes 442376 | tf_op jit(solution)/shard_map/ppermute | solution.py:225
  142.8 7.7 %collective-permute-start.16 = (f32[32,16384]{1,0:T(8,128)}, f32[32,16384]{1,0:T(8,128)}, u32[]{:S(2)}, u32[]{:S(2)}) collective-permute-start(f32[32,16384]{1,0:T(8,128)} %collective-permute-done.14.refs_4_.refs_3_), channel_id=1, source_target_pairs={{0,1},{1,0},{2,3},{3,2},{4,5},{5,4},{6,7},{7,6},{8,9},{9,8},{10,11... | collective-permute-start | bytes 6291464 | tf_op jit(solution)/shard_map/ppermute | solution.py:225
  143.3 32.1 %collective-permute-start.21 = (f32[96,1024]{1,0:T(8,128)S(1)}, f32[96,1024]{1,0:T(8,128)S(1)}, u32[]{:S(2)}, u32[]{:S(2)}) collective-permute-start(f32[96,1024]{1,0:T(8,128)S(1)} %copy-done.5), channel_id=1, source_target_pairs={{0,4},{4,0},{8,12},{12,8},{16,20},{20,16},{24,28},{28,24},{1,5},{5... | collective-permute-start | bytes 1179656 | tf_op jit(solution)/shard_map/ppermute | solution.py:225
  144.2 31.4 %collective-permute-start.22 = (f32[96,1024]{1,0:T(8,128)S(1)}, f32[96,1024]{1,0:T(8,128)}, u32[]{:S(2)}, u32[]{:S(2)}) collective-permute-start(f32[96,1024]{1,0:T(8,128)S(1)} %copy-done.5), channel_id=1, source_target_pairs={{0,8},{4,12},{8,0},{12,4},{16,24},{20,28},{24,16},{28,20},{1,9},{5... | collective-permute-start | bytes 1179656 | tf_op jit(solution)/shard_map/ppermute | solution.py:225
  145.7 30.2 %collective-permute-start.23 = (f32[96,1024]{1,0:T(8,128)S(1)}, f32[96,1024]{1,0:T(8,128)}, u32[]{:S(2)}, u32[]{:S(2)}) collective-permute-start(f32[96,1024]{1,0:T(8,128)S(1)} %copy-done.5), channel_id=1, source_target_pairs={{0,12},{4,8},{8,4},{12,0},{16,28},{20,24},{24,20},{28,16},{1,13},{... | collective-permute-start | bytes 1179656 | tf_op jit(solution)/shard_map/ppermute | solution.py:225
  174.8 17.9 %collective-permute-start.17 = (f32[16,8192]{1,0:T(8,128)}, f32[16,8192]{1,0:T(8,128)S(1)}, u32[]{:S(2)}, u32[]{:S(2)}) collective-permute-start(f32[16,8192]{1,0:T(8,128)} %get-tuple-element.129), channel_id=1, source_target_pairs={{0,1},{1,0},{2,3},{3,2},{4,5},{5,4},{6,7},{7,6},{8,9},{9,8},{10,11... | collective-permute-start | bytes 1572872 | tf_op jit(solution)/shard_map/ppermute | solution.py:225
  175.0 17.7 %collective-permute-start.18 = (f32[16,8192]{1,0:T(8,128)}, f32[16,8192]{1,0:T(8,128)S(1)}, u32[]{:S(2)}, u32[]{:S(2)}) collective-permute-start(f32[16,8192]{1,0:T(8,128)} %get-tuple-element.130), channel_id=1, source_target_pairs={{0,1},{1,0},{2,3},{3,2},{4,5},{5,4},{6,7},{7,6},{8,9},{9,8},{10,11... | collective-permute-start | bytes 1572872 | tf_op jit(solution)/shard_map/ppermute | solution.py:225
  175.4 17.3 %collective-permute-start.19 = (f32[16,8192]{1,0:T(8,128)}, f32[16,8192]{1,0:T(8,128)S(1)}, u32[]{:S(2)}, u32[]{:S(2)}) collective-permute-start(f32[16,8192]{1,0:T(8,128)} %get-tuple-element.131), channel_id=1, source_target_pairs={{0,1},{1,0},{2,3},{3,2},{4,5},{5,4},{6,7},{7,6},{8,9},{9,8},{10,11... | collective-permute-start | bytes 1572872 | tf_op jit(solution)/shard_map/ppermute | solution.py:225
  175.5 17.2 %collective-permute-start.20 = (f32[16,8192]{1,0:T(8,128)}, f32[16,8192]{1,0:T(8,128)S(1)}, u32[]{:S(2)}, u32[]{:S(2)}) collective-permute-start(f32[16,8192]{1,0:T(8,128)} %get-tuple-element.132), channel_id=1, source_target_pairs={{0,1},{1,0},{2,3},{3,2},{4,5},{5,4},{6,7},{7,6},{8,9},{9,8},{10,11... | collective-permute-start | bytes 1572872 | tf_op jit(solution)/shard_map/ppermute | solution.py:225
  197.3 68.4 %collective-permute-start.38 = (f32[64,8192]{1,0:T(8,128)}, f32[64,8192]{1,0:T(8,128)}, u32[]{:S(2)}, u32[]{:S(2)}) collective-permute-start(f32[64,8192]{1,0:T(8,128)} %joined.8.refs_10_.refs_0_), channel_id=1, source_target_pairs={{0,2},{1,3},{2,0},{3,1},{4,6},{5,7},{6,4},{7,5},{8,10},{9,11},{10,... | collective-permute-start | bytes 6291464 | tf_op jit(solution)/shard_map/ppermute | solution.py:225
  226.1 8.5 %collective-permute-start.26 = (f32[32,1152]{1,0:T(8,128)}, f32[32,1152]{1,0:T(8,128)S(1)}, u32[]{:S(2)}, u32[]{:S(2)}) collective-permute-start(f32[32,1152]{1,0:T(8,128)} %get-tuple-element.137), channel_id=1, source_target_pairs={{0,4},{4,0},{8,12},{12,8},{16,20},{20,16},{24,28},{28,24},{1,5},{5... | collective-permute-start | bytes 442376 | tf_op jit(solution)/shard_map/ppermute | solution.py:225
  226.9 7.6 %collective-permute-start.27 = (f32[32,1152]{1,0:T(8,128)}, f32[32,1152]{1,0:T(8,128)S(1)}, u32[]{:S(2)}, u32[]{:S(2)}) collective-permute-start(f32[32,1152]{1,0:T(8,128)} %get-tuple-element.138), channel_id=1, source_target_pairs={{0,8},{4,12},{8,0},{12,4},{16,24},{20,28},{24,16},{28,20},{1,9},{5... | collective-permute-start | bytes 442376 | tf_op jit(solution)/shard_map/ppermute | solution.py:225
  228.5 8.0 %collective-permute-start.28 = (f32[32,1152]{1,0:T(8,128)}, f32[32,1152]{1,0:T(8,128)S(1)}, u32[]{:S(2)}, u32[]{:S(2)}) collective-permute-start(f32[32,1152]{1,0:T(8,128)} %get-tuple-element.139), channel_id=1, source_target_pairs={{0,12},{4,8},{8,4},{12,0},{16,28},{20,24},{24,20},{28,16},{1,13},{... | collective-permute-start | bytes 442376 | tf_op jit(solution)/shard_map/ppermute | solution.py:225
  234.0 78.4 %collective-permute-start.37 = (f32[64,8192]{1,0:T(8,128)}, f32[64,8192]{1,0:T(8,128)S(1)}, u32[]{:S(2)}, u32[]{:S(2)}) collective-permute-start(f32[64,8192]{1,0:T(8,128)} %joined.9.refs_8_.refs_0_), channel_id=1, source_target_pairs={{0,2},{1,3},{2,0},{3,1},{4,6},{5,7},{6,4},{7,5},{8,10},{9,11},{10,... | collective-permute-start | bytes 6291464 | tf_op jit(solution)/shard_map/ppermute | solution.py:225
  239.0 9.2 %collective-permute-start.29 = (f32[32,1152]{1,0:T(8,128)}, f32[32,1152]{1,0:T(8,128)S(1)}, u32[]{:S(2)}, u32[]{:S(2)}) collective-permute-start(f32[32,1152]{1,0:T(8,128)} %total.19.refs_0_), channel_id=1, source_target_pairs={{0,16},{4,20},{8,24},{12,28},{16,0},{20,4},{24,8},{28,12},{1,17},{... | collective-permute-start | bytes 442376 | tf_op jit(solution)/shard_map/ppermute | solution.py:225
  252.4 7.7 %collective-permute-start.32 = (f32[32,1152]{1,0:T(8,128)}, f32[32,1152]{1,0:T(8,128)S(1)}, u32[]{:S(2)}, u32[]{:S(2)}) collective-permute-start(f32[32,1152]{1,0:T(8,128)} %total.20.refs_1_), channel_id=1, source_target_pairs={{0,12},{4,8},{8,4},{12,0},{16,28},{20,24},{24,20},{28,16},{1,13},{... | collective-permute-start | bytes 442376 | tf_op jit(solution)/shard_map/ppermute | solution.py:225
  265.6 10.5 %collective-permute-start.47 = (f32[64,384]{1,0:T(8,128)}, f32[64,384]{1,0:T(8,128)S(1)}, u32[]{:S(2)}, u32[]{:S(2)}) collective-permute-start(f32[64,384]{1,0:T(8,128)} %get-tuple-element.155), channel_id=1, source_target_pairs={{0,1},{1,0},{2,3},{3,2},{4,5},{5,4},{6,7},{7,6},{8,9},{9,8},{10,11... | collective-permute-start | bytes 294920 | tf_op jit(solution)/shard_map/ppermute | solution.py:225
  278.4 26.5 %collective-permute-start.48 = (f32[64,384]{1,0:T(8,128)}, f32[64,384]{1,0:T(8,128)S(1)}, u32[]{:S(2)}, u32[]{:S(2)}) collective-permute-start(f32[64,384]{1,0:T(8,128)} %total.21.refs_0_), channel_id=1, source_target_pairs={{0,2},{1,3},{2,0},{3,1},{4,6},{5,7},{6,4},{7,5},{8,10},{9,11},{10,... | collective-permute-start | bytes 294920 | tf_op jit(solution)/shard_map/ppermute | solution.py:225
  311.8 83.5 %collective-permute-start.60 = (f32[64,8192]{1,0:T(8,128)}, f32[64,8192]{1,0:T(8,128)}, u32[]{:S(2)}, u32[]{:S(2)}) collective-permute-start(f32[64,8192]{1,0:T(8,128)} %joined.10.refs_7_.refs_0_), channel_id=1, source_target_pairs={{0,2},{1,3},{2,0},{3,1},{4,6},{5,7},{6,4},{7,5},{8,10},{9,11},{10,... | collective-permute-start | bytes 6291464 | tf_op jit(solution)/shard_map/ppermute | solution.py:225
  356.0 8.9 %collective-permute-start.53 = (f32[32,1152]{1,0:T(8,128)}, f32[32,1152]{1,0:T(8,128)S(1)}, u32[]{:S(2)}, u32[]{:S(2)}) collective-permute-start(f32[32,1152]{1,0:T(8,128)} %get-tuple-element.163), channel_id=1, source_target_pairs={{0,4},{4,0},{8,12},{12,8},{16,20},{20,16},{24,28},{28,24},{1,5},{5... | collective-permute-start | bytes 442376 | tf_op jit(solution)/shard_map/ppermute | solution.py:225
  356.8 8.1 %collective-permute-start.54 = (f32[32,1152]{1,0:T(8,128)}, f32[32,1152]{1,0:T(8,128)S(1)}, u32[]{:S(2)}, u32[]{:S(2)}) collective-permute-start(f32[32,1152]{1,0:T(8,128)} %get-tuple-element.164), channel_id=1, source_target_pairs={{0,8},{4,12},{8,0},{12,4},{16,24},{20,28},{24,16},{28,20},{1,9},{5... | collective-permute-start | bytes 442376 | tf_op jit(solution)/shard_map/ppermute | solution.py:225
  358.2 8.2 %collective-permute-start.55 = (f32[32,1152]{1,0:T(8,128)}, f32[32,1152]{1,0:T(8,128)S(1)}, u32[]{:S(2)}, u32[]{:S(2)}) collective-permute-start(f32[32,1152]{1,0:T(8,128)} %get-tuple-element.165), channel_id=1, source_target_pairs={{0,12},{4,8},{8,4},{12,0},{16,28},{20,24},{24,20},{28,16},{1,13},{... | collective-permute-start | bytes 442376 | tf_op jit(solution)/shard_map/ppermute | solution.py:225
  363.5 102.4 %collective-permute-start.76 = (f32[64,8192]{1,0:T(8,128)}, f32[64,8192]{1,0:T(8,128)S(1)}, u32[]{:S(2)}, u32[]{:S(2)}) collective-permute-start(f32[64,8192]{1,0:T(8,128)} %joined.11.refs_7_.refs_0_), channel_id=1, source_target_pairs={{0,2},{1,3},{2,0},{3,1},{4,6},{5,7},{6,4},{7,5},{8,10},{9,11},{10,... | collective-permute-start | bytes 6291464 | tf_op jit(solution)/shard_map/ppermute | solution.py:225
  368.9 9.1 %collective-permute-start.56 = (f32[32,1152]{1,0:T(8,128)}, f32[32,1152]{1,0:T(8,128)S(1)}, u32[]{:S(2)}, u32[]{:S(2)}) collective-permute-start(f32[32,1152]{1,0:T(8,128)} %total.22.refs_0_), channel_id=1, source_target_pairs={{0,16},{4,20},{8,24},{12,28},{16,0},{20,4},{24,8},{28,12},{1,17},{... | collective-permute-start | bytes 442376 | tf_op jit(solution)/shard_map/ppermute | solution.py:225
  382.2 7.5 %collective-permute-start.59 = (f32[32,1152]{1,0:T(8,128)}, f32[32,1152]{1,0:T(8,128)S(1)}, u32[]{:S(2)}, u32[]{:S(2)}) collective-permute-start(f32[32,1152]{1,0:T(8,128)} %total.23.refs_1_), channel_id=1, source_target_pairs={{0,12},{4,8},{8,4},{12,0},{16,28},{20,24},{24,20},{28,16},{1,13},{... | collective-permute-start | bytes 442376 | tf_op jit(solution)/shard_map/ppermute | solution.py:225
  395.3 10.5 %collective-permute-start.73 = (f32[64,384]{1,0:T(8,128)}, f32[64,384]{1,0:T(8,128)S(1)}, u32[]{:S(2)}, u32[]{:S(2)}) collective-permute-start(f32[64,384]{1,0:T(8,128)} %get-tuple-element.181), channel_id=1, source_target_pairs={{0,1},{1,0},{2,3},{3,2},{4,5},{5,4},{6,7},{7,6},{8,9},{9,8},{10,11... | collective-permute-start | bytes 294920 | tf_op jit(solution)/shard_map/ppermute | solution.py:225
  408.0 26.8 %collective-permute-start.74 = (f32[64,384]{1,0:T(8,128)}, f32[64,384]{1,0:T(8,128)S(1)}, u32[]{:S(2)}, u32[]{:S(2)}) collective-permute-start(f32[64,384]{1,0:T(8,128)} %total.24.refs_0_), channel_id=1, source_target_pairs={{0,2},{1,3},{2,0},{3,1},{4,6},{5,7},{6,4},{7,5},{8,10},{9,11},{10,... | collective-permute-start | bytes 294920 | tf_op jit(solution)/shard_map/ppermute | solution.py:225
  477.1 29.6 %collective-permute-start.75 = (f32[32,8192]{1,0:T(8,128)}, f32[32,8192]{1,0:T(8,128)S(1)}, u32[]{:S(2)}, u32[]{:S(2)}) collective-permute-start(f32[32,8192]{1,0:T(8,128)} %get-tuple-element.183), channel_id=1, source_target_pairs={{0,2},{1,3},{2,0},{3,1},{4,6},{5,7},{6,4},{7,5},{8,10},{9,11},{10,... | collective-permute-start | bytes 3145736 | tf_op jit(solution)/shard_map/ppermute | solution.py:225
  478.4 46.5 %collective-permute-start.85 = (f32[32,8192]{1,0:T(8,128)}, f32[32,8192]{1,0:T(8,128)S(1)}, u32[]{:S(2)}, u32[]{:S(2)}) collective-permute-start(f32[32,8192]{1,0:T(8,128)} %get-tuple-element.197), channel_id=1, source_target_pairs={{0,2},{1,3},{2,0},{3,1},{4,6},{5,7},{6,4},{7,5},{8,10},{9,11},{10,... | collective-permute-start | bytes 3145736 | tf_op jit(solution)/shard_map/ppermute | solution.py:225
  502.5 13.2 %collective-permute-start.86 = (f32[32,1152]{1,0:T(8,128)}, f32[32,1152]{1,0:T(8,128)S(1)}, u32[]{:S(2)}, u32[]{:S(2)}) collective-permute-start(f32[32,1152]{1,0:T(8,128)} %get-tuple-element.198), channel_id=1, source_target_pairs={{0,4},{4,0},{8,12},{12,8},{16,20},{20,16},{24,28},{28,24},{1,5},{5... | collective-permute-start | bytes 442376 | tf_op jit(solution)/shard_map/ppermute | solution.py:225
  503.5 12.3 %collective-permute-start.87 = (f32[32,1152]{1,0:T(8,128)}, f32[32,1152]{1,0:T(8,128)S(1)}, u32[]{:S(2)}, u32[]{:S(2)}) collective-permute-start(f32[32,1152]{1,0:T(8,128)} %get-tuple-element.199), channel_id=1, source_target_pairs={{0,8},{4,12},{8,0},{12,4},{16,24},{20,28},{24,16},{28,20},{1,9},{5... | collective-permute-start | bytes 442376 | tf_op jit(solution)/shard_map/ppermute | solution.py:225
  505.0 10.9 %collective-permute-start.88 = (f32[32,1152]{1,0:T(8,128)}, f32[32,1152]{1,0:T(8,128)S(1)}, u32[]{:S(2)}, u32[]{:S(2)}) collective-permute-start(f32[32,1152]{1,0:T(8,128)} %get-tuple-element.200), channel_id=1, source_target_pairs={{0,12},{4,8},{8,4},{12,0},{16,28},{20,24},{24,20},{28,16},{1,13},{... | collective-permute-start | bytes 442376 | tf_op jit(solution)/shard_map/ppermute | solution.py:225
  518.4 15.8 %collective-permute-start.89 = (f32[32,1152]{1,0:T(8,128)}, f32[32,1152]{1,0:T(8,128)S(1)}, u32[]{:S(2)}, u32[]{:S(2)}) collective-permute-start(f32[32,1152]{1,0:T(8,128)} %total.25.refs_7_.refs_0_), channel_id=1, source_target_pairs={{0,16},{4,20},{8,24},{12,28},{16,0},{20,4},{24,8},{28,12},{1,17},{... | collective-permute-start | bytes 442376 | tf_op jit(solution)/shard_map/ppermute | solution.py:225
  568.4 12.4 %collective-permute-start.93 = (f32[16,8192]{1,0:T(8,128)}, f32[16,8192]{1,0:T(8,128)S(1)}, u32[]{:S(2)}, u32[]{:S(2)}) collective-permute-start(f32[16,8192]{1,0:T(8,128)} %get-tuple-element.204), channel_id=1, source_target_pairs={{0,1},{1,0},{2,3},{3,2},{4,5},{5,4},{6,7},{7,6},{8,9},{9,8},{10,11... | collective-permute-start | bytes 1572872 | tf_op jit(solution)/shard_map/ppermute | solution.py:225
  568.4 12.4 %collective-permute-start.94 = (f32[16,8192]{1,0:T(8,128)}, f32[16,8192]{1,0:T(8,128)S(1)}, u32[]{:S(2)}, u32[]{:S(2)}) collective-permute-start(f32[16,8192]{1,0:T(8,128)} %get-tuple-element.205), channel_id=1, source_target_pairs={{0,1},{1,0},{2,3},{3,2},{4,5},{5,4},{6,7},{7,6},{8,9},{9,8},{10,11... | collective-permute-start | bytes 1572872 | tf_op jit(solution)/shard_map/ppermute | solution.py:225
  568.9 12.0 %collective-permute-start.95 = (f32[16,8192]{1,0:T(8,128)}, f32[16,8192]{1,0:T(8,128)S(1)}, u32[]{:S(2)}, u32[]{:S(2)}) collective-permute-start(f32[16,8192]{1,0:T(8,128)} %get-tuple-element.206), channel_id=1, source_target_pairs={{0,1},{1,0},{2,3},{3,2},{4,5},{5,4},{6,7},{7,6},{8,9},{9,8},{10,11... | collective-permute-start | bytes 1572872 | tf_op jit(solution)/shard_map/ppermute | solution.py:225
  569.0 11.9 %collective-permute-start.96 = (f32[16,8192]{1,0:T(8,128)}, f32[16,8192]{1,0:T(8,128)S(1)}, u32[]{:S(2)}, u32[]{:S(2)}) collective-permute-start(f32[16,8192]{1,0:T(8,128)} %get-tuple-element.207), channel_id=1, source_target_pairs={{0,1},{1,0},{2,3},{3,2},{4,5},{5,4},{6,7},{7,6},{8,9},{9,8},{10,11... | collective-permute-start | bytes 1572872 | tf_op jit(solution)/shard_map/ppermute | solution.py:225
  603.2 26.2 %collective-permute-start.99 = (f32[32,8192]{1,0:T(8,128)}, f32[32,8192]{1,0:T(8,128)S(1)}, u32[]{:S(2)}, u32[]{:S(2)}) collective-permute-start(f32[32,8192]{1,0:T(8,128)} %get-tuple-element.210), channel_id=1, source_target_pairs={{0,2},{1,3},{2,0},{3,1},{4,6},{5,7},{6,4},{7,5},{8,10},{9,11},{10,... | collective-permute-start | bytes 3145736 | tf_op jit(solution)/shard_map/ppermute | solution.py:225
  610.7 40.2 %collective-permute-start.104 = (f32[32,8192]{1,0:T(8,128)}, f32[32,8192]{1,0:T(8,128)S(1)}, u32[]{:S(2)}, u32[]{:S(2)}) collective-permute-start(f32[32,8192]{1,0:T(8,128)} %get-tuple-element.218), channel_id=1, source_target_pairs={{0,2},{1,3},{2,0},{3,1},{4,6},{5,7},{6,4},{7,5},{8,10},{9,11},{10,... | collective-permute-start | bytes 3145736 | tf_op jit(solution)/shard_map/ppermute | solution.py:225
  (159 other events, 789.1 us)

commit v3 on v2

--- a/solution.py
+++ b/solution.py
@@ -9,7 +9,7 @@
 
 ROUNDS = 2
 PIECES = 4
-VMEM = 61 * 1024 * 1024
+VMEM = 56 * 1024 * 1024
 NN = (((1,), (0,)), ((), ()))
 NT = (((1,), (1,)), ((), ()))
 
@@ -243,7 +243,7 @@
         out_shape=out,
         in_specs=specs,
         out_specs=tuple(pl.BlockSpec(memory_space=pltpu.VMEM) for _ in out),
-        compiler_params=pltpu.CompilerParams(vmem_limit_bytes=VMEM),
+        compiler_params=pltpu.CompilerParams(vmem_limit_bytes=VMEM // 2),
         cost_estimate=light(),
         name=name,
     )(*args)
@@ -400,11 +400,13 @@
         (keep,) = joined(keep, [aux_swap(x, distance=1) for x in send], 1, after)
         return [keep], [aux_swap(keep, distance=2)]
 
-    def new_vectors(g, c, pair, projection, token):
+    def new_vectors(g, c, projection, token):
         new, square = assemble(
-            *pair, everyone[g][:2], (c, c), projection, stored, gaps, c, True, after=token
+            *sent[g][c], everyone[g][:2], (c, c), projection, stored, gaps, c, True, after=token
         )
-        return new + [aux_swap(x, distance=1) for x in new], square[:h]
+        current[g].append(new + [aux_swap(x, distance=1) for x in new])
+        squares[g] = squares[g] + square[:h]
+        return new[0]
 
     begun, first = project(one)
     projected = [[None, None], [None, None]]
@@ -422,14 +424,16 @@
     begun, second = project(two_sum)
     projected[0][1] = second[:h]
 
-    partial, token = None, [two_sum, sent[0][-1][0][0]]
+    partial, token = None, new_vectors(0, 0, first, [two_sum, sent[0][-1][0][0]])
     for c in range(chunks):
-        x, square = new_vectors(0, c, sent[0][c], first, token)
-        current[0].append(x)
-        squares[0] = squares[0] + square
-        keep, send, partial = over(c, kc, fitted=two_sum, parts=x, before=partial, after=[begun], **wide)
-        sent[1].append(summed(keep, send, [second]))
-        token = [sent[1][-1][0][0]]
+        keep, send, partial = over(
+            c, kc, fitted=two_sum, parts=current[0][c], before=partial, after=[begun, token], **wide
+        )
+        token = partial
+        if c + 1 < chunks:
+            token = new_vectors(0, c + 1, first, [partial])
+        sent[1].append(summed(keep, send, [second, token]))
+        token = sent[1][-1][0][0]
     one = pair_sum(partial, n_pair)
     begun, aux_sum = project(one)
     first = aux_sum[:h]
@@ -440,19 +444,16 @@
         out = joined(keep, near, 2 * split_in, after)
         return out[:split_in], [aux_swap(x, distance=2) for x in out[split_in:]]
 
-    partial, last = None, [[], []]
-    for c in range(chunks):
-        x, square = new_vectors(1, c, sent[1][c], second, token)
-        current[1].append(x)
-        squares[1] = squares[1] + square
-        if c == 0:
-            keep, send, partial = over(c, kc, fitted=one, parts=x, before=partial, after=[begun], **wide)
-            last[0].append(last_sum(keep, send, [aux_sum]))
-            keep, send = over(c + 1, kc, fitted=one, after=[last[0][-1][0][0]])
-            last[0].append(last_sum(keep, send, []))
-            token = [last[0][-1][0][0]]
-        else:
-            (partial,) = over(c, kc, parts=x, before=partial, **wide)
+    last = [[], []]
+    token = new_vectors(1, 0, second, [token])
+    keep, send, partial = over(0, kc, fitted=one, parts=current[1][0], after=[begun, token], **wide)
+    last[0].append(last_sum(keep, send, [aux_sum]))
+    for c in range(1, chunks):
+        keep, send = over(c, kc, fitted=one, after=[last[0][-1][0][0]])
+        last[0].append(last_sum(keep, send, []))
+    for c in range(1, chunks):
+        new_vectors(1, c, second, [last[0][-1][0][0]])
+        (partial,) = over(c, kc, parts=current[1][c], before=partial, **wide)
     ends = [[], []]
     norms = [0.0, 0.0]
 
@@ -482,8 +483,8 @@
     projected[1][1] = second
     token = [begun]
     for c in range(chunks):
-        keep, send = over(c, kc, fitted=two_sum, after=token)
-        last[1].append(last_sum(keep, send, [aux_sum]))
+        keep, send = over(c, kc, fitted=two_sum, after=token, pieces=PIECES * (c + 1))
+        last[1].append(last_sum(keep, send, [aux_sum], 4 if c else 1))
         token = [last[1][-1][0][0]]
     token = []
     for c in range(chunks):

time: 692 us -> 642 us (0.928)
  Pallas kernels: 429 us -> 370 us
  local copies, waits for them, and re-layouts: 33.7 us -> 45 us
    pallas_call x32, Pallas kernels: 63.3 us -> 3.59 us  [small(): pl.pallas_call(body, out_shape=out, in_specs=specs, out_specs=tuple((pl.B...]
    unnamed x194 -> x230, local copies, waits for them, and re-layouts: 28.7 us -> 39.2 us
    ppermute x108 -> x115, waiting for transfers between devices: 125 us -> 119 us  [swap_with(): return lax.ppermute(value, axis, [(i, i ^ distance) for i in range(size)])]
    ppermute x108 -> x115, starting transfers between devices: 87.2 us -> 91.1 us  [swap_with(): return lax.ppermute(value, axis, [(i, i ^ distance) for i in range(size)])]
  transfers between devices with their start and end apart: 108 -> 115, of which waited for: 53 -> 69; matrix products, arithmetic and copies ran while one was open for 0% -> 0% of each run, Pallas kernels for 53% -> 51%
where the time goes in v3:
time: 642 us; the launch traced here: 633 us
  Pallas kernels  370 us (58%)
  waiting for transfers between devices  119 us (19%)
  starting transfers between devices  91.1 us (14%)
  local copies, waits for them, and re-layouts  45 us (7%)
    pallas_call x12, Pallas kernels, pass_over(): pl.pallas_call(kernel, out_shape=tuple(shapes), grid_spec=pltpu.PrefetchS...  268 us
    ppermute x115, waiting for transfers between devices, swap_with(): return lax.ppermute(value, axis, [(i, i ^ distance) for i in range(size)])  119 us
    ppermute x115, starting transfers between devices, swap_with(): return lax.ppermute(value, axis, [(i, i ^ distance) for i in range(size)])  91.1 us
    pallas_call x8, Pallas kernels, assemble(): pl.pallas_call(kernel, out_shape=(*[jax.ShapeDtypeStruct((piece, columns)...  71.3 us
    unnamed x230, local copies, waits for them, and re-layouts  39.2 us
    pallas_call x8, Pallas kernels, joined(): pl.pallas_call(kernel, out_shape=tuple([jax.ShapeDtypeStruct((height, col...  26.7 us
  transfers between devices with their start and end apart: 115, of which 69 were waited for; matrix products, arithmetic and copies ran while one was open for 0% of the time, Pallas kernels for 51%

profile of v3, /device:TPU:0, one launch (start us, length us, event | category | flops | bytes accessed | tf_op | source)
XLA Modules:
  0.0 633.0 jit_solution(612281899571013928)
XLA Ops:
  0.6 4.6 fusion.10
  5.2 3.0 collective-permute-start
  8.2 46.1 %fit.4.refs_1_ = f32[384,1024]{1,0:T(8,128)} custom-call(f32[16384,1024]{1,0:T(8,128)} %refs_0_.7, f32[384,16384]{1,0:T(8,128)} %refs_11_.3), custom_call_target="tpu_custom_call" | custom-call | flops 1 | bytes 1 | tf_op jit(solution)/shard_map/fit/pallas_call | solution.py:136
  62.1 16.7 %fit.5.refs_4_.refs_8_ = f32[128,1152]{1,0:T(8,128)} custom-call(s32[1]{0:T(128)} %bitcast.refs_0_, f32[16384,1024]{1,0:T(8,128)} %refs_0_.7, f32[32,16384]{1,0:T(8,128)} %get-tuple-element.125.refs_2_, f32[32,16384]{1,0:T(8,128)} %collective-permute-done.refs_3_, f32[32,16384]{1,0:T(8,128)} %collective-permute-done.1.refs_4_, ...), custom_call_target="tpu_custom_call" | custom-call | flops 1 | bytes 1 | tf_op jit(solution)/shard_map/fit/pallas_call | solution.py:136
  82.8 17.0 %fit.6.refs_2_.refs_1_ = f32[128,1152]{1,0:T(8,128)} custom-call(s32[1]{0:T(128)} %bitcast.refs_0_, f32[16384,1024]{1,0:T(8,128)} %refs_0_.7, f32[32,16384]{1,0:T(8,128)} %get-tuple-element.125.refs_2_, f32[32,16384]{1,0:T(8,128)} %collective-permute-done.refs_3_, f32[32,16384]{1,0:T(8,128)} %collective-permute-done.1.refs_4_, ...), custom_call_target="tpu_custom_call" | custom-call | flops 1 | bytes 1 | tf_op jit(solution)/shard_map/fit/pallas_call | solution.py:136
  113.2 2.8 collective-permute-start.10
  116.0 6.5 %collective-permute-done.10.refs_1_ = f32[32,1152]{1,0:T(8,128)S(1)} collective-permute-done((f32[32,1152]{1,0:T(8,128)S(1)}, f32[32,1152]{1,0:T(8,128)S(1)}, u32[]{:S(2)}, u32[]{:S(2)}) %collective-permute-start.10) | collective-permute-done | bytes 147488 | tf_op jit(solution)/shard_map/ppermute | solution.py:225
  137.4 3.0 collective-permute-done.16.refs_6_
  141.7 24.4 %spreadfit.5 = (f32[64,8192]{1,0:T(8,128)}, f32[16,8192]{1,0:T(8,128)}, f32[16,8192]{1,0:T(8,128)}, f32[16,8192]{1,0:T(8,128)}, f32[16,8192]{1,0:T(8,128)}, /*index=5*/f32[128,1152]{1,0:T(8,128)}) custom-call(s32[1]{0:T(128)} %bitcast.refs_0_, f32[16384,1024]{1,0:T(8,128)} %refs_0_.7, f32[128,1152]{1,0:T(8,128)} %copy-done.1, ...), custom_call_target="tpu_custom_call" | custom-call | flops 1 | bytes 1 | tf_op jit(solution)/shard_map/spreadfit/pallas_call | solution.py:136
  172.1 3.3 collective-permute-done.25.refs_1_
  177.3 3.3 joined.8.refs_10_.refs_0_
  182.2 24.2 %spreadfit.6 = (f32[64,8192]{1,0:T(8,128)}, f32[16,8192]{1,0:T(8,128)}, f32[16,8192]{1,0:T(8,128)}, f32[16,8192]{1,0:T(8,128)}, f32[16,8192]{1,0:T(8,128)}, /*index=5*/f32[128,1152]{1,0:T(8,128)}) custom-call(s32[1]{0:T(128)} %bitcast.refs_0_, f32[16384,1024]{1,0:T(8,128)} %refs_0_.7, f32[128,1152]{1,0:T(8,128)} %copy-done.1, ...), custom_call_target="tpu_custom_call" | custom-call | flops 1 | bytes 1 | tf_op jit(solution)/shard_map/spreadfit/pallas_call | solution.py:136
  211.6 3.7 joined.9.refs_8_.refs_0_
  228.5 6.3 collective-permute-done.29.refs_1_
  238.4 2.7 collective-permute-done.30.refs_2_
  246.5 9.4 %assemble.8 = (f32[16,8192]{1,0:T(8,128)}, f32[16,8192]{1,0:T(8,128)}, f32[16,8192]{1,0:T(8,128)}, f32[16,8192]{1,0:T(8,128)}, f32[64,128]{1,0:T(8,128)}) custom-call(f32[64,8192]{1,0:T(8,128)} %joined.8.refs_10_.refs_0_, f32[64,8192]{1,0:T(8,128)} %copy-done.42, f32[32,16384]{1,0:T(8,128)} %get-tuple-element.125.refs_2_, ...), custom_call_target="tpu_custom_call" | custom-call | flops 1 | bytes 1 | tf_op jit(solution)/shard_map/assemble/pallas_call | solution.py:205
  261.5 24.2 %spreadfit.7 = (f32[64,8192]{1,0:T(8,128)}, f32[16,8192]{1,0:T(8,128)}, f32[16,8192]{1,0:T(8,128)}, f32[16,8192]{1,0:T(8,128)}, f32[16,8192]{1,0:T(8,128)}, /*index=5*/f32[128,1152]{1,0:T(8,128)}) custom-call(s32[1]{0:T(128)} %bitcast.refs_0_, f32[16384,1024]{1,0:T(8,128)} %refs_0_.7, f32[128,1152]{1,0:T(8,128)} %copy-done, ...), custom_call_target="tpu_custom_call" | custom-call | flops 1 | bytes 1 | tf_op jit(solution)/shard_map/spreadfit/pallas_call | solution.py:136
  288.8 9.4 %assemble.9 = (f32[16,8192]{1,0:T(8,128)}, f32[16,8192]{1,0:T(8,128)}, f32[16,8192]{1,0:T(8,128)}, f32[16,8192]{1,0:T(8,128)}, f32[64,128]{1,0:T(8,128)}) custom-call(f32[64,8192]{1,0:T(8,128)} %joined.9.refs_8_.refs_0_, f32[64,8192]{1,0:T(8,128)} %copy-done.40, f32[32,16384]{1,0:T(8,128)} %get-tuple-element.125.refs_2_, ...), custom_call_target="tpu_custom_call" | custom-call | flops 1 | bytes 1 | tf_op jit(solution)/shard_map/assemble/pallas_call | solution.py:205
  299.5 3.4 joined.10.refs_15_.refs_0_
  309.2 24.6 %spreadfit.8 = (f32[64,8192]{1,0:T(8,128)}, f32[16,8192]{1,0:T(8,128)}, f32[16,8192]{1,0:T(8,128)}, f32[16,8192]{1,0:T(8,128)}, f32[16,8192]{1,0:T(8,128)}, /*index=5*/f32[128,1152]{1,0:T(8,128)}) custom-call(s32[1]{0:T(128)} %bitcast.refs_0_, f32[16384,1024]{1,0:T(8,128)} %refs_0_.7, f32[128,1152]{1,0:T(8,128)} %copy-done, ...), custom_call_target="tpu_custom_call" | custom-call | flops 1 | bytes 1 | tf_op jit(solution)/shard_map/spreadfit/pallas_call | solution.py:136
  340.4 3.3 joined.11.refs_7_.refs_0_
  349.0 6.3 collective-permute-done.56.refs_1_
  358.8 3.2 collective-permute-done.57.refs_2_
  366.5 9.4 %assemble.10 = (f32[16,8192]{1,0:T(8,128)}, f32[16,8192]{1,0:T(8,128)}, f32[16,8192]{1,0:T(8,128)}, f32[16,8192]{1,0:T(8,128)}, f32[64,128]{1,0:T(8,128)}) custom-call(f32[64,8192]{1,0:T(8,128)} %joined.10.refs_15_.refs_0_, f32[64,8192]{1,0:T(8,128)} %copy-done.41, f32[32,16384]{1,0:T(8,128)} %get-tuple-element.135.refs_3_.refs_2_, ...), custom_call_target="tpu_custom_call" | custom-call | flops 1 | bytes 1 | tf_op jit(solution)/shard_map/assemble/pallas_call | solution.py:205
  381.3 24.4 %spreadfit.9 = (f32[64,8192]{1,0:T(8,128)}, f32[16,8192]{1,0:T(8,128)}, f32[16,8192]{1,0:T(8,128)}, f32[16,8192]{1,0:T(8,128)}, f32[16,8192]{1,0:T(8,128)}, /*index=5*/f32[128,1152]{1,0:T(8,128)}) custom-call(s32[1]{0:T(128)} %bitcast.refs_0_, f32[16384,1024]{1,0:T(8,128)} %refs_0_.7, f32[128,1152]{1,0:T(8,128)} %copy-done.3, ...), custom_call_target="tpu_custom_call" | custom-call | flops 1 | bytes 1 | tf_op jit(solution)/shard_map/spreadfit/pallas_call | solution.py:136
  410.9 3.3 joined.12
  414.2 16.5 %spread.3 = (f32[64,8192]{1,0:T(8,128)}, f32[16,8192]{1,0:T(8,128)}, f32[16,8192]{1,0:T(8,128)}, f32[16,8192]{1,0:T(8,128)}, f32[16,8192]{1,0:T(8,128)}) custom-call(f32[16384,1024]{1,0:T(8,128)} %refs_0_.7, f32[128,1152]{1,0:T(8,128)} %copy-done.3, f32[32,8192]{1,0:T(8,128)} %get-tuple-element.192.refs_2_.refs_0_), custom_call_target="tpu_custom_call" | custom-call | flops 1 | bytes 1 | tf_op jit(solution)/shard_map/spread/pallas_call | solution.py:136
  435.9 3.3 joined.13
  440.5 9.5 %assemble.11 = (f32[16,8192]{1,0:T(8,128)}, f32[16,8192]{1,0:T(8,128)}, f32[16,8192]{1,0:T(8,128)}, f32[16,8192]{1,0:T(8,128)}, f32[64,128]{1,0:T(8,128)}) custom-call(f32[64,8192]{1,0:T(8,128)} %joined.11.refs_7_.refs_0_, f32[64,8192]{1,0:T(8,128)} %copy-done.39, f32[32,16384]{1,0:T(8,128)} %get-tuple-element.135.refs_3_.refs_2_, ...), custom_call_target="tpu_custom_call" | custom-call | flops 1 | bytes 1 | tf_op jit(solution)/shard_map/assemble/pallas_call | solution.py:205
  456.9 17.1 %fit.7.refs_1_ = f32[128,1152]{1,0:T(8,128)} custom-call(s32[1]{0:T(128)} %bitcast.refs_0_, f32[16384,1024]{1,0:T(8,128)} %refs_0_.7, f32[16,8192]{1,0:T(8,128)} %get-tuple-element.200.refs_2_.refs_8_, f32[16,8192]{1,0:T(8,128)} %get-tuple-element.201.refs_3_.refs_9_, f32[16,8192]{1,0:T(8,128)} %get-tuple-element.202.refs_4_, ...), custom_call_target="tpu_custom_call" | custom-call | flops 1 | bytes 1 | tf_op jit(solution)/shard_map/fit/pallas_call | solution.py:136
  480.9 8.2 %assemble.12 = (f32[32,8192]{1,0:T(8,128)}, f32[32,128]{1,0:T(8,128)}) custom-call(f32[32,8192]{1,0:T(8,128)} %get-tuple-element.192.refs_2_.refs_0_, f32[32,8192]{1,0:T(8,128)} %copy-done.45, f32[16,8192]{1,0:T(8,128)} %get-tuple-element.155.refs_3_.refs_14_.refs_2_, f32[16,8192]{1,0:T(8,128)} %get-tuple-element.156.refs_4_.refs_3_, ...), custom_call_target="tpu_custom_call" | custom-call | flops 1 | bytes 1 | tf_op jit(solution)/shard_map/assemble/pallas_call | solution.py:205
  490.4 3.1 collective-permute-start.89
  493.4 4.8 collective-permute-done.85.refs_1_
  499.2 8.2 %assemble.13 = (f32[32,8192]{1,0:T(8,128)}, f32[32,128]{1,0:T(8,128)}) custom-call(f32[32,8192]{1,0:T(8,128)} %get-tuple-element.199.refs_7_.refs_0_, f32[32,8192]{1,0:T(8,128)} %copy-done.44, f32[16,8192]{1,0:T(8,128)} %get-tuple-element.161.refs_5_.refs_3_.refs_2_, f32[16,8192]{1,0:T(8,128)} %get-tuple-element.162.refs_4_.refs_3_, ...), custom_call_target="tpu_custom_call" | custom-call | flops 1 | bytes 1 | tf_op jit(solution)/shard_map/assemble/pallas_call | solution.py:205
  520.3 16.7 %spread.4 = (f32[64,8192]{1,0:T(8,128)}, f32[16,8192]{1,0:T(8,128)}, f32[16,8192]{1,0:T(8,128)}, f32[16,8192]{1,0:T(8,128)}, f32[16,8192]{1,0:T(8,128)}) custom-call(f32[16384,1024]{1,0:T(8,128)} %refs_0_.7, f32[128,1152]{1,0:T(8,128)} %copy-done.4, f32[64,384]{1,0:T(8,128)} %copy-done.33), custom_call_target="tpu_custom_call" | custom-call | flops 1 | bytes 1 | tf_op jit(solution)/shard_map/spread/pallas_call | solution.py:136
  540.9 4.0 collective-permute-done.98.refs_1_
  547.0 3.3 joined.14
  551.1 16.5 %spread.5 = (f32[64,8192]{1,0:T(8,128)}, f32[8,8192]{1,0:T(8,128)}, f32[8,8192]{1,0:T(8,128)}, f32[8,8192]{1,0:T(8,128)}, f32[8,8192]{1,0:T(8,128)}, /*index=5*/...) custom-call(f32[16384,1024]{1,0:T(8,128)} %refs_0_.7, f32[128,1152]{1,0:T(8,128)} %copy-done.4, ...), custom_call_target="tpu_custom_call" | custom-call | flops 1 | bytes 1 | tf_op jit(solution)/shard_map/spread/pallas_call | solution.py:136
  573.0 3.3 joined.15
  582.1 8.2 %assemble.14 = (f32[32,8192]{1,0:T(8,128)}, f32[32,128]{1,0:T(8,128)}) custom-call(f32[32,8192]{1,0:T(8,128)} %get-tuple-element.219.refs_0_.refs_2_, f32[32,8192]{1,0:T(8,128)} %copy-done.46, f32[16,8192]{1,0:T(8,128)} %get-tuple-element.181.refs_3_.refs_14_.refs_2_, f32[16,8192]{1,0:T(8,128)} %get-tuple-element.182.refs_4_.refs_3_, ...), custom_call_target="tpu_custom_call" | custom-call | flops 1 | bytes 1 | tf_op jit(solution)/shard_map/assemble/pallas_call | solution.py:205
  591.3 5.6 collective-permute-done.110.refs_6_
  597.0 4.8 collective-permute-done.111.refs_7_
  602.5 9.1 %assemble.15 = (f32[32,8192]{1,0:T(8,128)}, f32[32,128]{1,0:T(8,128)}) custom-call(f32[8,8192]{1,0:T(8,128)} %get-tuple-element.231.refs_0_, f32[8,8192]{1,0:T(8,128)} %get-tuple-element.232.refs_1_, f32[8,8192]{1,0:T(8,128)} %get-tuple-element.233.refs_2_, f32[8,8192]{1,0:T(8,128)} %get-tuple-element.234.refs_3_, f32[8,8192]{1,0:T(8,128)} %copy-done.94, ...), custom_call_target="tpu_custom_call" | custom-call | flops 1 | bytes 1 | tf_op jit(solution)/shard_map/assemble/pallas_call | solution.py:205
  614.0 2.8 collective-permute-done.112
  618.2 2.9 collective-permute-done.113
  621.1 3.9 collective-permute-start.114
  625.0 2.9 collective-permute-done.114
  628.9 3.6 maximum_divide_fusion
  (492 shorter events, 184.7 us)
Async XLA Ops:
  5.2 49.1 %collective-permute-start = (f32[32,16384]{1,0:T(8,128)}, f32[32,16384]{1,0:T(8,128)}, u32[]{:S(2)}, u32[]{:S(2)}) collective-permute-start(f32[32,16384]{1,0:T(8,128)} %get-tuple-element.125.refs_2_), channel_id=1, source_target_pairs={{0,2},{1,3},{2,0},{3,1},{4,6},{5,7},{6,4},{7,5},{8,10},{9,11},{10,... | collective-permute-start | bytes 6291464 | tf_op jit(solution)/shard_map/ppermute | solution.py:225
  54.3 7.8 %collective-permute-start.2 = (f32[32,16384]{1,0:T(8,128)}, f32[32,16384]{1,0:T(8,128)}, u32[]{:S(2)}, u32[]{:S(2)}) collective-permute-start(f32[32,16384]{1,0:T(8,128)} %collective-permute-done.refs_3_), channel_id=1, source_target_pairs={{0,1},{1,0},{2,3},{3,2},{4,5},{5,4},{6,7},{7,6},{8,9},{9,8},{10,11... | collective-permute-start | bytes 6291464 | tf_op jit(solution)/shard_map/ppermute | solution.py:225
  54.8 78.2 %collective-permute-start.14 = (f32[32,16384]{1,0:T(8,128)}, f32[32,16384]{1,0:T(8,128)}, u32[]{:S(2)}, u32[]{:S(2)}) collective-permute-start(f32[32,16384]{1,0:T(8,128)} %get-tuple-element.135.refs_3_.refs_2_), channel_id=1, source_target_pairs={{0,2},{1,3},{2,0},{3,1},{4,6},{5,7},{6,4},{7,5},{8,10},{9,11},{10,... | collective-permute-start | bytes 6291464 | tf_op jit(solution)/shard_map/ppermute | solution.py:225
  58.6 20.2 %collective-permute-start.3 = (f32[96,1024]{1,0:T(8,128)S(1)}, f32[96,1024]{1,0:T(8,128)S(1)}, u32[]{:S(2)}, u32[]{:S(2)}) collective-permute-start(f32[96,1024]{1,0:T(8,128)S(1)} %get-tuple-element.128), channel_id=1, source_target_pairs={{0,4},{4,0},{8,12},{12,8},{16,20},{20,16},{24,28},{28,24},{1,5},{5... | collective-permute-start | bytes 1179656 | tf_op jit(solution)/shard_map/ppermute | solution.py:225
  60.1 18.7 %collective-permute-start.4 = (f32[96,1024]{1,0:T(8,128)S(1)}, f32[96,1024]{1,0:T(8,128)S(1)}, u32[]{:S(2)}, u32[]{:S(2)}) collective-permute-start(f32[96,1024]{1,0:T(8,128)S(1)} %get-tuple-element.129), channel_id=1, source_target_pairs={{0,8},{4,12},{8,0},{12,4},{16,24},{20,28},{24,16},{28,20},{1,9},{5... | collective-permute-start | bytes 1179656 | tf_op jit(solution)/shard_map/ppermute | solution.py:225
  61.7 17.3 %collective-permute-start.5 = (f32[96,1024]{1,0:T(8,128)S(1)}, f32[96,1024]{1,0:T(8,128)S(1)}, u32[]{:S(2)}, u32[]{:S(2)}) collective-permute-start(f32[96,1024]{1,0:T(8,128)S(1)} %get-tuple-element.130), channel_id=1, source_target_pairs={{0,12},{4,8},{8,4},{12,0},{16,28},{20,24},{24,20},{28,16},{1,13},{... | collective-permute-start | bytes 1179656 | tf_op jit(solution)/shard_map/ppermute | solution.py:225
  80.1 20.1 %collective-permute-start.6 = (f32[96,1024]{1,0:T(8,128)S(1)}, f32[96,1024]{1,0:T(8,128)S(1)}, u32[]{:S(2)}, u32[]{:S(2)}) collective-permute-start(f32[96,1024]{1,0:T(8,128)S(1)} %total.14.refs_9_.refs_0_), channel_id=1, source_target_pairs={{0,16},{4,20},{8,24},{12,28},{16,0},{20,4},{24,8},{28,12},{1,17},{... | collective-permute-start | bytes 1179656 | tf_op jit(solution)/shard_map/ppermute | solution.py:225
  113.2 9.2 %collective-permute-start.10 = (f32[32,1152]{1,0:T(8,128)S(1)}, f32[32,1152]{1,0:T(8,128)S(1)}, u32[]{:S(2)}, u32[]{:S(2)}) collective-permute-start(f32[32,1152]{1,0:T(8,128)S(1)} %total.16.refs_0_), channel_id=1, source_target_pairs={{0,16},{4,20},{8,24},{12,28},{16,0},{20,4},{24,8},{28,12},{1,17},{... | collective-permute-start | bytes 442376 | tf_op jit(solution)/shard_map/ppermute | solution.py:225
  133.5 33.1 %collective-permute-start.21 = (f32[96,1024]{1,0:T(8,128)S(1)}, f32[96,1024]{1,0:T(8,128)S(1)}, u32[]{:S(2)}, u32[]{:S(2)}) collective-permute-start(f32[96,1024]{1,0:T(8,128)S(1)} %total.15.refs_2_.refs_1_), channel_id=1, source_target_pairs={{0,4},{4,0},{8,12},{12,8},{16,20},{20,16},{24,28},{28,24},{1,5},{5... | collective-permute-start | bytes 1179656 | tf_op jit(solution)/shard_map/ppermute | solution.py:225
  134.5 32.3 %collective-permute-start.22 = (f32[96,1024]{1,0:T(8,128)S(1)}, f32[96,1024]{1,0:T(8,128)S(1)}, u32[]{:S(2)}, u32[]{:S(2)}) collective-permute-start(f32[96,1024]{1,0:T(8,128)S(1)} %total.15.refs_2_.refs_1_), channel_id=1, source_target_pairs={{0,8},{4,12},{8,0},{12,4},{16,24},{20,28},{24,16},{28,20},{1,9},{5... | collective-permute-start | bytes 1179656 | tf_op jit(solution)/shard_map/ppermute | solution.py:225
  135.9 31.2 %collective-permute-start.23 = (f32[96,1024]{1,0:T(8,128)S(1)}, f32[96,1024]{1,0:T(8,128)S(1)}, u32[]{:S(2)}, u32[]{:S(2)}) collective-permute-start(f32[96,1024]{1,0:T(8,128)S(1)} %total.15.refs_2_.refs_1_), channel_id=1, source_target_pairs={{0,12},{4,8},{8,4},{12,0},{16,28},{20,24},{24,20},{28,16},{1,13},{... | collective-permute-start | bytes 1179656 | tf_op jit(solution)/shard_map/ppermute | solution.py:225
  166.0 9.9 %collective-permute-start.17 = (f32[16,8192]{1,0:T(8,128)}, f32[16,8192]{1,0:T(8,128)S(1)}, u32[]{:S(2)}, u32[]{:S(2)}) collective-permute-start(f32[16,8192]{1,0:T(8,128)} %get-tuple-element.139), channel_id=1, source_target_pairs={{0,1},{1,0},{2,3},{3,2},{4,5},{5,4},{6,7},{7,6},{8,9},{9,8},{10,11... | collective-permute-start | bytes 1572872 | tf_op jit(solution)/shard_map/ppermute | solution.py:225
  166.2 9.8 %collective-permute-start.18 = (f32[16,8192]{1,0:T(8,128)}, f32[16,8192]{1,0:T(8,128)S(1)}, u32[]{:S(2)}, u32[]{:S(2)}) collective-permute-start(f32[16,8192]{1,0:T(8,128)} %get-tuple-element.140), channel_id=1, source_target_pairs={{0,1},{1,0},{2,3},{3,2},{4,5},{5,4},{6,7},{7,6},{8,9},{9,8},{10,11... | collective-permute-start | bytes 1572872 | tf_op jit(solution)/shard_map/ppermute | solution.py:225
  166.6 9.4 %collective-permute-start.19 = (f32[16,8192]{1,0:T(8,128)}, f32[16,8192]{1,0:T(8,128)S(1)}, u32[]{:S(2)}, u32[]{:S(2)}) collective-permute-start(f32[16,8192]{1,0:T(8,128)} %get-tuple-element.141), channel_id=1, source_target_pairs={{0,1},{1,0},{2,3},{3,2},{4,5},{5,4},{6,7},{7,6},{8,9},{9,8},{10,11... | collective-permute-start | bytes 1572872 | tf_op jit(solution)/shard_map/ppermute | solution.py:225
  166.8 9.3 %collective-permute-start.20 = (f32[16,8192]{1,0:T(8,128)}, f32[16,8192]{1,0:T(8,128)S(1)}, u32[]{:S(2)}, u32[]{:S(2)}) collective-permute-start(f32[16,8192]{1,0:T(8,128)} %get-tuple-element.142), channel_id=1, source_target_pairs={{0,1},{1,0},{2,3},{3,2},{4,5},{5,4},{6,7},{7,6},{8,9},{9,8},{10,11... | collective-permute-start | bytes 1572872 | tf_op jit(solution)/shard_map/ppermute | solution.py:225
  180.6 64.5 %collective-permute-start.38 = (f32[64,8192]{1,0:T(8,128)}, f32[64,8192]{1,0:T(8,128)S(1)}, u32[]{:S(2)}, u32[]{:S(2)}) collective-permute-start(f32[64,8192]{1,0:T(8,128)} %joined.8.refs_10_.refs_0_), channel_id=1, source_target_pairs={{0,2},{1,3},{2,0},{3,1},{4,6},{5,7},{6,4},{7,5},{8,10},{9,11},{10,... | collective-permute-start | bytes 6291464 | tf_op jit(solution)/shard_map/ppermute | solution.py:225
  215.3 72.1 %collective-permute-start.37 = (f32[64,8192]{1,0:T(8,128)}, f32[64,8192]{1,0:T(8,128)S(1)}, u32[]{:S(2)}, u32[]{:S(2)}) collective-permute-start(f32[64,8192]{1,0:T(8,128)} %joined.9.refs_8_.refs_0_), channel_id=1, source_target_pairs={{0,2},{1,3},{2,0},{3,1},{4,6},{5,7},{6,4},{7,5},{8,10},{9,11},{10,... | collective-permute-start | bytes 6291464 | tf_op jit(solution)/shard_map/ppermute | solution.py:225
  225.9 8.9 %collective-permute-start.29 = (f32[32,1152]{1,0:T(8,128)S(1)}, f32[32,1152]{1,0:T(8,128)S(1)}, u32[]{:S(2)}, u32[]{:S(2)}) collective-permute-start(f32[32,1152]{1,0:T(8,128)S(1)} %total.19.refs_0_), channel_id=1, source_target_pairs={{0,16},{4,20},{8,24},{12,28},{16,0},{20,4},{24,8},{28,12},{1,17},{... | collective-permute-start | bytes 442376 | tf_op jit(solution)/shard_map/ppermute | solution.py:225
  236.7 7.6 %collective-permute-start.32 = (f32[32,1152]{1,0:T(8,128)S(1)}, f32[32,1152]{1,0:T(8,128)S(1)}, u32[]{:S(2)}, u32[]{:S(2)}) collective-permute-start(f32[32,1152]{1,0:T(8,128)S(1)} %total.20.refs_1_), channel_id=1, source_target_pairs={{0,12},{4,8},{8,4},{12,0},{16,28},{20,24},{24,20},{28,16},{1,13},{... | collective-permute-start | bytes 442376 | tf_op jit(solution)/shard_map/ppermute | solution.py:225
  245.0 11.8 %collective-permute-start.51 = (f32[64,384]{1,0:T(8,128)S(1)}, f32[64,384]{1,0:T(8,128)S(1)}, u32[]{:S(2)}, u32[]{:S(2)}) collective-permute-start(f32[64,384]{1,0:T(8,128)S(1)} %get-tuple-element.170), channel_id=1, source_target_pairs={{0,1},{1,0},{2,3},{3,2},{4,5},{5,4},{6,7},{7,6},{8,9},{9,8},{10,11... | collective-permute-start | bytes 294920 | tf_op jit(solution)/shard_map/ppermute | solution.py:225
  258.1 28.3 %collective-permute-start.52 = (f32[64,384]{1,0:T(8,128)S(1)}, f32[64,384]{1,0:T(8,128)S(1)}, u32[]{:S(2)}, u32[]{:S(2)}) collective-permute-start(f32[64,384]{1,0:T(8,128)S(1)} %total.21.refs_0_), channel_id=1, source_target_pairs={{0,2},{1,3},{2,0},{3,1},{4,6},{5,7},{6,4},{7,5},{8,10},{9,11},{10,... | collective-permute-start | bytes 294920 | tf_op jit(solution)/shard_map/ppermute | solution.py:225
  285.7 12.4 %collective-permute-start.47 = (f32[16,8192]{1,0:T(8,128)}, f32[16,8192]{1,0:T(8,128)S(1)}, u32[]{:S(2)}, u32[]{:S(2)}) collective-permute-start(f32[16,8192]{1,0:T(8,128)} %get-tuple-element.166), channel_id=1, source_target_pairs={{0,1},{1,0},{2,3},{3,2},{4,5},{5,4},{6,7},{7,6},{8,9},{9,8},{10,11... | collective-permute-start | bytes 1572872 | tf_op jit(solution)/shard_map/ppermute | solution.py:225
  285.9 12.3 %collective-permute-start.48 = (f32[16,8192]{1,0:T(8,128)}, f32[16,8192]{1,0:T(8,128)S(1)}, u32[]{:S(2)}, u32[]{:S(2)}) collective-permute-start(f32[16,8192]{1,0:T(8,128)} %get-tuple-element.167), channel_id=1, source_target_pairs={{0,1},{1,0},{2,3},{3,2},{4,5},{5,4},{6,7},{7,6},{8,9},{9,8},{10,11... | collective-permute-start | bytes 1572872 | tf_op jit(solution)/shard_map/ppermute | solution.py:225
  286.3 11.9 %collective-permute-start.49 = (f32[16,8192]{1,0:T(8,128)}, f32[16,8192]{1,0:T(8,128)S(1)}, u32[]{:S(2)}, u32[]{:S(2)}) collective-permute-start(f32[16,8192]{1,0:T(8,128)} %get-tuple-element.168), channel_id=1, source_target_pairs={{0,1},{1,0},{2,3},{3,2},{4,5},{5,4},{6,7},{7,6},{8,9},{9,8},{10,11... | collective-permute-start | bytes 1572872 | tf_op jit(solution)/shard_map/ppermute | solution.py:225
  286.4 11.8 %collective-permute-start.50 = (f32[16,8192]{1,0:T(8,128)}, f32[16,8192]{1,0:T(8,128)S(1)}, u32[]{:S(2)}, u32[]{:S(2)}) collective-permute-start(f32[16,8192]{1,0:T(8,128)} %get-tuple-element.169), channel_id=1, source_target_pairs={{0,1},{1,0},{2,3},{3,2},{4,5},{5,4},{6,7},{7,6},{8,9},{9,8},{10,11... | collective-permute-start | bytes 1572872 | tf_op jit(solution)/shard_map/ppermute | solution.py:225
  302.9 62.2 %collective-permute-start.60 = (f32[64,8192]{1,0:T(8,128)}, f32[64,8192]{1,0:T(8,128)S(1)}, u32[]{:S(2)}, u32[]{:S(2)}) collective-permute-start(f32[64,8192]{1,0:T(8,128)} %joined.10.refs_15_.refs_0_), channel_id=1, source_target_pairs={{0,2},{1,3},{2,0},{3,1},{4,6},{5,7},{6,4},{7,5},{8,10},{9,11},{10,... | collective-permute-start | bytes 6291464 | tf_op jit(solution)/shard_map/ppermute | solution.py:225
  336.0 8.3 %collective-permute-start.53 = (f32[32,1152]{1,0:T(8,128)S(1)}, f32[32,1152]{1,0:T(8,128)S(1)}, u32[]{:S(2)}, u32[]{:S(2)}) collective-permute-start(f32[32,1152]{1,0:T(8,128)S(1)} %get-tuple-element.173), channel_id=1, source_target_pairs={{0,4},{4,0},{8,12},{12,8},{16,20},{20,16},{24,28},{28,24},{1,5},{5... | collective-permute-start | bytes 442376 | tf_op jit(solution)/shard_map/ppermute | solution.py:225
  336.8 7.6 %collective-permute-start.54 = (f32[32,1152]{1,0:T(8,128)S(1)}, f32[32,1152]{1,0:T(8,128)S(1)}, u32[]{:S(2)}, u32[]{:S(2)}) collective-permute-start(f32[32,1152]{1,0:T(8,128)S(1)} %get-tuple-element.174), channel_id=1, source_target_pairs={{0,8},{4,12},{8,0},{12,4},{16,24},{20,28},{24,16},{28,20},{1,9},{5... | collective-permute-start | bytes 442376 | tf_op jit(solution)/shard_map/ppermute | solution.py:225
  337.9 8.5 %collective-permute-start.55 = (f32[32,1152]{1,0:T(8,128)S(1)}, f32[32,1152]{1,0:T(8,128)S(1)}, u32[]{:S(2)}, u32[]{:S(2)}) collective-permute-start(f32[32,1152]{1,0:T(8,128)S(1)} %get-tuple-element.175), channel_id=1, source_target_pairs={{0,12},{4,8},{8,4},{12,0},{16,28},{20,24},{24,20},{28,16},{1,13},{... | collective-permute-start | bytes 442376 | tf_op jit(solution)/shard_map/ppermute | solution.py:225
  343.7 95.5 %collective-permute-start.76 = (f32[64,8192]{1,0:T(8,128)}, f32[64,8192]{1,0:T(8,128)S(1)}, u32[]{:S(2)}, u32[]{:S(2)}) collective-permute-start(f32[64,8192]{1,0:T(8,128)} %joined.11.refs_7_.refs_0_), channel_id=1, source_target_pairs={{0,2},{1,3},{2,0},{3,1},{4,6},{5,7},{6,4},{7,5},{8,10},{9,11},{10,... | collective-permute-start | bytes 6291464 | tf_op jit(solution)/shard_map/ppermute | solution.py:225
  346.4 8.9 %collective-permute-start.56 = (f32[32,1152]{1,0:T(8,128)S(1)}, f32[32,1152]{1,0:T(8,128)S(1)}, u32[]{:S(2)}, u32[]{:S(2)}) collective-permute-start(f32[32,1152]{1,0:T(8,128)S(1)} %total.22.refs_0_), channel_id=1, source_target_pairs={{0,16},{4,20},{8,24},{12,28},{16,0},{20,4},{24,8},{28,12},{1,17},{... | collective-permute-start | bytes 442376 | tf_op jit(solution)/shard_map/ppermute | solution.py:225
  365.1 11.9 %collective-permute-start.73 = (f32[64,384]{1,0:T(8,128)S(1)}, f32[64,384]{1,0:T(8,128)S(1)}, u32[]{:S(2)}, u32[]{:S(2)}) collective-permute-start(f32[64,384]{1,0:T(8,128)S(1)} %get-tuple-element.191), channel_id=1, source_target_pairs={{0,1},{1,0},{2,3},{3,2},{4,5},{5,4},{6,7},{7,6},{8,9},{9,8},{10,11... | collective-permute-start | bytes 294920 | tf_op jit(solution)/shard_map/ppermute | solution.py:225
  378.1 28.5 %collective-permute-start.74 = (f32[64,384]{1,0:T(8,128)S(1)}, f32[64,384]{1,0:T(8,128)S(1)}, u32[]{:S(2)}, u32[]{:S(2)}) collective-permute-start(f32[64,384]{1,0:T(8,128)S(1)} %total.24.refs_0_), channel_id=1, source_target_pairs={{0,2},{1,3},{2,0},{3,1},{4,6},{5,7},{6,4},{7,5},{8,10},{9,11},{10,... | collective-permute-start | bytes 294920 | tf_op jit(solution)/shard_map/ppermute | solution.py:225
  450.5 29.4 %collective-permute-start.75 = (f32[32,8192]{1,0:T(8,128)S(1)}, f32[32,8192]{1,0:T(8,128)S(1)}, u32[]{:S(2)}, u32[]{:S(2)}) collective-permute-start(f32[32,8192]{1,0:T(8,128)S(1)} %copy-done.113), channel_id=1, source_target_pairs={{0,2},{1,3},{2,0},{3,1},{4,6},{5,7},{6,4},{7,5},{8,10},{9,11},{10,... | collective-permute-start | bytes 3145736 | tf_op jit(solution)/shard_map/ppermute | solution.py:225
  451.2 47.0 %collective-permute-start.85 = (f32[32,8192]{1,0:T(8,128)S(1)}, f32[32,8192]{1,0:T(8,128)S(1)}, u32[]{:S(2)}, u32[]{:S(2)}) collective-permute-start(f32[32,8192]{1,0:T(8,128)S(1)} %copy-done.114), channel_id=1, source_target_pairs={{0,2},{1,3},{2,0},{3,1},{4,6},{5,7},{6,4},{7,5},{8,10},{9,11},{10,... | collective-permute-start | bytes 3145736 | tf_op jit(solution)/shard_map/ppermute | solution.py:225
  475.8 13.3 %collective-permute-start.86 = (f32[32,1152]{1,0:T(8,128)S(1)}, f32[32,1152]{1,0:T(8,128)S(1)}, u32[]{:S(2)}, u32[]{:S(2)}) collective-permute-start(f32[32,1152]{1,0:T(8,128)S(1)} %get-tuple-element.208), channel_id=1, source_target_pairs={{0,4},{4,0},{8,12},{12,8},{16,20},{20,16},{24,28},{28,24},{1,5},{5... | collective-permute-start | bytes 442376 | tf_op jit(solution)/shard_map/ppermute | solution.py:225
  477.3 11.8 %collective-permute-start.87 = (f32[32,1152]{1,0:T(8,128)S(1)}, f32[32,1152]{1,0:T(8,128)S(1)}, u32[]{:S(2)}, u32[]{:S(2)}) collective-permute-start(f32[32,1152]{1,0:T(8,128)S(1)} %get-tuple-element.209), channel_id=1, source_target_pairs={{0,8},{4,12},{8,0},{12,4},{16,24},{20,28},{24,16},{28,20},{1,9},{5... | collective-permute-start | bytes 442376 | tf_op jit(solution)/shard_map/ppermute | solution.py:225
  478.2 10.9 %collective-permute-start.88 = (f32[32,1152]{1,0:T(8,128)S(1)}, f32[32,1152]{1,0:T(8,128)S(1)}, u32[]{:S(2)}, u32[]{:S(2)}) collective-permute-start(f32[32,1152]{1,0:T(8,128)S(1)} %get-tuple-element.210), channel_id=1, source_target_pairs={{0,12},{4,8},{8,4},{12,0},{16,28},{20,24},{24,20},{28,16},{1,13},{... | collective-permute-start | bytes 442376 | tf_op jit(solution)/shard_map/ppermute | solution.py:225
  490.4 17.0 %collective-permute-start.89 = (f32[32,1152]{1,0:T(8,128)S(1)}, f32[32,1152]{1,0:T(8,128)S(1)}, u32[]{:S(2)}, u32[]{:S(2)}) collective-permute-start(f32[32,1152]{1,0:T(8,128)S(1)} %total.25.refs_7_.refs_0_), channel_id=1, source_target_pairs={{0,16},{4,20},{8,24},{12,28},{16,0},{20,4},{24,8},{28,12},{1,17},{... | collective-permute-start | bytes 442376 | tf_op jit(solution)/shard_map/ppermute | solution.py:225
  537.1 8.5 %collective-permute-start.93 = (f32[16,8192]{1,0:T(8,128)}, f32[16,8192]{1,0:T(8,128)S(1)}, u32[]{:S(2)}, u32[]{:S(2)}) collective-permute-start(f32[16,8192]{1,0:T(8,128)} %get-tuple-element.214), channel_id=1, source_target_pairs={{0,1},{1,0},{2,3},{3,2},{4,5},{5,4},{6,7},{7,6},{8,9},{9,8},{10,11... | collective-permute-start | bytes 1572872 | tf_op jit(solution)/shard_map/ppermute | solution.py:225
  537.1 8.5 %collective-permute-start.94 = (f32[16,8192]{1,0:T(8,128)}, f32[16,8192]{1,0:T(8,128)S(1)}, u32[]{:S(2)}, u32[]{:S(2)}) collective-permute-start(f32[16,8192]{1,0:T(8,128)} %get-tuple-element.215), channel_id=1, source_target_pairs={{0,1},{1,0},{2,3},{3,2},{4,5},{5,4},{6,7},{7,6},{8,9},{9,8},{10,11... | collective-permute-start | bytes 1572872 | tf_op jit(solution)/shard_map/ppermute | solution.py:225
  537.6 8.0 %collective-permute-start.95 = (f32[16,8192]{1,0:T(8,128)}, f32[16,8192]{1,0:T(8,128)S(1)}, u32[]{:S(2)}, u32[]{:S(2)}) collective-permute-start(f32[16,8192]{1,0:T(8,128)} %get-tuple-element.216), channel_id=1, source_target_pairs={{0,1},{1,0},{2,3},{3,2},{4,5},{5,4},{6,7},{7,6},{8,9},{9,8},{10,11... | collective-permute-start | bytes 1572872 | tf_op jit(solution)/shard_map/ppermute | solution.py:225
  537.6 8.0 %collective-permute-start.96 = (f32[16,8192]{1,0:T(8,128)}, f32[16,8192]{1,0:T(8,128)S(1)}, u32[]{:S(2)}, u32[]{:S(2)}) collective-permute-start(f32[16,8192]{1,0:T(8,128)} %get-tuple-element.217), channel_id=1, source_target_pairs={{0,1},{1,0},{2,3},{3,2},{4,5},{5,4},{6,7},{7,6},{8,9},{9,8},{10,11... | collective-permute-start | bytes 1572872 | tf_op jit(solution)/shard_map/ppermute | solution.py:225
  550.2 30.9 %collective-permute-start.99 = (f32[32,8192]{1,0:T(8,128)}, f32[32,8192]{1,0:T(8,128)S(1)}, u32[]{:S(2)}, u32[]{:S(2)}) collective-permute-start(f32[32,8192]{1,0:T(8,128)} %get-tuple-element.220), channel_id=1, source_target_pairs={{0,2},{1,3},{2,0},{3,1},{4,6},{5,7},{6,4},{7,5},{8,10},{9,11},{10,... | collective-permute-start | bytes 3145736 | tf_op jit(solution)/shard_map/ppermute | solution.py:225
  576.3 14.0 %collective-permute-start.108 = (f32[8,8192]{1,0:T(8,128)}, f32[8,8192]{1,0:T(8,128)S(1)}, u32[]{:S(2)}, u32[]{:S(2)}) collective-permute-start(f32[8,8192]{1,0:T(8,128)} %get-tuple-element.235), channel_id=1, source_target_pairs={{0,2},{1,3},{2,0},{3,1},{4,6},{5,7},{6,4},{7,5},{8,10},{9,11},{10,... | collective-permute-start | bytes 786440 | tf_op jit(solution)/shard_map/ppermute | solution.py:225
  577.5 13.8 %collective-permute-start.109 = (f32[8,8192]{1,0:T(8,128)}, f32[8,8192]{1,0:T(8,128)S(1)}, u32[]{:S(2)}, u32[]{:S(2)}) collective-permute-start(f32[8,8192]{1,0:T(8,128)} %get-tuple-element.236), channel_id=1, source_target_pairs={{0,2},{1,3},{2,0},{3,1},{4,6},{5,7},{6,4},{7,5},{8,10},{9,11},{10,... | collective-permute-start | bytes 786440 | tf_op jit(solution)/shard_map/ppermute | solution.py:225
  578.4 18.6 %collective-permute-start.110 = (f32[8,8192]{1,0:T(8,128)}, f32[8,8192]{1,0:T(8,128)S(1)}, u32[]{:S(2)}, u32[]{:S(2)}) collective-permute-start(f32[8,8192]{1,0:T(8,128)} %get-tuple-element.237), channel_id=1, source_target_pairs={{0,2},{1,3},{2,0},{3,1},{4,6},{5,7},{6,4},{7,5},{8,10},{9,11},{10,... | collective-permute-start | bytes 786440 | tf_op jit(solution)/shard_map/ppermute | solution.py:225
  579.6 22.2 %collective-permute-start.111 = (f32[8,8192]{1,0:T(8,128)}, f32[8,8192]{1,0:T(8,128)S(1)}, u32[]{:S(2)}, u32[]{:S(2)}) collective-permute-start(f32[8,8192]{1,0:T(8,128)} %get-tuple-element.238), channel_id=1, source_target_pairs={{0,2},{1,3},{2,0},{3,1},{4,6},{5,7},{6,4},{7,5},{8,10},{9,11},{10,... | collective-permute-start | bytes 786440 | tf_op jit(solution)/shard_map/ppermute | solution.py:225
  (184 other events, 787.8 us)

commit v4 on v3

--- a/solution.py
+++ b/solution.py
@@ -285,40 +285,57 @@
     )(keep, *near, *after)
 
 
-def pair_sum(value, size, between=(None, None), last=None, after=()):
+def quarter_index():
+    return jnp.reshape(lax.axis_index("pair") % 4, (1,)).astype(jnp.int32)
+
+
+def scatter_sum(value, size, hook=None, after=()):
     rows, columns = value.shape
     block = rows // 4
-    me = jnp.reshape(lax.axis_index("pair") % 4, (1,)).astype(jnp.int32)
 
     def cut(m_ref, v_ref, *out):
         for d, o in enumerate(out):
             o[...] = v_ref[pl.ds(pl.multiple_of((m_ref[0] ^ d) * block, 8), block), :]
 
+    mine, *rest = small(cut, [(block, columns)] * 4, value, scalar=quarter_index(), name="cut", after=after)
+    others = [swap_with(r, "pair", size, d) for d, r in enumerate(rest, 1)]
+    return total_of(mine, *others, after=[hook([mine])] if hook else [])
+
+
+def across_sum(total, size, hook=None):
+    distance = 4
+    while distance < size:
+        other = swap_with(total, "pair", size, distance)
+        total = total_of(total, other, after=[hook([total])] if hook and distance == 4 else [])
+        distance *= 2
+    return total
+
+
+def gather_all(total, size):
+    block, columns = total.shape
+
     def gather(m_ref, *refs):
         for d, r in enumerate(refs[:-1]):
             refs[-1][pl.ds(pl.multiple_of((m_ref[0] ^ d) * block, 8), block), :] = r[...]
 
-    mine, *rest = small(cut, [(block, columns)] * 4, value, scalar=me, name="cut", after=after)
-    others = [swap_with(r, "pair", size, d) for d, r in enumerate(rest, 1)]
-    after = [between[0]([mine])] if between[0] else []
-    total = total_of(mine, *others, after=after)
-    distance = 4
-    while distance < size:
-        other = swap_with(total, "pair", size, distance)
-        after = [between[1]([total])] if between[1] and distance == 4 else []
-        total = total_of(total, other, after=after)
-        distance *= 2
     every = [total] + [swap_with(total, "pair", size, d) for d in (1, 2, 3)]
-    after = [last([total])] if last else []
-    return small(gather, [(rows, columns)], *every, scalar=me, name="gather", after=after)[0]
+    return small(gather, [(4 * block, columns)], *every, scalar=quarter_index(), name="gather")[0]
+
+
+def pair_sum(value, size, between=(None, None), after=()):
+    total = scatter_sum(value, size, between[0], after)
+    return gather_all(across_sum(total, size, between[1]), size)
 
 
 def small_sum(value, size):
     if size & (size - 1):
         return lax.psum(value, "pair")
     distance = 1
+    if size % 4 == 0:
+        value = total_of(value, *(swap_with(value, "pair", size, d) for d in (1, 2, 3)))
+        distance = 4
     while distance < size:
-        value = value + swap_with(value, "pair", size, distance)
+        value = total_of(value, swap_with(value, "pair", size, distance))
         distance *= 2
     return value
 
@@ -340,7 +357,7 @@
     over = functools.partial(pass_over, factor)
     wide = dict(gaps=gaps, stored=stored, which=which)
 
-    def project(fitted):
+    def project(fitted, after=()):
         def part(m_ref, f_ref, w_ref, keep_ref, send_ref):
             f = jnp.concatenate(split(4.0 * f_ref[:, :aux]), axis=0)
             own = f_ref[:, aux:]
@@ -359,7 +376,7 @@
             o_ref[:h] = k_ref[:h] + t_ref[h:]
             o_ref[h:] = k_ref[h:] + t_ref[:h]
 
-        keep, send = small(part, [(two, total)] * 2, fitted, crossed, scalar=which[0], name="project")
+        keep, send = small(part, [(two, total)] * 2, fitted, crossed, scalar=which[0], name="project", after=after)
         first_part = keep
         keep = total_of(keep, aux_swap(send, distance=1))
         part_sum = small(both, [(two, total)], keep, aux_swap(keep, distance=2), name="both")[0]
@@ -373,28 +390,6 @@
     def near_too(parts, token):
         parts = lax.optimization_barrier((*parts, token))[:2]
         return [*parts, *(aux_swap(p, distance=1) for p in parts)]
-
-    (crossed,) = over(0, local, parts=[stored])
-    everyone[0] = near_too(everyone[0], crossed)
-    held = [None]
-
-    def first_fit(c):
-        def run(after):
-            held.extend(over(c, kc, parts=everyone[0], before=held[-1], after=after, **wide))
-            return held[-1]
-
-        return run
-
-    begins = []
-
-    def first_way(after):
-        begins.append(pair_sum(held[-1], n_pair, after=after))
-        everyone[1] = near_too(everyone[1], begins[0])
-        begins.append(over(0, kc, fitted=begins[0], parts=everyone[1], **wide))
-        return begins[1][2]
-
-    crossed = pair_sum(crossed, n_pair, (first_fit(0), first_fit(1)), first_way)
-    one = begins[0]
 
     def summed(keep, send, after):
         (keep,) = joined(keep, [aux_swap(x, distance=1) for x in send], 1, after)
@@ -408,23 +403,61 @@
         squares[g] = squares[g] + square[:h]
         return new[0]
 
-    begun, first = project(one)
+    (crossed,) = over(0, local // 2, parts=[stored])
+    everyone[0] = near_too(everyone[0], crossed)
+    partial, held = None, [crossed]
+    for c in range(chunks):
+        (partial,) = over(c, kc, parts=everyone[0], before=partial, after=[crossed], **wide)
+
+    def other_half(after):
+        held.extend(over(1, local // 2, parts=[stored], before=crossed, after=after))
+        return held[-1]
+
+    one = pair_sum(partial, n_pair, (other_half, None))
+    everyone[1] = near_too(everyone[1], one)
+
     projected = [[None, None], [None, None]]
-    projected[0][0] = first[:h]
-    keep, send, partial = begins[1]
-    sent = [[summed(keep, send, [first])], []]
-    for c in range(1, chunks):
-        keep, send, partial = over(
-            c, kc, fitted=one, parts=everyone[1], before=partial, after=[sent[0][-1][0][0]], **wide
-        )
-        sent[0].append(summed(keep, send, []))
-    two_sum = pair_sum(partial, n_pair)
     current = [[], []]
     squares = [0.0, 0.0]
+    sent = [[], []]
+    held = [held[-1], None]
+
+    ways = []
+
+    def first_way(c):
+        def run(after):
+            if c:
+                sent[0].append(summed(*ways[0], after))
+                after = [*after, sent[0][0][0][0]]
+            keep, send, held[1] = over(
+                c, kc, fitted=one, parts=everyone[1], before=held[1], after=after, **wide
+            )
+            ways.append((keep, send))
+            return held[1]
+
+        return run
+
+    crossed = pair_sum(held[0], n_pair, (first_way(0), first_way(1)))
+    two_sum = scatter_sum(held[1], n_pair)
+    begun, first = project(one, [two_sum])
+    projected[0][0] = first[:h]
+    sent[0].append(summed(*ways[1], [first]))
+    firsts = []
+
+    def early(g, projection):
+        def run(after):
+            firsts.append(new_vectors(g, 0, projection, after))
+            return firsts[-1]
+
+        return run
+
+    hook = early(0, first)
+    two_sum = across_sum(two_sum, n_pair, lambda after: hook([*after, sent[0][-1][0][0]]))
+    two_sum = gather_all(two_sum, n_pair)
     begun, second = project(two_sum)
     projected[0][1] = second[:h]
 
-    partial, token = None, new_vectors(0, 0, first, [two_sum, sent[0][-1][0][0]])
+    partial, token = None, firsts[0]
     for c in range(chunks):
         keep, send, partial = over(
             c, kc, fitted=two_sum, parts=current[0][c], before=partial, after=[begun, token], **wide
@@ -434,7 +467,7 @@
             token = new_vectors(0, c + 1, first, [partial])
         sent[1].append(summed(keep, send, [second, token]))
         token = sent[1][-1][0][0]
-    one = pair_sum(partial, n_pair)
+    one = pair_sum(partial, n_pair, (None, early(1, second)))
     begun, aux_sum = project(one)
     first = aux_sum[:h]
     projected[1][0] = first
@@ -445,7 +478,6 @@
         return out[:split_in], [aux_swap(x, distance=2) for x in out[split_in:]]
 
     last = [[], []]
-    token = new_vectors(1, 0, second, [token])
     keep, send, partial = over(0, kc, fitted=one, parts=current[1][0], after=[begun, token], **wide)
     last[0].append(last_sum(keep, send, [aux_sum]))
     for c in range(1, chunks):

time: 642 us -> 670 us (1.044)
  waiting for transfers between devices: 119 us -> 139 us
  Pallas kernels: 370 us -> 378 us
    ppermute x115 -> x116, waiting for transfers between devices: 119 us -> 139 us  [swap_with(): return lax.ppermute(value, axis, [(i, i ^ distance) for i in range(size)])]
    pallas_call x12 -> x13, Pallas kernels: 268 us -> 275 us  [pass_over(): pl.pallas_call(kernel, out_shape=tuple(shapes), grid_spec=pltpu.PrefetchS...]
    unnamed x230 -> x266, local copies, waits for them, and re-layouts: 39.2 us -> 41.8 us
    ppermute x115 -> x116, starting transfers between devices: 91.1 us -> 89.8 us  [swap_with(): return lax.ppermute(value, axis, [(i, i ^ distance) for i in range(size)])]
  transfers between devices with their start and end apart: 115 -> 116, of which waited for: 69 -> 66; matrix products, arithmetic and copies ran while one was open for 0% -> 0% of each run, Pallas kernels for 51% -> 51%
where the time goes in v4:
time: 670 us; the launch traced here: 662 us
  Pallas kernels  378 us (56%)
  waiting for transfers between devices  139 us (21%)
  starting transfers between devices  89.8 us (13%)
  local copies, waits for them, and re-layouts  47 us (7%)
    pallas_call x13, Pallas kernels, pass_over(): pl.pallas_call(kernel, out_shape=tuple(shapes), grid_spec=pltpu.PrefetchS...  275 us
    ppermute x116, waiting for transfers between devices, swap_with(): return lax.ppermute(value, axis, [(i, i ^ distance) for i in range(size)])  139 us
    ppermute x116, starting transfers between devices, swap_with(): return lax.ppermute(value, axis, [(i, i ^ distance) for i in range(size)])  89.8 us
    pallas_call x8, Pallas kernels, assemble(): pl.pallas_call(kernel, out_shape=(*[jax.ShapeDtypeStruct((piece, columns)...  71.7 us
    unnamed x266, local copies, waits for them, and re-layouts  41.8 us
    pallas_call x8, Pallas kernels, joined(): pl.pallas_call(kernel, out_shape=tuple([jax.ShapeDtypeStruct((height, col...  26.4 us
  transfers between devices with their start and end apart: 116, of which 66 were waited for; matrix products, arithmetic and copies ran while one was open for 0% of the time, Pallas kernels for 51%

profile of v4, /device:TPU:0, one launch (start us, length us, event | category | flops | bytes accessed | tf_op | source)
XLA Modules:
  0.0 662.0 jit_solution(12093306300977078255)
XLA Ops:
  0.6 3.8 fusion.9
  4.5 3.0 collective-permute-start
  7.4 25.8 %fit.5.refs_8_.refs_9_.refs_2_ = f32[384,1024]{1,0:T(8,128)} custom-call(f32[16384,1024]{1,0:T(8,128)} %refs_0_.9, f32[384,16384]{1,0:T(8,128)} %refs_11_.3), custom_call_target="tpu_custom_call" | custom-call | flops 1 | bytes 1 | tf_op jit(solution)/shard_map/fit/pallas_call | solution.py:136
  33.2 20.1 %collective-permute-done.refs_3_ = f32[32,16384]{1,0:T(8,128)} collective-permute-done((f32[32,16384]{1,0:T(8,128)}, f32[32,16384]{1,0:T(8,128)}, u32[]{:S(2)}, u32[]{:S(2)}) %collective-permute-start) | collective-permute-done | bytes 2097184 | tf_op jit(solution)/shard_map/ppermute | solution.py:225
  57.9 3.0 collective-permute-done.2.refs_5_
  60.9 16.6 %fit.6.refs_8_ = f32[128,1152]{1,0:T(8,128)} custom-call(s32[1]{0:T(128)} %bitcast.refs_0_, f32[16384,1024]{1,0:T(8,128)} %refs_0_.9, f32[32,16384]{1,0:T(8,128)} %get-tuple-element.125.refs_2_, f32[32,16384]{1,0:T(8,128)} %collective-permute-done.refs_3_, f32[32,16384]{1,0:T(8,128)} %collective-permute-done.1.refs_4_, ...), custom_call_target="tpu_custom_call" | custom-call | flops 1 | bytes 1 | tf_op jit(solution)/shard_map/fit/pallas_call | solution.py:136
  77.5 17.0 %fit.7.refs_1_ = f32[128,1152]{1,0:T(8,128)} custom-call(s32[1]{0:T(128)} %bitcast.refs_0_, f32[16384,1024]{1,0:T(8,128)} %refs_0_.9, f32[32,16384]{1,0:T(8,128)} %get-tuple-element.125.refs_2_, f32[32,16384]{1,0:T(8,128)} %collective-permute-done.refs_3_, f32[32,16384]{1,0:T(8,128)} %collective-permute-done.1.refs_4_, ...), custom_call_target="tpu_custom_call" | custom-call | flops 1 | bytes 1 | tf_op jit(solution)/shard_map/fit/pallas_call | solution.py:136
  99.7 26.5 %fit.8.refs_4_.refs_1_ = f32[384,1024]{1,0:T(8,128)} custom-call(f32[16384,1024]{1,0:T(8,128)} %refs_0_.9, f32[384,16384]{1,0:T(8,128)} %refs_11_.3, f32[384,1024]{1,0:T(8,128)} %fit.5.refs_8_.refs_9_.refs_2_, f32[32,1152]{1,0:T(8,128)} %copy-done.38), custom_call_target="tpu_custom_call" | custom-call | flops 1 | bytes 1 | tf_op jit(solution)/shard_map/fit/pallas_call | solution.py:136
  127.7 2.9 collective-permute-start.6
  130.6 6.4 collective-permute-done.6.refs_1_
  156.0 24.1 %spreadfit.5 = (f32[64,8192]{1,0:T(8,128)}, f32[16,8192]{1,0:T(8,128)}, f32[16,8192]{1,0:T(8,128)}, f32[16,8192]{1,0:T(8,128)}, f32[16,8192]{1,0:T(8,128)}, /*index=5*/f32[128,1152]{1,0:T(8,128)}) custom-call(s32[1]{0:T(128)} %bitcast.refs_0_, f32[16384,1024]{1,0:T(8,128)} %refs_0_.9, f32[128,1152]{1,0:T(8,128)} %copy-done.2, f32[32,16384]{1,0:T(8,128)} %copy-done.43, ...), custom_call_target="tpu_custom_call" | custom-call | flops 1 | bytes 1 | tf_op jit(solution)/shard_map/spreadfit/pallas_call | solution.py:136
  183.1 2.7 collective-permute-start.25
  187.1 3.2 joined.8.refs_11_.refs_0_
  191.9 24.8 %spreadfit.6 = (f32[64,8192]{1,0:T(8,128)}, f32[16,8192]{1,0:T(8,128)}, f32[16,8192]{1,0:T(8,128)}, f32[16,8192]{1,0:T(8,128)}, f32[16,8192]{1,0:T(8,128)}, /*index=5*/f32[128,1152]{1,0:T(8,128)}) custom-call(s32[1]{0:T(128)} %bitcast.refs_0_, f32[16384,1024]{1,0:T(8,128)} %refs_0_.9, f32[128,1152]{1,0:T(8,128)} %copy-done.2, f32[32,16384]{1,0:T(8,128)} %copy-done.43, ...), custom_call_target="tpu_custom_call" | custom-call | flops 1 | bytes 1 | tf_op jit(solution)/shard_map/spreadfit/pallas_call | solution.py:136
  226.8 16.9 %collective-permute-done.21.refs_2_ = f32[32,1152]{1,0:T(8,128)S(1)} collective-permute-done((f32[32,1152]{1,0:T(8,128)S(1)}, f32[32,1152]{1,0:T(8,128)S(1)}, u32[]{:S(2)}, u32[]{:S(2)}) %collective-permute-start.21) | collective-permute-done | bytes 147488 | tf_op jit(solution)/shard_map/ppermute | solution.py:225
  243.7 2.7 collective-permute-start.22
  246.4 3.4 collective-permute-done.22.refs_3_
  253.2 3.8 collective-permute-done.30.refs_1_
  259.7 3.3 joined.9.refs_8_.refs_0_
  265.9 9.4 %assemble.8 = (f32[16,8192]{1,0:T(8,128)}, f32[16,8192]{1,0:T(8,128)}, f32[16,8192]{1,0:T(8,128)}, f32[16,8192]{1,0:T(8,128)}, f32[64,128]{1,0:T(8,128)}) custom-call(f32[64,8192]{1,0:T(8,128)} %joined.8.refs_11_.refs_0_, f32[64,8192]{1,0:T(8,128)} %copy-done.50, f32[32,16384]{1,0:T(8,128)} %get-tuple-element.125.refs_2_, ...), custom_call_target="tpu_custom_call" | custom-call | flops 1 | bytes 1 | tf_op jit(solution)/shard_map/assemble/pallas_call | solution.py:205
  282.7 2.8 collective-permute-done.36.refs_3_
  293.1 24.4 %spreadfit.7 = (f32[64,8192]{1,0:T(8,128)}, f32[16,8192]{1,0:T(8,128)}, f32[16,8192]{1,0:T(8,128)}, f32[16,8192]{1,0:T(8,128)}, f32[16,8192]{1,0:T(8,128)}, /*index=5*/f32[128,1152]{1,0:T(8,128)}) custom-call(s32[1]{0:T(128)} %bitcast.refs_0_, f32[16384,1024]{1,0:T(8,128)} %refs_0_.9, f32[128,1152]{1,0:T(8,128)} %copy-done.6, ...), custom_call_target="tpu_custom_call" | custom-call | flops 1 | bytes 1 | tf_op jit(solution)/shard_map/spreadfit/pallas_call | solution.py:136
  320.6 9.4 %assemble.9 = (f32[16,8192]{1,0:T(8,128)}, f32[16,8192]{1,0:T(8,128)}, f32[16,8192]{1,0:T(8,128)}, f32[16,8192]{1,0:T(8,128)}, f32[64,128]{1,0:T(8,128)}) custom-call(f32[64,8192]{1,0:T(8,128)} %joined.9.refs_8_.refs_0_, f32[64,8192]{1,0:T(8,128)} %copy-done.51, f32[32,16384]{1,0:T(8,128)} %get-tuple-element.125.refs_2_, ...), custom_call_target="tpu_custom_call" | custom-call | flops 1 | bytes 1 | tf_op jit(solution)/shard_map/assemble/pallas_call | solution.py:205
  331.3 3.4 joined.10.refs_15_.refs_0_
  341.3 24.5 %spreadfit.8 = (f32[64,8192]{1,0:T(8,128)}, f32[16,8192]{1,0:T(8,128)}, f32[16,8192]{1,0:T(8,128)}, f32[16,8192]{1,0:T(8,128)}, f32[16,8192]{1,0:T(8,128)}, /*index=5*/f32[128,1152]{1,0:T(8,128)}) custom-call(s32[1]{0:T(128)} %bitcast.refs_0_, f32[16384,1024]{1,0:T(8,128)} %refs_0_.9, f32[128,1152]{1,0:T(8,128)} %copy-done.6, ...), custom_call_target="tpu_custom_call" | custom-call | flops 1 | bytes 1 | tf_op jit(solution)/shard_map/spreadfit/pallas_call | solution.py:136
  372.9 3.3 joined.11.refs_14_.refs_0_
  380.4 3.0 collective-permute-done.57.refs_1_
  384.7 9.6 %assemble.10 = (f32[16,8192]{1,0:T(8,128)}, f32[16,8192]{1,0:T(8,128)}, f32[16,8192]{1,0:T(8,128)}, f32[16,8192]{1,0:T(8,128)}, f32[64,128]{1,0:T(8,128)}) custom-call(f32[64,8192]{1,0:T(8,128)} %joined.10.refs_15_.refs_0_, f32[64,8192]{1,0:T(8,128)} %copy-done.52, f32[32,16384]{1,0:T(8,128)} %copy-done.43, ...), custom_call_target="tpu_custom_call" | custom-call | flops 1 | bytes 1 | tf_op jit(solution)/shard_map/assemble/pallas_call | solution.py:205
  412.1 24.2 %spreadfit.9 = (f32[64,8192]{1,0:T(8,128)}, f32[16,8192]{1,0:T(8,128)}, f32[16,8192]{1,0:T(8,128)}, f32[16,8192]{1,0:T(8,128)}, f32[16,8192]{1,0:T(8,128)}, /*index=5*/f32[128,1152]{1,0:T(8,128)}) custom-call(s32[1]{0:T(128)} %bitcast.refs_0_, f32[16384,1024]{1,0:T(8,128)} %refs_0_.9, f32[128,1152]{1,0:T(8,128)} %copy-done.4, ...), custom_call_target="tpu_custom_call" | custom-call | flops 1 | bytes 1 | tf_op jit(solution)/shard_map/spreadfit/pallas_call | solution.py:136
  441.5 3.3 joined.12
  444.8 16.5 %spread.3 = (f32[64,8192]{1,0:T(8,128)}, f32[16,8192]{1,0:T(8,128)}, f32[16,8192]{1,0:T(8,128)}, f32[16,8192]{1,0:T(8,128)}, f32[16,8192]{1,0:T(8,128)}) custom-call(f32[16384,1024]{1,0:T(8,128)} %refs_0_.9, f32[128,1152]{1,0:T(8,128)} %copy-done.4, f32[32,8192]{1,0:T(8,128)} %get-tuple-element.192.refs_2_.refs_0_), custom_call_target="tpu_custom_call" | custom-call | flops 1 | bytes 1 | tf_op jit(solution)/shard_map/spread/pallas_call | solution.py:136
  466.5 3.3 joined.13
  471.1 9.6 %assemble.11 = (f32[16,8192]{1,0:T(8,128)}, f32[16,8192]{1,0:T(8,128)}, f32[16,8192]{1,0:T(8,128)}, f32[16,8192]{1,0:T(8,128)}, f32[64,128]{1,0:T(8,128)}) custom-call(f32[64,8192]{1,0:T(8,128)} %joined.11.refs_14_.refs_0_, f32[64,8192]{1,0:T(8,128)} %copy-done.49, f32[32,16384]{1,0:T(8,128)} %copy-done.43, ...), custom_call_target="tpu_custom_call" | custom-call | flops 1 | bytes 1 | tf_op jit(solution)/shard_map/assemble/pallas_call | solution.py:205
  487.5 17.4 %fit.9.refs_1_ = f32[128,1152]{1,0:T(8,128)} custom-call(s32[1]{0:T(128)} %bitcast.refs_0_, f32[16384,1024]{1,0:T(8,128)} %refs_0_.9, f32[16,8192]{1,0:T(8,128)} %get-tuple-element.200.refs_2_.refs_8_, f32[16,8192]{1,0:T(8,128)} %get-tuple-element.201.refs_3_.refs_9_, f32[16,8192]{1,0:T(8,128)} %get-tuple-element.202.refs_4_, ...), custom_call_target="tpu_custom_call" | custom-call | flops 1 | bytes 1 | tf_op jit(solution)/shard_map/fit/pallas_call | solution.py:136
  511.9 8.2 %assemble.12 = (f32[32,8192]{1,0:T(8,128)}, f32[32,128]{1,0:T(8,128)}) custom-call(f32[32,8192]{1,0:T(8,128)} %get-tuple-element.192.refs_2_.refs_0_, f32[32,8192]{1,0:T(8,128)} %copy-done.56, f32[16,8192]{1,0:T(8,128)} %get-tuple-element.155.refs_2_.refs_3_.refs_14_, f32[16,8192]{1,0:T(8,128)} %get-tuple-element.156.refs_4_.refs_3_, ...), custom_call_target="tpu_custom_call" | custom-call | flops 1 | bytes 1 | tf_op jit(solution)/shard_map/assemble/pallas_call | solution.py:205
  523.2 5.6 collective-permute-done.85.refs_1_
  529.8 8.2 %assemble.13 = (f32[32,8192]{1,0:T(8,128)}, f32[32,128]{1,0:T(8,128)}) custom-call(f32[32,8192]{1,0:T(8,128)} %get-tuple-element.199.refs_7_.refs_0_, f32[32,8192]{1,0:T(8,128)} %copy-done.55, f32[16,8192]{1,0:T(8,128)} %get-tuple-element.161.refs_5_.refs_3_.refs_2_, f32[16,8192]{1,0:T(8,128)} %get-tuple-element.162.refs_4_.refs_3_, ...), custom_call_target="tpu_custom_call" | custom-call | flops 1 | bytes 1 | tf_op jit(solution)/shard_map/assemble/pallas_call | solution.py:205
  551.1 16.5 %spread.4 = (f32[64,8192]{1,0:T(8,128)}, f32[16,8192]{1,0:T(8,128)}, f32[16,8192]{1,0:T(8,128)}, f32[16,8192]{1,0:T(8,128)}, f32[16,8192]{1,0:T(8,128)}) custom-call(f32[16384,1024]{1,0:T(8,128)} %refs_0_.9, f32[128,1152]{1,0:T(8,128)} %copy-done.5, f32[64,384]{1,0:T(8,128)} %copy-done.41), custom_call_target="tpu_custom_call" | custom-call | flops 1 | bytes 1 | tf_op jit(solution)/shard_map/spread/pallas_call | solution.py:136
  572.2 3.3 collective-permute-done.98.refs_1_
  577.5 3.2 joined.14
  582.2 16.5 %spread.5 = (f32[64,8192]{1,0:T(8,128)}, f32[8,8192]{1,0:T(8,128)}, f32[8,8192]{1,0:T(8,128)}, f32[8,8192]{1,0:T(8,128)}, f32[8,8192]{1,0:T(8,128)}, /*index=5*/...) custom-call(f32[16384,1024]{1,0:T(8,128)} %refs_0_.9, f32[128,1152]{1,0:T(8,128)} %copy-done.5, ...), custom_call_target="tpu_custom_call" | custom-call | flops 1 | bytes 1 | tf_op jit(solution)/shard_map/spread/pallas_call | solution.py:136
  604.1 3.5 joined.15
  613.5 8.2 %assemble.14 = (f32[32,8192]{1,0:T(8,128)}, f32[32,128]{1,0:T(8,128)}) custom-call(f32[32,8192]{1,0:T(8,128)} %get-tuple-element.219.refs_0_.refs_2_, f32[32,8192]{1,0:T(8,128)} %copy-done.57, f32[16,8192]{1,0:T(8,128)} %get-tuple-element.176.refs_2_.refs_3_, f32[16,8192]{1,0:T(8,128)} %get-tuple-element.177.refs_4_.refs_3_, ...), custom_call_target="tpu_custom_call" | custom-call | flops 1 | bytes 1 | tf_op jit(solution)/shard_map/assemble/pallas_call | solution.py:205
  622.7 5.6 collective-permute-done.110.refs_6_
  628.4 4.8 collective-permute-done.111.refs_7_
  633.9 9.1 %assemble.15 = (f32[32,8192]{1,0:T(8,128)}, f32[32,128]{1,0:T(8,128)}) custom-call(f32[8,8192]{1,0:T(8,128)} %get-tuple-element.231.refs_0_, f32[8,8192]{1,0:T(8,128)} %get-tuple-element.232.refs_1_, f32[8,8192]{1,0:T(8,128)} %get-tuple-element.233.refs_2_, f32[8,8192]{1,0:T(8,128)} %get-tuple-element.234.refs_3_, f32[8,8192]{1,0:T(8,128)} %copy-done.108, ...), custom_call_target="tpu_custom_call" | custom-call | flops 1 | bytes 1 | tf_op jit(solution)/shard_map/assemble/pallas_call | solution.py:205
  653.3 3.9 collective-permute-done.115.refs_1_
  658.2 3.6 maximum_divide_fusion
  (530 shorter events, 185.7 us)
Async XLA Ops:
  4.5 48.9 %collective-permute-start = (f32[32,16384]{1,0:T(8,128)}, f32[32,16384]{1,0:T(8,128)}, u32[]{:S(2)}, u32[]{:S(2)}) collective-permute-start(f32[32,16384]{1,0:T(8,128)} %get-tuple-element.125.refs_2_), channel_id=1, source_target_pairs={{0,2},{1,3},{2,0},{3,1},{4,6},{5,7},{6,4},{7,5},{8,10},{9,11},{10,... | collective-permute-start | bytes 6291464 | tf_op jit(solution)/shard_map/ppermute | solution.py:225
  53.4 7.5 %collective-permute-start.2 = (f32[32,16384]{1,0:T(8,128)}, f32[32,16384]{1,0:T(8,128)}, u32[]{:S(2)}, u32[]{:S(2)}) collective-permute-start(f32[32,16384]{1,0:T(8,128)} %collective-permute-done.refs_3_), channel_id=1, source_target_pairs={{0,1},{1,0},{2,3},{3,2},{4,5},{5,4},{6,7},{7,6},{8,9},{9,8},{10,11... | collective-permute-start | bytes 6291464 | tf_op jit(solution)/shard_map/ppermute | solution.py:225
  53.9 93.0 %collective-permute-start.10 = (f32[32,16384]{1,0:T(8,128)S(1)}, f32[32,16384]{1,0:T(8,128)}, u32[]{:S(2)}, u32[]{:S(2)}) collective-permute-start(f32[32,16384]{1,0:T(8,128)S(1)} %get-tuple-element.131.refs_3_.refs_2_), channel_id=1, source_target_pairs={{0,2},{1,3},{2,0},{3,1},{4,6},{5,7},{6,4},{7,5},{8,10},{9,11},{10,... | collective-permute-start | bytes 6291464 | tf_op jit(solution)/shard_map/ppermute | solution.py:225
  96.3 30.0 %collective-permute-start.3 = (f32[32,1152]{1,0:T(8,128)S(1)}, f32[32,1152]{1,0:T(8,128)S(1)}, u32[]{:S(2)}, u32[]{:S(2)}) collective-permute-start(f32[32,1152]{1,0:T(8,128)S(1)} %get-tuple-element.128), channel_id=1, source_target_pairs={{0,4},{4,0},{8,12},{12,8},{16,20},{20,16},{24,28},{28,24},{1,5},{5... | collective-permute-start | bytes 442376 | tf_op jit(solution)/shard_map/ppermute | solution.py:225
  98.0 28.3 %collective-permute-start.4 = (f32[32,1152]{1,0:T(8,128)S(1)}, f32[32,1152]{1,0:T(8,128)S(1)}, u32[]{:S(2)}, u32[]{:S(2)}) collective-permute-start(f32[32,1152]{1,0:T(8,128)S(1)} %get-tuple-element.129), channel_id=1, source_target_pairs={{0,8},{4,12},{8,0},{12,4},{16,24},{20,28},{24,16},{28,20},{1,9},{5... | collective-permute-start | bytes 442376 | tf_op jit(solution)/shard_map/ppermute | solution.py:225
  99.5 26.7 %collective-permute-start.5 = (f32[32,1152]{1,0:T(8,128)S(1)}, f32[32,1152]{1,0:T(8,128)S(1)}, u32[]{:S(2)}, u32[]{:S(2)}) collective-permute-start(f32[32,1152]{1,0:T(8,128)S(1)} %get-tuple-element.130), channel_id=1, source_target_pairs={{0,12},{4,8},{8,4},{12,0},{16,28},{20,24},{24,20},{28,16},{1,13},{... | collective-permute-start | bytes 442376 | tf_op jit(solution)/shard_map/ppermute | solution.py:225
  127.7 9.3 %collective-permute-start.6 = (f32[32,1152]{1,0:T(8,128)S(1)}, f32[32,1152]{1,0:T(8,128)S(1)}, u32[]{:S(2)}, u32[]{:S(2)}) collective-permute-start(f32[32,1152]{1,0:T(8,128)S(1)} %total.16.refs_0_), channel_id=1, source_target_pairs={{0,16},{4,20},{8,24},{12,28},{16,0},{20,4},{24,8},{28,12},{1,17},{... | collective-permute-start | bytes 442376 | tf_op jit(solution)/shard_map/ppermute | solution.py:225
  139.3 7.5 %collective-permute-start.9 = (f32[32,1152]{1,0:T(8,128)S(1)}, f32[32,1152]{1,0:T(8,128)S(1)}, u32[]{:S(2)}, u32[]{:S(2)}) collective-permute-start(f32[32,1152]{1,0:T(8,128)S(1)} %total.17.refs_1_), channel_id=1, source_target_pairs={{0,12},{4,8},{8,4},{12,0},{16,28},{20,24},{24,20},{28,16},{1,13},{... | collective-permute-start | bytes 442376 | tf_op jit(solution)/shard_map/ppermute | solution.py:225
  147.0 7.4 %collective-permute-start.12 = (f32[32,16384]{1,0:T(8,128)}, f32[32,16384]{1,0:T(8,128)S(1)}, u32[]{:S(2)}, u32[]{:S(2)}) collective-permute-start(f32[32,16384]{1,0:T(8,128)} %collective-permute-done.10.refs_4_.refs_3_), channel_id=1, source_target_pairs={{0,1},{1,0},{2,3},{3,2},{4,5},{5,4},{6,7},{7,6},{8,9},{9,8},{10,11... | collective-permute-start | bytes 6291464 | tf_op jit(solution)/shard_map/ppermute | solution.py:225
  148.5 32.2 %collective-permute-start.13 = (f32[96,1024]{1,0:T(8,128)S(1)}, f32[96,1024]{1,0:T(8,128)S(1)}, u32[]{:S(2)}, u32[]{:S(2)}) collective-permute-start(f32[96,1024]{1,0:T(8,128)S(1)} %get-tuple-element.135), channel_id=1, source_target_pairs={{0,4},{4,0},{8,12},{12,8},{16,20},{20,16},{24,28},{28,24},{1,5},{5... | collective-permute-start | bytes 1179656 | tf_op jit(solution)/shard_map/ppermute | solution.py:225
  149.3 31.5 %collective-permute-start.14 = (f32[96,1024]{1,0:T(8,128)S(1)}, f32[96,1024]{1,0:T(8,128)S(1)}, u32[]{:S(2)}, u32[]{:S(2)}) collective-permute-start(f32[96,1024]{1,0:T(8,128)S(1)} %get-tuple-element.136), channel_id=1, source_target_pairs={{0,8},{4,12},{8,0},{12,4},{16,24},{20,28},{24,16},{28,20},{1,9},{5... | collective-permute-start | bytes 1179656 | tf_op jit(solution)/shard_map/ppermute | solution.py:225
  151.1 30.2 %collective-permute-start.15 = (f32[96,1024]{1,0:T(8,128)S(1)}, f32[96,1024]{1,0:T(8,128)S(1)}, u32[]{:S(2)}, u32[]{:S(2)}) collective-permute-start(f32[96,1024]{1,0:T(8,128)S(1)} %get-tuple-element.137), channel_id=1, source_target_pairs={{0,12},{4,8},{8,4},{12,0},{16,28},{20,24},{24,20},{28,16},{1,13},{... | collective-permute-start | bytes 1179656 | tf_op jit(solution)/shard_map/ppermute | solution.py:225
  183.1 36.3 %collective-permute-start.25 = (f32[96,1024]{1,0:T(8,128)}, f32[96,1024]{1,0:T(8,128)S(1)}, u32[]{:S(2)}, u32[]{:S(2)}) collective-permute-start(f32[96,1024]{1,0:T(8,128)} %total.18.refs_4_.refs_10_.refs_0_), channel_id=1, source_target_pairs={{0,16},{4,20},{8,24},{12,28},{16,0},{20,4},{24,8},{28,12},{1,17},{... | collective-permute-start | bytes 1179656 | tf_op jit(solution)/shard_map/ppermute | solution.py:225
  190.4 74.2 %collective-permute-start.24 = (f32[64,8192]{1,0:T(8,128)}, f32[64,8192]{1,0:T(8,128)S(1)}, u32[]{:S(2)}, u32[]{:S(2)}) collective-permute-start(f32[64,8192]{1,0:T(8,128)} %joined.8.refs_11_.refs_0_), channel_id=1, source_target_pairs={{0,2},{1,3},{2,0},{3,1},{4,6},{5,7},{6,4},{7,5},{8,10},{9,11},{10,... | collective-permute-start | bytes 6291464 | tf_op jit(solution)/shard_map/ppermute | solution.py:225
  217.8 7.2 %collective-permute-start.20 = (f32[32,1152]{1,0:T(8,128)S(1)}, f32[32,1152]{1,0:T(8,128)S(1)}, u32[]{:S(2)}, u32[]{:S(2)}) collective-permute-start(f32[32,1152]{1,0:T(8,128)S(1)} %get-tuple-element.145), channel_id=1, source_target_pairs={{0,4},{4,0},{8,12},{12,8},{16,20},{20,16},{24,28},{28,24},{1,5},{5... | collective-permute-start | bytes 442376 | tf_op jit(solution)/shard_map/ppermute | solution.py:225
  221.5 28.4 %collective-permute-start.26 = (f32[96,1024]{1,0:T(8,128)S(1)}, f32[96,1024]{1,0:T(8,128)S(1)}, u32[]{:S(2)}, u32[]{:S(2)}) collective-permute-start(f32[96,1024]{1,0:T(8,128)S(1)} %total.20.refs_1_), channel_id=1, source_target_pairs={{0,4},{4,0},{8,12},{12,8},{16,20},{20,16},{24,28},{28,24},{1,5},{5... | collective-permute-start | bytes 1179656 | tf_op jit(solution)/shard_map/ppermute | solution.py:225
  222.1 27.8 %collective-permute-start.27 = (f32[96,1024]{1,0:T(8,128)S(1)}, f32[96,1024]{1,0:T(8,128)S(1)}, u32[]{:S(2)}, u32[]{:S(2)}) collective-permute-start(f32[96,1024]{1,0:T(8,128)S(1)} %total.20.refs_1_), channel_id=1, source_target_pairs={{0,8},{4,12},{8,0},{12,4},{16,24},{20,28},{24,16},{28,20},{1,9},{5... | collective-permute-start | bytes 1179656 | tf_op jit(solution)/shard_map/ppermute | solution.py:225
  223.8 26.0 %collective-permute-start.28 = (f32[96,1024]{1,0:T(8,128)S(1)}, f32[96,1024]{1,0:T(8,128)S(1)}, u32[]{:S(2)}, u32[]{:S(2)}) collective-permute-start(f32[96,1024]{1,0:T(8,128)S(1)} %total.20.refs_1_), channel_id=1, source_target_pairs={{0,12},{4,8},{8,4},{12,0},{16,28},{20,24},{24,20},{28,16},{1,13},{... | collective-permute-start | bytes 1179656 | tf_op jit(solution)/shard_map/ppermute | solution.py:225
  225.0 18.7 %collective-permute-start.21 = (f32[32,1152]{1,0:T(8,128)S(1)}, f32[32,1152]{1,0:T(8,128)S(1)}, u32[]{:S(2)}, u32[]{:S(2)}) collective-permute-start(f32[32,1152]{1,0:T(8,128)S(1)} %get-tuple-element.146), channel_id=1, source_target_pairs={{0,8},{4,12},{8,0},{12,4},{16,24},{20,28},{24,16},{28,20},{1,9},{5... | collective-permute-start | bytes 442376 | tf_op jit(solution)/shard_map/ppermute | solution.py:225
  263.0 56.3 %collective-permute-start.38 = (f32[64,8192]{1,0:T(8,128)}, f32[64,8192]{1,0:T(8,128)S(1)}, u32[]{:S(2)}, u32[]{:S(2)}) collective-permute-start(f32[64,8192]{1,0:T(8,128)} %joined.9.refs_8_.refs_0_), channel_id=1, source_target_pairs={{0,2},{1,3},{2,0},{3,1},{4,6},{5,7},{6,4},{7,5},{8,10},{9,11},{10,... | collective-permute-start | bytes 6291464 | tf_op jit(solution)/shard_map/ppermute | solution.py:225
  263.4 11.9 %collective-permute-start.23 = (f32[32,1152]{1,0:T(8,128)S(1)}, f32[32,1152]{1,0:T(8,128)S(1)}, u32[]{:S(2)}, u32[]{:S(2)}) collective-permute-start(f32[32,1152]{1,0:T(8,128)S(1)} %total.19.refs_3_.refs_7_.refs_0_), channel_id=1, source_target_pairs={{0,16},{4,20},{8,24},{12,28},{16,0},{20,4},{24,8},{28,12},{1,17},{... | collective-permute-start | bytes 442376 | tf_op jit(solution)/shard_map/ppermute | solution.py:225
  290.0 28.4 %collective-permute-start.52 = (f32[64,384]{1,0:T(8,128)S(1)}, f32[64,384]{1,0:T(8,128)S(1)}, u32[]{:S(2)}, u32[]{:S(2)}) collective-permute-start(f32[64,384]{1,0:T(8,128)S(1)} %total.23.refs_0_), channel_id=1, source_target_pairs={{0,2},{1,3},{2,0},{3,1},{4,6},{5,7},{6,4},{7,5},{8,10},{9,11},{10,... | collective-permute-start | bytes 294920 | tf_op jit(solution)/shard_map/ppermute | solution.py:225
  317.5 12.4 %collective-permute-start.47 = (f32[16,8192]{1,0:T(8,128)}, f32[16,8192]{1,0:T(8,128)S(1)}, u32[]{:S(2)}, u32[]{:S(2)}) collective-permute-start(f32[16,8192]{1,0:T(8,128)} %get-tuple-element.166), channel_id=1, source_target_pairs={{0,1},{1,0},{2,3},{3,2},{4,5},{5,4},{6,7},{7,6},{8,9},{9,8},{10,11... | collective-permute-start | bytes 1572872 | tf_op jit(solution)/shard_map/ppermute | solution.py:225
  317.9 12.0 %collective-permute-start.48 = (f32[16,8192]{1,0:T(8,128)}, f32[16,8192]{1,0:T(8,128)S(1)}, u32[]{:S(2)}, u32[]{:S(2)}) collective-permute-start(f32[16,8192]{1,0:T(8,128)} %get-tuple-element.167), channel_id=1, source_target_pairs={{0,1},{1,0},{2,3},{3,2},{4,5},{5,4},{6,7},{7,6},{8,9},{9,8},{10,11... | collective-permute-start | bytes 1572872 | tf_op jit(solution)/shard_map/ppermute | solution.py:225
  318.1 11.9 %collective-permute-start.49 = (f32[16,8192]{1,0:T(8,128)}, f32[16,8192]{1,0:T(8,128)S(1)}, u32[]{:S(2)}, u32[]{:S(2)}) collective-permute-start(f32[16,8192]{1,0:T(8,128)} %get-tuple-element.168), channel_id=1, source_target_pairs={{0,1},{1,0},{2,3},{3,2},{4,5},{5,4},{6,7},{7,6},{8,9},{9,8},{10,11... | collective-permute-start | bytes 1572872 | tf_op jit(solution)/shard_map/ppermute | solution.py:225
  318.4 11.6 %collective-permute-start.50 = (f32[16,8192]{1,0:T(8,128)}, f32[16,8192]{1,0:T(8,128)S(1)}, u32[]{:S(2)}, u32[]{:S(2)}) collective-permute-start(f32[16,8192]{1,0:T(8,128)} %get-tuple-element.169), channel_id=1, source_target_pairs={{0,1},{1,0},{2,3},{3,2},{4,5},{5,4},{6,7},{7,6},{8,9},{9,8},{10,11... | collective-permute-start | bytes 1572872 | tf_op jit(solution)/shard_map/ppermute | solution.py:225
  334.7 48.7 %collective-permute-start.57 = (f32[64,8192]{1,0:T(8,128)}, f32[64,8192]{1,0:T(8,128)S(1)}, u32[]{:S(2)}, u32[]{:S(2)}) collective-permute-start(f32[64,8192]{1,0:T(8,128)} %joined.10.refs_15_.refs_0_), channel_id=1, source_target_pairs={{0,2},{1,3},{2,0},{3,1},{4,6},{5,7},{6,4},{7,5},{8,10},{9,11},{10,... | collective-permute-start | bytes 6291464 | tf_op jit(solution)/shard_map/ppermute | solution.py:225
  368.0 8.6 %collective-permute-start.53 = (f32[32,1152]{1,0:T(8,128)S(1)}, f32[32,1152]{1,0:T(8,128)S(1)}, u32[]{:S(2)}, u32[]{:S(2)}) collective-permute-start(f32[32,1152]{1,0:T(8,128)S(1)} %get-tuple-element.173), channel_id=1, source_target_pairs={{0,4},{4,0},{8,12},{12,8},{16,20},{20,16},{24,28},{28,24},{1,5},{5... | collective-permute-start | bytes 442376 | tf_op jit(solution)/shard_map/ppermute | solution.py:225
  369.5 7.2 %collective-permute-start.54 = (f32[32,1152]{1,0:T(8,128)S(1)}, f32[32,1152]{1,0:T(8,128)S(1)}, u32[]{:S(2)}, u32[]{:S(2)}) collective-permute-start(f32[32,1152]{1,0:T(8,128)S(1)} %get-tuple-element.174), channel_id=1, source_target_pairs={{0,8},{4,12},{8,0},{12,4},{16,24},{20,28},{24,16},{28,20},{1,9},{5... | collective-permute-start | bytes 442376 | tf_op jit(solution)/shard_map/ppermute | solution.py:225
  371.2 7.4 %collective-permute-start.55 = (f32[32,1152]{1,0:T(8,128)S(1)}, f32[32,1152]{1,0:T(8,128)S(1)}, u32[]{:S(2)}, u32[]{:S(2)}) collective-permute-start(f32[32,1152]{1,0:T(8,128)S(1)} %get-tuple-element.175), channel_id=1, source_target_pairs={{0,12},{4,8},{8,4},{12,0},{16,28},{20,24},{24,20},{28,16},{1,13},{... | collective-permute-start | bytes 442376 | tf_op jit(solution)/shard_map/ppermute | solution.py:225
  376.1 93.7 %collective-permute-start.76 = (f32[64,8192]{1,0:T(8,128)}, f32[64,8192]{1,0:T(8,128)S(1)}, u32[]{:S(2)}, u32[]{:S(2)}) collective-permute-start(f32[64,8192]{1,0:T(8,128)} %joined.11.refs_14_.refs_0_), channel_id=1, source_target_pairs={{0,2},{1,3},{2,0},{3,1},{4,6},{5,7},{6,4},{7,5},{8,10},{9,11},{10,... | collective-permute-start | bytes 6291464 | tf_op jit(solution)/shard_map/ppermute | solution.py:225
  378.7 15.7 %collective-permute-start.56 = (f32[32,1152]{1,0:T(8,128)S(1)}, f32[32,1152]{1,0:T(8,128)S(1)}, u32[]{:S(2)}, u32[]{:S(2)}) collective-permute-start(f32[32,1152]{1,0:T(8,128)S(1)} %total.24.refs_7_.refs_0_), channel_id=1, source_target_pairs={{0,16},{4,20},{8,24},{12,28},{16,0},{20,4},{24,8},{28,12},{1,17},{... | collective-permute-start | bytes 442376 | tf_op jit(solution)/shard_map/ppermute | solution.py:225
  409.0 28.2 %collective-permute-start.74 = (f32[64,384]{1,0:T(8,128)S(1)}, f32[64,384]{1,0:T(8,128)S(1)}, u32[]{:S(2)}, u32[]{:S(2)}) collective-permute-start(f32[64,384]{1,0:T(8,128)S(1)} %total.26.refs_0_), channel_id=1, source_target_pairs={{0,2},{1,3},{2,0},{3,1},{4,6},{5,7},{6,4},{7,5},{8,10},{9,11},{10,... | collective-permute-start | bytes 294920 | tf_op jit(solution)/shard_map/ppermute | solution.py:225
  481.1 29.8 %collective-permute-start.75 = (f32[32,8192]{1,0:T(8,128)S(1)}, f32[32,8192]{1,0:T(8,128)S(1)}, u32[]{:S(2)}, u32[]{:S(2)}) collective-permute-start(f32[32,8192]{1,0:T(8,128)S(1)} %copy-done.127), channel_id=1, source_target_pairs={{0,2},{1,3},{2,0},{3,1},{4,6},{5,7},{6,4},{7,5},{8,10},{9,11},{10,... | collective-permute-start | bytes 3145736 | tf_op jit(solution)/shard_map/ppermute | solution.py:225
  482.7 46.1 %collective-permute-start.85 = (f32[32,8192]{1,0:T(8,128)S(1)}, f32[32,8192]{1,0:T(8,128)S(1)}, u32[]{:S(2)}, u32[]{:S(2)}) collective-permute-start(f32[32,8192]{1,0:T(8,128)S(1)} %copy-done.128), channel_id=1, source_target_pairs={{0,2},{1,3},{2,0},{3,1},{4,6},{5,7},{6,4},{7,5},{8,10},{9,11},{10,... | collective-permute-start | bytes 3145736 | tf_op jit(solution)/shard_map/ppermute | solution.py:225
  506.7 13.3 %collective-permute-start.86 = (f32[32,1152]{1,0:T(8,128)S(1)}, f32[32,1152]{1,0:T(8,128)S(1)}, u32[]{:S(2)}, u32[]{:S(2)}) collective-permute-start(f32[32,1152]{1,0:T(8,128)S(1)} %get-tuple-element.208), channel_id=1, source_target_pairs={{0,4},{4,0},{8,12},{12,8},{16,20},{20,16},{24,28},{28,24},{1,5},{5... | collective-permute-start | bytes 442376 | tf_op jit(solution)/shard_map/ppermute | solution.py:225
  507.6 12.5 %collective-permute-start.87 = (f32[32,1152]{1,0:T(8,128)S(1)}, f32[32,1152]{1,0:T(8,128)S(1)}, u32[]{:S(2)}, u32[]{:S(2)}) collective-permute-start(f32[32,1152]{1,0:T(8,128)S(1)} %get-tuple-element.209), channel_id=1, source_target_pairs={{0,8},{4,12},{8,0},{12,4},{16,24},{20,28},{24,16},{28,20},{1,9},{5... | collective-permute-start | bytes 442376 | tf_op jit(solution)/shard_map/ppermute | solution.py:225
  509.3 10.8 %collective-permute-start.88 = (f32[32,1152]{1,0:T(8,128)S(1)}, f32[32,1152]{1,0:T(8,128)S(1)}, u32[]{:S(2)}, u32[]{:S(2)}) collective-permute-start(f32[32,1152]{1,0:T(8,128)S(1)} %get-tuple-element.210), channel_id=1, source_target_pairs={{0,12},{4,8},{8,4},{12,0},{16,28},{20,24},{24,20},{28,16},{1,13},{... | collective-permute-start | bytes 442376 | tf_op jit(solution)/shard_map/ppermute | solution.py:225
  521.4 16.6 %collective-permute-start.89 = (f32[32,1152]{1,0:T(8,128)S(1)}, f32[32,1152]{1,0:T(8,128)S(1)}, u32[]{:S(2)}, u32[]{:S(2)}) collective-permute-start(f32[32,1152]{1,0:T(8,128)S(1)} %total.27.refs_7_.refs_0_), channel_id=1, source_target_pairs={{0,16},{4,20},{8,24},{12,28},{16,0},{20,4},{24,8},{28,12},{1,17},{... | collective-permute-start | bytes 442376 | tf_op jit(solution)/shard_map/ppermute | solution.py:225
  567.6 8.5 %collective-permute-start.93 = (f32[16,8192]{1,0:T(8,128)}, f32[16,8192]{1,0:T(8,128)S(1)}, u32[]{:S(2)}, u32[]{:S(2)}) collective-permute-start(f32[16,8192]{1,0:T(8,128)} %get-tuple-element.214), channel_id=1, source_target_pairs={{0,1},{1,0},{2,3},{3,2},{4,5},{5,4},{6,7},{7,6},{8,9},{9,8},{10,11... | collective-permute-start | bytes 1572872 | tf_op jit(solution)/shard_map/ppermute | solution.py:225
  567.6 8.5 %collective-permute-start.94 = (f32[16,8192]{1,0:T(8,128)}, f32[16,8192]{1,0:T(8,128)S(1)}, u32[]{:S(2)}, u32[]{:S(2)}) collective-permute-start(f32[16,8192]{1,0:T(8,128)} %get-tuple-element.215), channel_id=1, source_target_pairs={{0,1},{1,0},{2,3},{3,2},{4,5},{5,4},{6,7},{7,6},{8,9},{9,8},{10,11... | collective-permute-start | bytes 1572872 | tf_op jit(solution)/shard_map/ppermute | solution.py:225
  568.2 8.0 %collective-permute-start.95 = (f32[16,8192]{1,0:T(8,128)}, f32[16,8192]{1,0:T(8,128)S(1)}, u32[]{:S(2)}, u32[]{:S(2)}) collective-permute-start(f32[16,8192]{1,0:T(8,128)} %get-tuple-element.216), channel_id=1, source_target_pairs={{0,1},{1,0},{2,3},{3,2},{4,5},{5,4},{6,7},{7,6},{8,9},{9,8},{10,11... | collective-permute-start | bytes 1572872 | tf_op jit(solution)/shard_map/ppermute | solution.py:225
  568.2 8.0 %collective-permute-start.96 = (f32[16,8192]{1,0:T(8,128)}, f32[16,8192]{1,0:T(8,128)S(1)}, u32[]{:S(2)}, u32[]{:S(2)}) collective-permute-start(f32[16,8192]{1,0:T(8,128)} %get-tuple-element.217), channel_id=1, source_target_pairs={{0,1},{1,0},{2,3},{3,2},{4,5},{5,4},{6,7},{7,6},{8,9},{9,8},{10,11... | collective-permute-start | bytes 1572872 | tf_op jit(solution)/shard_map/ppermute | solution.py:225
  580.7 31.8 %collective-permute-start.99 = (f32[32,8192]{1,0:T(8,128)}, f32[32,8192]{1,0:T(8,128)S(1)}, u32[]{:S(2)}, u32[]{:S(2)}) collective-permute-start(f32[32,8192]{1,0:T(8,128)} %get-tuple-element.220), channel_id=1, source_target_pairs={{0,2},{1,3},{2,0},{3,1},{4,6},{5,7},{6,4},{7,5},{8,10},{9,11},{10,... | collective-permute-start | bytes 3145736 | tf_op jit(solution)/shard_map/ppermute | solution.py:225
  607.7 14.0 %collective-permute-start.108 = (f32[8,8192]{1,0:T(8,128)}, f32[8,8192]{1,0:T(8,128)S(1)}, u32[]{:S(2)}, u32[]{:S(2)}) collective-permute-start(f32[8,8192]{1,0:T(8,128)} %get-tuple-element.235), channel_id=1, source_target_pairs={{0,2},{1,3},{2,0},{3,1},{4,6},{5,7},{6,4},{7,5},{8,10},{9,11},{10,... | collective-permute-start | bytes 786440 | tf_op jit(solution)/shard_map/ppermute | solution.py:225
  608.2 14.5 %collective-permute-start.109 = (f32[8,8192]{1,0:T(8,128)}, f32[8,8192]{1,0:T(8,128)S(1)}, u32[]{:S(2)}, u32[]{:S(2)}) collective-permute-start(f32[8,8192]{1,0:T(8,128)} %get-tuple-element.236), channel_id=1, source_target_pairs={{0,2},{1,3},{2,0},{3,1},{4,6},{5,7},{6,4},{7,5},{8,10},{9,11},{10,... | collective-permute-start | bytes 786440 | tf_op jit(solution)/shard_map/ppermute | solution.py:225
  609.8 18.6 %collective-permute-start.110 = (f32[8,8192]{1,0:T(8,128)}, f32[8,8192]{1,0:T(8,128)S(1)}, u32[]{:S(2)}, u32[]{:S(2)}) collective-permute-start(f32[8,8192]{1,0:T(8,128)} %get-tuple-element.237), channel_id=1, source_target_pairs={{0,2},{1,3},{2,0},{3,1},{4,6},{5,7},{6,4},{7,5},{8,10},{9,11},{10,... | collective-permute-start | bytes 786440 | tf_op jit(solution)/shard_map/ppermute | solution.py:225
  610.3 22.9 %collective-permute-start.111 = (f32[8,8192]{1,0:T(8,128)}, f32[8,8192]{1,0:T(8,128)S(1)}, u32[]{:S(2)}, u32[]{:S(2)}) collective-permute-start(f32[8,8192]{1,0:T(8,128)} %get-tuple-element.238), channel_id=1, source_target_pairs={{0,2},{1,3},{2,0},{3,1},{4,6},{5,7},{6,4},{7,5},{8,10},{9,11},{10,... | collective-permute-start | bytes 786440 | tf_op jit(solution)/shard_map/ppermute | solution.py:225
  (203 other events, 1088.1 us)

commit v5 on v3

--- a/solution.py
+++ b/solution.py
@@ -317,8 +317,11 @@
     if size & (size - 1):
         return lax.psum(value, "pair")
     distance = 1
+    if size % 4 == 0:
+        value = total_of(value, *(swap_with(value, "pair", size, d) for d in (1, 2, 3)))
+        distance = 4
     while distance < size:
-        value = value + swap_with(value, "pair", size, distance)
+        value = total_of(value, swap_with(value, "pair", size, distance))
         distance *= 2
     return value
 
@@ -418,13 +421,22 @@
             c, kc, fitted=one, parts=everyone[1], before=partial, after=[sent[0][-1][0][0]], **wide
         )
         sent[0].append(summed(keep, send, []))
-    two_sum = pair_sum(partial, n_pair)
     current = [[], []]
     squares = [0.0, 0.0]
+    firsts = []
+
+    def early(g, projection, token):
+        def run(after):
+            firsts.append(new_vectors(g, 0, projection, [*after, *token]))
+            return firsts[-1]
+
+        return run
+
+    two_sum = pair_sum(partial, n_pair, (None, early(0, first, [sent[0][-1][0][0]])))
     begun, second = project(two_sum)
     projected[0][1] = second[:h]
 
-    partial, token = None, new_vectors(0, 0, first, [two_sum, sent[0][-1][0][0]])
+    partial, token = None, firsts[0]
     for c in range(chunks):
         keep, send, partial = over(
             c, kc, fitted=two_sum, parts=current[0][c], before=partial, after=[begun, token], **wide
@@ -434,7 +446,7 @@
             token = new_vectors(0, c + 1, first, [partial])
         sent[1].append(summed(keep, send, [second, token]))
         token = sent[1][-1][0][0]
-    one = pair_sum(partial, n_pair)
+    one = pair_sum(partial, n_pair, (None, early(1, second, [token])))
     begun, aux_sum = project(one)
     first = aux_sum[:h]
     projected[1][0] = first
@@ -445,8 +457,7 @@
         return out[:split_in], [aux_swap(x, distance=2) for x in out[split_in:]]
 
     last = [[], []]
-    token = new_vectors(1, 0, second, [token])
-    keep, send, partial = over(0, kc, fitted=one, parts=current[1][0], after=[begun, token], **wide)
+    keep, send, partial = over(0, kc, fitted=one, parts=current[1][0], after=[begun, firsts[1]], **wide)
     last[0].append(last_sum(keep, send, [aux_sum]))
     for c in range(1, chunks):
         keep, send = over(c, kc, fitted=one, after=[last[0][-1][0][0]])

time: 642 us -> 634 us (0.988)
  waiting for transfers between devices: 119 us -> 104 us
    ppermute x115 -> x116, waiting for transfers between devices: 119 us -> 104 us  [swap_with(): return lax.ppermute(value, axis, [(i, i ^ distance) for i in range(size)])]
    ppermute x115 -> x116, starting transfers between devices: 91.1 us -> 95.1 us  [swap_with(): return lax.ppermute(value, axis, [(i, i ^ distance) for i in range(size)])]
    unnamed x230 -> x256, local copies, waits for them, and re-layouts: 39.2 us -> 42.6 us
  transfers between devices with their start and end apart: 115 -> 116, of which waited for: 69 -> 72; matrix products, arithmetic and copies ran while one was open for 0% -> 0% of each run, Pallas kernels for 51% -> 52%
where the time goes in v5:
time: 634 us; the launch traced here: 625 us
  Pallas kernels  370 us (58%)
  waiting for transfers between devices  104 us (16%)
  starting transfers between devices  95.1 us (15%)
  local copies, waits for them, and re-layouts  48.4 us (8%)
    pallas_call x12, Pallas kernels, pass_over(): pl.pallas_call(kernel, out_shape=tuple(shapes), grid_spec=pltpu.PrefetchS...  268 us
    ppermute x116, waiting for transfers between devices, swap_with(): return lax.ppermute(value, axis, [(i, i ^ distance) for i in range(size)])  104 us
    ppermute x116, starting transfers between devices, swap_with(): return lax.ppermute(value, axis, [(i, i ^ distance) for i in range(size)])  95.1 us
    pallas_call x8, Pallas kernels, assemble(): pl.pallas_call(kernel, out_shape=(*[jax.ShapeDtypeStruct((piece, columns)...  71.9 us
    unnamed x256, local copies, waits for them, and re-layouts  42.6 us
    pallas_call x8, Pallas kernels, joined(): pl.pallas_call(kernel, out_shape=tuple([jax.ShapeDtypeStruct((height, col...  26.2 us
  transfers between devices with their start and end apart: 116, of which 72 were waited for; matrix products, arithmetic and copies ran while one was open for 0% of the time, Pallas kernels for 52%

profile of v5, /device:TPU:0, one launch (start us, length us, event | category | flops | bytes accessed | tf_op | source)
XLA Modules:
  0.0 625.4 jit_solution(15771924796848477050)
XLA Ops:
  0.6 4.6 fusion.9
  5.2 3.0 collective-permute-start
  8.2 46.1 %fit.4.refs_1_ = f32[384,1024]{1,0:T(8,128)} custom-call(f32[16384,1024]{1,0:T(8,128)} %refs_0_.7, f32[384,16384]{1,0:T(8,128)} %refs_11_.3), custom_call_target="tpu_custom_call" | custom-call | flops 1 | bytes 1 | tf_op jit(solution)/shard_map/fit/pallas_call | solution.py:136
  62.1 16.7 %fit.5.refs_4_.refs_8_ = f32[128,1152]{1,0:T(8,128)} custom-call(s32[1]{0:T(128)} %bitcast.refs_0_, f32[16384,1024]{1,0:T(8,128)} %refs_0_.7, f32[32,16384]{1,0:T(8,128)} %get-tuple-element.125.refs_2_, f32[32,16384]{1,0:T(8,128)} %collective-permute-done.refs_3_, f32[32,16384]{1,0:T(8,128)} %collective-permute-done.1.refs_4_, ...), custom_call_target="tpu_custom_call" | custom-call | flops 1 | bytes 1 | tf_op jit(solution)/shard_map/fit/pallas_call | solution.py:136
  80.1 2.7 collective-permute-start.6
  82.8 17.0 %fit.6.refs_2_.refs_1_ = f32[128,1152]{1,0:T(8,128)} custom-call(s32[1]{0:T(128)} %bitcast.refs_0_, f32[16384,1024]{1,0:T(8,128)} %refs_0_.7, f32[32,16384]{1,0:T(8,128)} %get-tuple-element.125.refs_2_, f32[32,16384]{1,0:T(8,128)} %collective-permute-done.refs_3_, f32[32,16384]{1,0:T(8,128)} %collective-permute-done.1.refs_4_, ...), custom_call_target="tpu_custom_call" | custom-call | flops 1 | bytes 1 | tf_op jit(solution)/shard_map/fit/pallas_call | solution.py:136
  113.2 2.7 collective-permute-start.10
  116.0 6.5 %collective-permute-done.10.refs_1_ = f32[32,1152]{1,0:T(8,128)S(1)} collective-permute-done((f32[32,1152]{1,0:T(8,128)S(1)}, f32[32,1152]{1,0:T(8,128)S(1)}, u32[]{:S(2)}, u32[]{:S(2)}) %collective-permute-start.10) | collective-permute-done | bytes 147488 | tf_op jit(solution)/shard_map/ppermute | solution.py:225
  137.3 3.0 collective-permute-done.16.refs_6_
  141.6 24.3 %spreadfit.5 = (f32[64,8192]{1,0:T(8,128)}, f32[16,8192]{1,0:T(8,128)}, f32[16,8192]{1,0:T(8,128)}, f32[16,8192]{1,0:T(8,128)}, f32[16,8192]{1,0:T(8,128)}, /*index=5*/f32[128,1152]{1,0:T(8,128)}) custom-call(s32[1]{0:T(128)} %bitcast.refs_0_, f32[16384,1024]{1,0:T(8,128)} %refs_0_.7, f32[128,1152]{1,0:T(8,128)} %copy-done, ...), custom_call_target="tpu_custom_call" | custom-call | flops 1 | bytes 1 | tf_op jit(solution)/shard_map/spreadfit/pallas_call | solution.py:136
  172.0 3.3 collective-permute-done.25.refs_1_
  177.3 3.2 joined.8.refs_10_.refs_0_
  182.1 24.2 %spreadfit.6 = (f32[64,8192]{1,0:T(8,128)}, f32[16,8192]{1,0:T(8,128)}, f32[16,8192]{1,0:T(8,128)}, f32[16,8192]{1,0:T(8,128)}, f32[16,8192]{1,0:T(8,128)}, /*index=5*/f32[128,1152]{1,0:T(8,128)}) custom-call(s32[1]{0:T(128)} %bitcast.refs_0_, f32[16384,1024]{1,0:T(8,128)} %refs_0_.7, f32[128,1152]{1,0:T(8,128)} %copy-done, ...), custom_call_target="tpu_custom_call" | custom-call | flops 1 | bytes 1 | tf_op jit(solution)/shard_map/spreadfit/pallas_call | solution.py:136
  211.6 3.3 joined.9.refs_8_.refs_0_
  225.4 2.6 collective-permute-start.29
  230.6 9.8 %assemble.8 = (f32[16,8192]{1,0:T(8,128)}, f32[16,8192]{1,0:T(8,128)}, f32[16,8192]{1,0:T(8,128)}, f32[16,8192]{1,0:T(8,128)}, f32[64,128]{1,0:T(8,128)}) custom-call(f32[64,8192]{1,0:T(8,128)} %joined.8.refs_10_.refs_0_, f32[64,8192]{1,0:T(8,128)} %copy-done.51, f32[32,16384]{1,0:T(8,128)} %get-tuple-element.125.refs_2_, ...), custom_call_target="tpu_custom_call" | custom-call | flops 1 | bytes 1 | tf_op jit(solution)/shard_map/assemble/pallas_call | solution.py:205
  246.0 2.9 collective-permute-done.35.refs_2_
  256.8 24.2 %spreadfit.7 = (f32[64,8192]{1,0:T(8,128)}, f32[16,8192]{1,0:T(8,128)}, f32[16,8192]{1,0:T(8,128)}, f32[16,8192]{1,0:T(8,128)}, f32[16,8192]{1,0:T(8,128)}, /*index=5*/f32[128,1152]{1,0:T(8,128)}) custom-call(s32[1]{0:T(128)} %bitcast.refs_0_, f32[16384,1024]{1,0:T(8,128)} %refs_0_.7, f32[128,1152]{1,0:T(8,128)} %copy-done.4, ...), custom_call_target="tpu_custom_call" | custom-call | flops 1 | bytes 1 | tf_op jit(solution)/shard_map/spreadfit/pallas_call | solution.py:136
  284.1 9.4 %assemble.9 = (f32[16,8192]{1,0:T(8,128)}, f32[16,8192]{1,0:T(8,128)}, f32[16,8192]{1,0:T(8,128)}, f32[16,8192]{1,0:T(8,128)}, f32[64,128]{1,0:T(8,128)}) custom-call(f32[64,8192]{1,0:T(8,128)} %joined.9.refs_8_.refs_0_, f32[64,8192]{1,0:T(8,128)} %copy-done.49, f32[32,16384]{1,0:T(8,128)} %get-tuple-element.125.refs_2_, ...), custom_call_target="tpu_custom_call" | custom-call | flops 1 | bytes 1 | tf_op jit(solution)/shard_map/assemble/pallas_call | solution.py:205
  294.9 3.4 joined.10.refs_15_.refs_0_
  304.9 24.6 %spreadfit.8 = (f32[64,8192]{1,0:T(8,128)}, f32[16,8192]{1,0:T(8,128)}, f32[16,8192]{1,0:T(8,128)}, f32[16,8192]{1,0:T(8,128)}, f32[16,8192]{1,0:T(8,128)}, /*index=5*/f32[128,1152]{1,0:T(8,128)}) custom-call(s32[1]{0:T(128)} %bitcast.refs_0_, f32[16384,1024]{1,0:T(8,128)} %refs_0_.7, f32[128,1152]{1,0:T(8,128)} %copy-done.4, ...), custom_call_target="tpu_custom_call" | custom-call | flops 1 | bytes 1 | tf_op jit(solution)/shard_map/spreadfit/pallas_call | solution.py:136
  336.1 3.2 joined.11.refs_8_.refs_0_
  342.1 3.4 collective-permute-start.56
  348.3 9.4 %assemble.10 = (f32[16,8192]{1,0:T(8,128)}, f32[16,8192]{1,0:T(8,128)}, f32[16,8192]{1,0:T(8,128)}, f32[16,8192]{1,0:T(8,128)}, f32[64,128]{1,0:T(8,128)}) custom-call(f32[64,8192]{1,0:T(8,128)} %joined.10.refs_15_.refs_0_, f32[64,8192]{1,0:T(8,128)} %copy-done.50, f32[32,16384]{1,0:T(8,128)} %get-tuple-element.135.refs_3_.refs_2_, ...), custom_call_target="tpu_custom_call" | custom-call | flops 1 | bytes 1 | tf_op jit(solution)/shard_map/assemble/pallas_call | solution.py:205
  363.3 3.2 collective-permute-done.62.refs_2_
  374.8 24.2 %spreadfit.9 = (f32[64,8192]{1,0:T(8,128)}, f32[16,8192]{1,0:T(8,128)}, f32[16,8192]{1,0:T(8,128)}, f32[16,8192]{1,0:T(8,128)}, f32[16,8192]{1,0:T(8,128)}, /*index=5*/f32[128,1152]{1,0:T(8,128)}) custom-call(s32[1]{0:T(128)} %bitcast.refs_0_, f32[16384,1024]{1,0:T(8,128)} %refs_0_.7, f32[128,1152]{1,0:T(8,128)} %copy-done.2, ...), custom_call_target="tpu_custom_call" | custom-call | flops 1 | bytes 1 | tf_op jit(solution)/shard_map/spreadfit/pallas_call | solution.py:136
  404.2 3.2 joined.12
  407.5 16.5 %spread.3 = (f32[64,8192]{1,0:T(8,128)}, f32[16,8192]{1,0:T(8,128)}, f32[16,8192]{1,0:T(8,128)}, f32[16,8192]{1,0:T(8,128)}, f32[16,8192]{1,0:T(8,128)}) custom-call(f32[16384,1024]{1,0:T(8,128)} %refs_0_.7, f32[128,1152]{1,0:T(8,128)} %copy-done.2, f32[32,8192]{1,0:T(8,128)} %get-tuple-element.192.refs_2_.refs_0_), custom_call_target="tpu_custom_call" | custom-call | flops 1 | bytes 1 | tf_op jit(solution)/shard_map/spread/pallas_call | solution.py:136
  429.2 3.3 joined.13
  433.8 9.7 %assemble.11 = (f32[16,8192]{1,0:T(8,128)}, f32[16,8192]{1,0:T(8,128)}, f32[16,8192]{1,0:T(8,128)}, f32[16,8192]{1,0:T(8,128)}, f32[64,128]{1,0:T(8,128)}) custom-call(f32[64,8192]{1,0:T(8,128)} %joined.11.refs_8_.refs_0_, f32[64,8192]{1,0:T(8,128)} %copy-done.48, f32[32,16384]{1,0:T(8,128)} %get-tuple-element.135.refs_3_.refs_2_, ...), custom_call_target="tpu_custom_call" | custom-call | flops 1 | bytes 1 | tf_op jit(solution)/shard_map/assemble/pallas_call | solution.py:205
  450.4 17.1 %fit.7.refs_1_ = f32[128,1152]{1,0:T(8,128)} custom-call(s32[1]{0:T(128)} %bitcast.refs_0_, f32[16384,1024]{1,0:T(8,128)} %refs_0_.7, f32[16,8192]{1,0:T(8,128)} %get-tuple-element.200.refs_2_.refs_8_, f32[16,8192]{1,0:T(8,128)} %get-tuple-element.201.refs_3_.refs_9_, f32[16,8192]{1,0:T(8,128)} %get-tuple-element.202.refs_4_, ...), custom_call_target="tpu_custom_call" | custom-call | flops 1 | bytes 1 | tf_op jit(solution)/shard_map/fit/pallas_call | solution.py:136
  474.3 8.2 %assemble.12 = (f32[32,8192]{1,0:T(8,128)}, f32[32,128]{1,0:T(8,128)}) custom-call(f32[32,8192]{1,0:T(8,128)} %get-tuple-element.192.refs_2_.refs_0_, f32[32,8192]{1,0:T(8,128)} %copy-done.55, f32[16,8192]{1,0:T(8,128)} %get-tuple-element.155.refs_2_.refs_3_.refs_14_, f32[16,8192]{1,0:T(8,128)} %get-tuple-element.156.refs_4_.refs_3_, ...), custom_call_target="tpu_custom_call" | custom-call | flops 1 | bytes 1 | tf_op jit(solution)/shard_map/assemble/pallas_call | solution.py:205
  483.8 3.5 collective-permute-start.89
  487.3 4.3 collective-permute-done.85.refs_1_
  492.6 8.2 %assemble.13 = (f32[32,8192]{1,0:T(8,128)}, f32[32,128]{1,0:T(8,128)}) custom-call(f32[32,8192]{1,0:T(8,128)} %get-tuple-element.199.refs_7_.refs_0_, f32[32,8192]{1,0:T(8,128)} %copy-done.54, f32[16,8192]{1,0:T(8,128)} %get-tuple-element.161.refs_5_.refs_3_.refs_2_, f32[16,8192]{1,0:T(8,128)} %get-tuple-element.162.refs_4_.refs_3_, ...), custom_call_target="tpu_custom_call" | custom-call | flops 1 | bytes 1 | tf_op jit(solution)/shard_map/assemble/pallas_call | solution.py:205
  506.5 2.6 collective-permute-done.90.refs_2_
  513.7 16.5 %spread.4 = (f32[64,8192]{1,0:T(8,128)}, f32[16,8192]{1,0:T(8,128)}, f32[16,8192]{1,0:T(8,128)}, f32[16,8192]{1,0:T(8,128)}, f32[16,8192]{1,0:T(8,128)}) custom-call(f32[16384,1024]{1,0:T(8,128)} %refs_0_.7, f32[128,1152]{1,0:T(8,128)} %copy-done.3, f32[64,384]{1,0:T(8,128)} %copy-done.41), custom_call_target="tpu_custom_call" | custom-call | flops 1 | bytes 1 | tf_op jit(solution)/shard_map/spread/pallas_call | solution.py:136
  534.9 3.2 collective-permute-done.98.refs_1_
  540.1 3.3 joined.14
  545.0 16.7 %spread.5 = (f32[64,8192]{1,0:T(8,128)}, f32[8,8192]{1,0:T(8,128)}, f32[8,8192]{1,0:T(8,128)}, f32[8,8192]{1,0:T(8,128)}, f32[8,8192]{1,0:T(8,128)}, /*index=5*/...) custom-call(f32[16384,1024]{1,0:T(8,128)} %refs_0_.7, f32[128,1152]{1,0:T(8,128)} %copy-done.3, ...), custom_call_target="tpu_custom_call" | custom-call | flops 1 | bytes 1 | tf_op jit(solution)/shard_map/spread/pallas_call | solution.py:136
  567.1 3.3 joined.15
  576.3 8.2 %assemble.14 = (f32[32,8192]{1,0:T(8,128)}, f32[32,128]{1,0:T(8,128)}) custom-call(f32[32,8192]{1,0:T(8,128)} %get-tuple-element.219.refs_0_.refs_2_, f32[32,8192]{1,0:T(8,128)} %copy-done.56, f32[16,8192]{1,0:T(8,128)} %get-tuple-element.181.refs_2_.refs_3_.refs_14_, f32[16,8192]{1,0:T(8,128)} %get-tuple-element.182.refs_4_.refs_3_, ...), custom_call_target="tpu_custom_call" | custom-call | flops 1 | bytes 1 | tf_op jit(solution)/shard_map/assemble/pallas_call | solution.py:205
  585.5 5.6 collective-permute-done.110.refs_6_
  591.1 4.8 collective-permute-done.111.refs_7_
  596.7 9.1 %assemble.15 = (f32[32,8192]{1,0:T(8,128)}, f32[32,128]{1,0:T(8,128)}) custom-call(f32[8,8192]{1,0:T(8,128)} %get-tuple-element.231.refs_0_, f32[8,8192]{1,0:T(8,128)} %get-tuple-element.232.refs_1_, f32[8,8192]{1,0:T(8,128)} %get-tuple-element.233.refs_2_, f32[8,8192]{1,0:T(8,128)} %get-tuple-element.234.refs_3_, f32[8,8192]{1,0:T(8,128)} %copy-done.107, ...), custom_call_target="tpu_custom_call" | custom-call | flops 1 | bytes 1 | tf_op jit(solution)/shard_map/assemble/pallas_call | solution.py:205
  614.1 3.6 collective-permute-start.115
  617.8 2.6 collective-permute-done.115.refs_1_
  621.3 3.6 maximum_divide_fusion
  (519 shorter events, 185.3 us)
Async XLA Ops:
  5.2 49.1 %collective-permute-start = (f32[32,16384]{1,0:T(8,128)}, f32[32,16384]{1,0:T(8,128)}, u32[]{:S(2)}, u32[]{:S(2)}) collective-permute-start(f32[32,16384]{1,0:T(8,128)} %get-tuple-element.125.refs_2_), channel_id=1, source_target_pairs={{0,2},{1,3},{2,0},{3,1},{4,6},{5,7},{6,4},{7,5},{8,10},{9,11},{10,... | collective-permute-start | bytes 6291464 | tf_op jit(solution)/shard_map/ppermute | solution.py:225
  54.3 7.4 %collective-permute-start.1 = (f32[32,16384]{1,0:T(8,128)}, f32[32,16384]{1,0:T(8,128)}, u32[]{:S(2)}, u32[]{:S(2)}) collective-permute-start(f32[32,16384]{1,0:T(8,128)} %get-tuple-element.125.refs_2_), channel_id=1, source_target_pairs={{0,1},{1,0},{2,3},{3,2},{4,5},{5,4},{6,7},{7,6},{8,9},{9,8},{10,11... | collective-permute-start | bytes 6291464 | tf_op jit(solution)/shard_map/ppermute | solution.py:225
  54.3 7.8 %collective-permute-start.2 = (f32[32,16384]{1,0:T(8,128)}, f32[32,16384]{1,0:T(8,128)}, u32[]{:S(2)}, u32[]{:S(2)}) collective-permute-start(f32[32,16384]{1,0:T(8,128)} %collective-permute-done.refs_3_), channel_id=1, source_target_pairs={{0,1},{1,0},{2,3},{3,2},{4,5},{5,4},{6,7},{7,6},{8,9},{9,8},{10,11... | collective-permute-start | bytes 6291464 | tf_op jit(solution)/shard_map/ppermute | solution.py:225
  54.8 78.1 %collective-permute-start.14 = (f32[32,16384]{1,0:T(8,128)}, f32[32,16384]{1,0:T(8,128)}, u32[]{:S(2)}, u32[]{:S(2)}) collective-permute-start(f32[32,16384]{1,0:T(8,128)} %get-tuple-element.135.refs_3_.refs_2_), channel_id=1, source_target_pairs={{0,2},{1,3},{2,0},{3,1},{4,6},{5,7},{6,4},{7,5},{8,10},{9,11},{10,... | collective-permute-start | bytes 6291464 | tf_op jit(solution)/shard_map/ppermute | solution.py:225
  58.6 20.2 %collective-permute-start.3 = (f32[96,1024]{1,0:T(8,128)S(1)}, f32[96,1024]{1,0:T(8,128)S(1)}, u32[]{:S(2)}, u32[]{:S(2)}) collective-permute-start(f32[96,1024]{1,0:T(8,128)S(1)} %get-tuple-element.128), channel_id=1, source_target_pairs={{0,4},{4,0},{8,12},{12,8},{16,20},{20,16},{24,28},{28,24},{1,5},{5... | collective-permute-start | bytes 1179656 | tf_op jit(solution)/shard_map/ppermute | solution.py:225
  60.1 18.7 %collective-permute-start.4 = (f32[96,1024]{1,0:T(8,128)S(1)}, f32[96,1024]{1,0:T(8,128)S(1)}, u32[]{:S(2)}, u32[]{:S(2)}) collective-permute-start(f32[96,1024]{1,0:T(8,128)S(1)} %get-tuple-element.129), channel_id=1, source_target_pairs={{0,8},{4,12},{8,0},{12,4},{16,24},{20,28},{24,16},{28,20},{1,9},{5... | collective-permute-start | bytes 1179656 | tf_op jit(solution)/shard_map/ppermute | solution.py:225
  61.7 17.3 %collective-permute-start.5 = (f32[96,1024]{1,0:T(8,128)S(1)}, f32[96,1024]{1,0:T(8,128)S(1)}, u32[]{:S(2)}, u32[]{:S(2)}) collective-permute-start(f32[96,1024]{1,0:T(8,128)S(1)} %get-tuple-element.130), channel_id=1, source_target_pairs={{0,12},{4,8},{8,4},{12,0},{16,28},{20,24},{24,20},{28,16},{1,13},{... | collective-permute-start | bytes 1179656 | tf_op jit(solution)/shard_map/ppermute | solution.py:225
  80.1 20.0 %collective-permute-start.6 = (f32[96,1024]{1,0:T(8,128)S(1)}, f32[96,1024]{1,0:T(8,128)S(1)}, u32[]{:S(2)}, u32[]{:S(2)}) collective-permute-start(f32[96,1024]{1,0:T(8,128)S(1)} %total.16.refs_9_.refs_0_), channel_id=1, source_target_pairs={{0,16},{4,20},{8,24},{12,28},{16,0},{20,4},{24,8},{28,12},{1,17},{... | collective-permute-start | bytes 1179656 | tf_op jit(solution)/shard_map/ppermute | solution.py:225
  113.2 9.2 %collective-permute-start.10 = (f32[32,1152]{1,0:T(8,128)S(1)}, f32[32,1152]{1,0:T(8,128)S(1)}, u32[]{:S(2)}, u32[]{:S(2)}) collective-permute-start(f32[32,1152]{1,0:T(8,128)S(1)} %total.18.refs_0_), channel_id=1, source_target_pairs={{0,16},{4,20},{8,24},{12,28},{16,0},{20,4},{24,8},{28,12},{1,17},{... | collective-permute-start | bytes 442376 | tf_op jit(solution)/shard_map/ppermute | solution.py:225
  124.6 7.5 %collective-permute-start.13 = (f32[32,1152]{1,0:T(8,128)S(1)}, f32[32,1152]{1,0:T(8,128)S(1)}, u32[]{:S(2)}, u32[]{:S(2)}) collective-permute-start(f32[32,1152]{1,0:T(8,128)S(1)} %total.19.refs_1_), channel_id=1, source_target_pairs={{0,12},{4,8},{8,4},{12,0},{16,28},{20,24},{24,20},{28,16},{1,13},{... | collective-permute-start | bytes 442376 | tf_op jit(solution)/shard_map/ppermute | solution.py:225
  133.0 7.4 %collective-permute-start.16 = (f32[32,16384]{1,0:T(8,128)}, f32[32,16384]{1,0:T(8,128)S(1)}, u32[]{:S(2)}, u32[]{:S(2)}) collective-permute-start(f32[32,16384]{1,0:T(8,128)} %collective-permute-done.14.refs_4_.refs_3_), channel_id=1, source_target_pairs={{0,1},{1,0},{2,3},{3,2},{4,5},{5,4},{6,7},{7,6},{8,9},{9,8},{10,11... | collective-permute-start | bytes 6291464 | tf_op jit(solution)/shard_map/ppermute | solution.py:225
  133.5 33.1 %collective-permute-start.21 = (f32[96,1024]{1,0:T(8,128)S(1)}, f32[96,1024]{1,0:T(8,128)S(1)}, u32[]{:S(2)}, u32[]{:S(2)}) collective-permute-start(f32[96,1024]{1,0:T(8,128)S(1)} %total.17.refs_2_.refs_1_), channel_id=1, source_target_pairs={{0,4},{4,0},{8,12},{12,8},{16,20},{20,16},{24,28},{28,24},{1,5},{5... | collective-permute-start | bytes 1179656 | tf_op jit(solution)/shard_map/ppermute | solution.py:225
  134.5 32.2 %collective-permute-start.22 = (f32[96,1024]{1,0:T(8,128)S(1)}, f32[96,1024]{1,0:T(8,128)S(1)}, u32[]{:S(2)}, u32[]{:S(2)}) collective-permute-start(f32[96,1024]{1,0:T(8,128)S(1)} %total.17.refs_2_.refs_1_), channel_id=1, source_target_pairs={{0,8},{4,12},{8,0},{12,4},{16,24},{20,28},{24,16},{28,20},{1,9},{5... | collective-permute-start | bytes 1179656 | tf_op jit(solution)/shard_map/ppermute | solution.py:225
  135.9 31.2 %collective-permute-start.23 = (f32[96,1024]{1,0:T(8,128)S(1)}, f32[96,1024]{1,0:T(8,128)S(1)}, u32[]{:S(2)}, u32[]{:S(2)}) collective-permute-start(f32[96,1024]{1,0:T(8,128)S(1)} %total.17.refs_2_.refs_1_), channel_id=1, source_target_pairs={{0,12},{4,8},{8,4},{12,0},{16,28},{20,24},{24,20},{28,16},{1,13},{... | collective-permute-start | bytes 1179656 | tf_op jit(solution)/shard_map/ppermute | solution.py:225
  166.0 9.9 %collective-permute-start.17 = (f32[16,8192]{1,0:T(8,128)}, f32[16,8192]{1,0:T(8,128)S(1)}, u32[]{:S(2)}, u32[]{:S(2)}) collective-permute-start(f32[16,8192]{1,0:T(8,128)} %get-tuple-element.139), channel_id=1, source_target_pairs={{0,1},{1,0},{2,3},{3,2},{4,5},{5,4},{6,7},{7,6},{8,9},{9,8},{10,11... | collective-permute-start | bytes 1572872 | tf_op jit(solution)/shard_map/ppermute | solution.py:225
  166.2 9.7 %collective-permute-start.18 = (f32[16,8192]{1,0:T(8,128)}, f32[16,8192]{1,0:T(8,128)S(1)}, u32[]{:S(2)}, u32[]{:S(2)}) collective-permute-start(f32[16,8192]{1,0:T(8,128)} %get-tuple-element.140), channel_id=1, source_target_pairs={{0,1},{1,0},{2,3},{3,2},{4,5},{5,4},{6,7},{7,6},{8,9},{9,8},{10,11... | collective-permute-start | bytes 1572872 | tf_op jit(solution)/shard_map/ppermute | solution.py:225
  166.6 9.4 %collective-permute-start.19 = (f32[16,8192]{1,0:T(8,128)}, f32[16,8192]{1,0:T(8,128)S(1)}, u32[]{:S(2)}, u32[]{:S(2)}) collective-permute-start(f32[16,8192]{1,0:T(8,128)} %get-tuple-element.141), channel_id=1, source_target_pairs={{0,1},{1,0},{2,3},{3,2},{4,5},{5,4},{6,7},{7,6},{8,9},{9,8},{10,11... | collective-permute-start | bytes 1572872 | tf_op jit(solution)/shard_map/ppermute | solution.py:225
  166.7 9.3 %collective-permute-start.20 = (f32[16,8192]{1,0:T(8,128)}, f32[16,8192]{1,0:T(8,128)S(1)}, u32[]{:S(2)}, u32[]{:S(2)}) collective-permute-start(f32[16,8192]{1,0:T(8,128)} %get-tuple-element.142), channel_id=1, source_target_pairs={{0,1},{1,0},{2,3},{3,2},{4,5},{5,4},{6,7},{7,6},{8,9},{9,8},{10,11... | collective-permute-start | bytes 1572872 | tf_op jit(solution)/shard_map/ppermute | solution.py:225
  180.5 48.8 %collective-permute-start.30 = (f32[64,8192]{1,0:T(8,128)}, f32[64,8192]{1,0:T(8,128)S(1)}, u32[]{:S(2)}, u32[]{:S(2)}) collective-permute-start(f32[64,8192]{1,0:T(8,128)} %joined.8.refs_10_.refs_0_), channel_id=1, source_target_pairs={{0,2},{1,3},{2,0},{3,1},{4,6},{5,7},{6,4},{7,5},{8,10},{9,11},{10,... | collective-permute-start | bytes 6291464 | tf_op jit(solution)/shard_map/ppermute | solution.py:225
  214.8 68.0 %collective-permute-start.38 = (f32[64,8192]{1,0:T(8,128)}, f32[64,8192]{1,0:T(8,128)S(1)}, u32[]{:S(2)}, u32[]{:S(2)}) collective-permute-start(f32[64,8192]{1,0:T(8,128)} %joined.9.refs_8_.refs_0_), channel_id=1, source_target_pairs={{0,2},{1,3},{2,0},{3,1},{4,6},{5,7},{6,4},{7,5},{8,10},{9,11},{10,... | collective-permute-start | bytes 6291464 | tf_op jit(solution)/shard_map/ppermute | solution.py:225
  217.8 7.5 %collective-permute-start.28 = (f32[32,1152]{1,0:T(8,128)S(1)}, f32[32,1152]{1,0:T(8,128)S(1)}, u32[]{:S(2)}, u32[]{:S(2)}) collective-permute-start(f32[32,1152]{1,0:T(8,128)S(1)} %get-tuple-element.149), channel_id=1, source_target_pairs={{0,12},{4,8},{8,4},{12,0},{16,28},{20,24},{24,20},{28,16},{1,13},{... | collective-permute-start | bytes 442376 | tf_op jit(solution)/shard_map/ppermute | solution.py:225
  225.4 15.0 %collective-permute-start.29 = (f32[32,1152]{1,0:T(8,128)S(1)}, f32[32,1152]{1,0:T(8,128)S(1)}, u32[]{:S(2)}, u32[]{:S(2)}) collective-permute-start(f32[32,1152]{1,0:T(8,128)S(1)} %total.21.refs_7_.refs_0_), channel_id=1, source_target_pairs={{0,16},{4,20},{8,24},{12,28},{16,0},{20,4},{24,8},{28,12},{1,17},{... | collective-permute-start | bytes 442376 | tf_op jit(solution)/shard_map/ppermute | solution.py:225
  253.8 28.2 %collective-permute-start.52 = (f32[64,384]{1,0:T(8,128)S(1)}, f32[64,384]{1,0:T(8,128)S(1)}, u32[]{:S(2)}, u32[]{:S(2)}) collective-permute-start(f32[64,384]{1,0:T(8,128)S(1)} %total.23.refs_0_), channel_id=1, source_target_pairs={{0,2},{1,3},{2,0},{3,1},{4,6},{5,7},{6,4},{7,5},{8,10},{9,11},{10,... | collective-permute-start | bytes 294920 | tf_op jit(solution)/shard_map/ppermute | solution.py:225
  281.1 12.5 %collective-permute-start.47 = (f32[16,8192]{1,0:T(8,128)}, f32[16,8192]{1,0:T(8,128)S(1)}, u32[]{:S(2)}, u32[]{:S(2)}) collective-permute-start(f32[16,8192]{1,0:T(8,128)} %get-tuple-element.166), channel_id=1, source_target_pairs={{0,1},{1,0},{2,3},{3,2},{4,5},{5,4},{6,7},{7,6},{8,9},{9,8},{10,11... | collective-permute-start | bytes 1572872 | tf_op jit(solution)/shard_map/ppermute | solution.py:225
  281.5 12.0 %collective-permute-start.48 = (f32[16,8192]{1,0:T(8,128)}, f32[16,8192]{1,0:T(8,128)S(1)}, u32[]{:S(2)}, u32[]{:S(2)}) collective-permute-start(f32[16,8192]{1,0:T(8,128)} %get-tuple-element.167), channel_id=1, source_target_pairs={{0,1},{1,0},{2,3},{3,2},{4,5},{5,4},{6,7},{7,6},{8,9},{9,8},{10,11... | collective-permute-start | bytes 1572872 | tf_op jit(solution)/shard_map/ppermute | solution.py:225
  281.6 11.9 %collective-permute-start.49 = (f32[16,8192]{1,0:T(8,128)}, f32[16,8192]{1,0:T(8,128)S(1)}, u32[]{:S(2)}, u32[]{:S(2)}) collective-permute-start(f32[16,8192]{1,0:T(8,128)} %get-tuple-element.168), channel_id=1, source_target_pairs={{0,1},{1,0},{2,3},{3,2},{4,5},{5,4},{6,7},{7,6},{8,9},{9,8},{10,11... | collective-permute-start | bytes 1572872 | tf_op jit(solution)/shard_map/ppermute | solution.py:225
  282.0 11.6 %collective-permute-start.50 = (f32[16,8192]{1,0:T(8,128)}, f32[16,8192]{1,0:T(8,128)S(1)}, u32[]{:S(2)}, u32[]{:S(2)}) collective-permute-start(f32[16,8192]{1,0:T(8,128)} %get-tuple-element.169), channel_id=1, source_target_pairs={{0,1},{1,0},{2,3},{3,2},{4,5},{5,4},{6,7},{7,6},{8,9},{9,8},{10,11... | collective-permute-start | bytes 1572872 | tf_op jit(solution)/shard_map/ppermute | solution.py:225
  298.3 48.7 %collective-permute-start.57 = (f32[64,8192]{1,0:T(8,128)}, f32[64,8192]{1,0:T(8,128)S(1)}, u32[]{:S(2)}, u32[]{:S(2)}) collective-permute-start(f32[64,8192]{1,0:T(8,128)} %joined.10.refs_15_.refs_0_), channel_id=1, source_target_pairs={{0,2},{1,3},{2,0},{3,1},{4,6},{5,7},{6,4},{7,5},{8,10},{9,11},{10,... | collective-permute-start | bytes 6291464 | tf_op jit(solution)/shard_map/ppermute | solution.py:225
  331.7 8.1 %collective-permute-start.53 = (f32[32,1152]{1,0:T(8,128)S(1)}, f32[32,1152]{1,0:T(8,128)S(1)}, u32[]{:S(2)}, u32[]{:S(2)}) collective-permute-start(f32[32,1152]{1,0:T(8,128)S(1)} %get-tuple-element.173), channel_id=1, source_target_pairs={{0,4},{4,0},{8,12},{12,8},{16,20},{20,16},{24,28},{28,24},{1,5},{5... | collective-permute-start | bytes 442376 | tf_op jit(solution)/shard_map/ppermute | solution.py:225
  334.0 8.1 %collective-permute-start.55 = (f32[32,1152]{1,0:T(8,128)S(1)}, f32[32,1152]{1,0:T(8,128)S(1)}, u32[]{:S(2)}, u32[]{:S(2)}) collective-permute-start(f32[32,1152]{1,0:T(8,128)S(1)} %get-tuple-element.175), channel_id=1, source_target_pairs={{0,12},{4,8},{8,4},{12,0},{16,28},{20,24},{24,20},{28,16},{1,13},{... | collective-permute-start | bytes 442376 | tf_op jit(solution)/shard_map/ppermute | solution.py:225
  339.4 93.1 %collective-permute-start.76 = (f32[64,8192]{1,0:T(8,128)}, f32[64,8192]{1,0:T(8,128)S(1)}, u32[]{:S(2)}, u32[]{:S(2)}) collective-permute-start(f32[64,8192]{1,0:T(8,128)} %joined.11.refs_8_.refs_0_), channel_id=1, source_target_pairs={{0,2},{1,3},{2,0},{3,1},{4,6},{5,7},{6,4},{7,5},{8,10},{9,11},{10,... | collective-permute-start | bytes 6291464 | tf_op jit(solution)/shard_map/ppermute | solution.py:225
  342.1 15.6 %collective-permute-start.56 = (f32[32,1152]{1,0:T(8,128)S(1)}, f32[32,1152]{1,0:T(8,128)S(1)}, u32[]{:S(2)}, u32[]{:S(2)}) collective-permute-start(f32[32,1152]{1,0:T(8,128)S(1)} %total.24.refs_7_.refs_0_), channel_id=1, source_target_pairs={{0,16},{4,20},{8,24},{12,28},{16,0},{20,4},{24,8},{28,12},{1,17},{... | collective-permute-start | bytes 442376 | tf_op jit(solution)/shard_map/ppermute | solution.py:225
  371.8 28.2 %collective-permute-start.74 = (f32[64,384]{1,0:T(8,128)S(1)}, f32[64,384]{1,0:T(8,128)S(1)}, u32[]{:S(2)}, u32[]{:S(2)}) collective-permute-start(f32[64,384]{1,0:T(8,128)S(1)} %total.26.refs_0_), channel_id=1, source_target_pairs={{0,2},{1,3},{2,0},{3,1},{4,6},{5,7},{6,4},{7,5},{8,10},{9,11},{10,... | collective-permute-start | bytes 294920 | tf_op jit(solution)/shard_map/ppermute | solution.py:225
  444.0 29.4 %collective-permute-start.75 = (f32[32,8192]{1,0:T(8,128)S(1)}, f32[32,8192]{1,0:T(8,128)S(1)}, u32[]{:S(2)}, u32[]{:S(2)}) collective-permute-start(f32[32,8192]{1,0:T(8,128)S(1)} %copy-done.126), channel_id=1, source_target_pairs={{0,2},{1,3},{2,0},{3,1},{4,6},{5,7},{6,4},{7,5},{8,10},{9,11},{10,... | collective-permute-start | bytes 3145736 | tf_op jit(solution)/shard_map/ppermute | solution.py:225
  445.6 46.1 %collective-permute-start.85 = (f32[32,8192]{1,0:T(8,128)S(1)}, f32[32,8192]{1,0:T(8,128)S(1)}, u32[]{:S(2)}, u32[]{:S(2)}) collective-permute-start(f32[32,8192]{1,0:T(8,128)S(1)} %copy-done.127), channel_id=1, source_target_pairs={{0,2},{1,3},{2,0},{3,1},{4,6},{5,7},{6,4},{7,5},{8,10},{9,11},{10,... | collective-permute-start | bytes 3145736 | tf_op jit(solution)/shard_map/ppermute | solution.py:225
  469.3 13.3 %collective-permute-start.86 = (f32[32,1152]{1,0:T(8,128)S(1)}, f32[32,1152]{1,0:T(8,128)S(1)}, u32[]{:S(2)}, u32[]{:S(2)}) collective-permute-start(f32[32,1152]{1,0:T(8,128)S(1)} %get-tuple-element.208), channel_id=1, source_target_pairs={{0,4},{4,0},{8,12},{12,8},{16,20},{20,16},{24,28},{28,24},{1,5},{5... | collective-permute-start | bytes 442376 | tf_op jit(solution)/shard_map/ppermute | solution.py:225
  470.0 12.6 %collective-permute-start.87 = (f32[32,1152]{1,0:T(8,128)S(1)}, f32[32,1152]{1,0:T(8,128)S(1)}, u32[]{:S(2)}, u32[]{:S(2)}) collective-permute-start(f32[32,1152]{1,0:T(8,128)S(1)} %get-tuple-element.209), channel_id=1, source_target_pairs={{0,8},{4,12},{8,0},{12,4},{16,24},{20,28},{24,16},{28,20},{1,9},{5... | collective-permute-start | bytes 442376 | tf_op jit(solution)/shard_map/ppermute | solution.py:225
  471.4 11.2 %collective-permute-start.88 = (f32[32,1152]{1,0:T(8,128)S(1)}, f32[32,1152]{1,0:T(8,128)S(1)}, u32[]{:S(2)}, u32[]{:S(2)}) collective-permute-start(f32[32,1152]{1,0:T(8,128)S(1)} %get-tuple-element.210), channel_id=1, source_target_pairs={{0,12},{4,8},{8,4},{12,0},{16,28},{20,24},{24,20},{28,16},{1,13},{... | collective-permute-start | bytes 442376 | tf_op jit(solution)/shard_map/ppermute | solution.py:225
  483.8 16.9 %collective-permute-start.89 = (f32[32,1152]{1,0:T(8,128)S(1)}, f32[32,1152]{1,0:T(8,128)S(1)}, u32[]{:S(2)}, u32[]{:S(2)}) collective-permute-start(f32[32,1152]{1,0:T(8,128)S(1)} %total.27.refs_7_.refs_0_), channel_id=1, source_target_pairs={{0,16},{4,20},{8,24},{12,28},{16,0},{20,4},{24,8},{28,12},{1,17},{... | collective-permute-start | bytes 442376 | tf_op jit(solution)/shard_map/ppermute | solution.py:225
  530.3 8.5 %collective-permute-start.93 = (f32[16,8192]{1,0:T(8,128)}, f32[16,8192]{1,0:T(8,128)S(1)}, u32[]{:S(2)}, u32[]{:S(2)}) collective-permute-start(f32[16,8192]{1,0:T(8,128)} %get-tuple-element.214), channel_id=1, source_target_pairs={{0,1},{1,0},{2,3},{3,2},{4,5},{5,4},{6,7},{7,6},{8,9},{9,8},{10,11... | collective-permute-start | bytes 1572872 | tf_op jit(solution)/shard_map/ppermute | solution.py:225
  530.3 8.5 %collective-permute-start.94 = (f32[16,8192]{1,0:T(8,128)}, f32[16,8192]{1,0:T(8,128)S(1)}, u32[]{:S(2)}, u32[]{:S(2)}) collective-permute-start(f32[16,8192]{1,0:T(8,128)} %get-tuple-element.215), channel_id=1, source_target_pairs={{0,1},{1,0},{2,3},{3,2},{4,5},{5,4},{6,7},{7,6},{8,9},{9,8},{10,11... | collective-permute-start | bytes 1572872 | tf_op jit(solution)/shard_map/ppermute | solution.py:225
  530.8 8.0 %collective-permute-start.95 = (f32[16,8192]{1,0:T(8,128)}, f32[16,8192]{1,0:T(8,128)S(1)}, u32[]{:S(2)}, u32[]{:S(2)}) collective-permute-start(f32[16,8192]{1,0:T(8,128)} %get-tuple-element.216), channel_id=1, source_target_pairs={{0,1},{1,0},{2,3},{3,2},{4,5},{5,4},{6,7},{7,6},{8,9},{9,8},{10,11... | collective-permute-start | bytes 1572872 | tf_op jit(solution)/shard_map/ppermute | solution.py:225
  530.8 8.0 %collective-permute-start.96 = (f32[16,8192]{1,0:T(8,128)}, f32[16,8192]{1,0:T(8,128)S(1)}, u32[]{:S(2)}, u32[]{:S(2)}) collective-permute-start(f32[16,8192]{1,0:T(8,128)} %get-tuple-element.217), channel_id=1, source_target_pairs={{0,1},{1,0},{2,3},{3,2},{4,5},{5,4},{6,7},{7,6},{8,9},{9,8},{10,11... | collective-permute-start | bytes 1572872 | tf_op jit(solution)/shard_map/ppermute | solution.py:225
  543.4 31.9 %collective-permute-start.99 = (f32[32,8192]{1,0:T(8,128)}, f32[32,8192]{1,0:T(8,128)S(1)}, u32[]{:S(2)}, u32[]{:S(2)}) collective-permute-start(f32[32,8192]{1,0:T(8,128)} %get-tuple-element.220), channel_id=1, source_target_pairs={{0,2},{1,3},{2,0},{3,1},{4,6},{5,7},{6,4},{7,5},{8,10},{9,11},{10,... | collective-permute-start | bytes 3145736 | tf_op jit(solution)/shard_map/ppermute | solution.py:225
  570.4 14.0 %collective-permute-start.108 = (f32[8,8192]{1,0:T(8,128)}, f32[8,8192]{1,0:T(8,128)S(1)}, u32[]{:S(2)}, u32[]{:S(2)}) collective-permute-start(f32[8,8192]{1,0:T(8,128)} %get-tuple-element.235), channel_id=1, source_target_pairs={{0,2},{1,3},{2,0},{3,1},{4,6},{5,7},{6,4},{7,5},{8,10},{9,11},{10,... | collective-permute-start | bytes 786440 | tf_op jit(solution)/shard_map/ppermute | solution.py:225
  570.9 14.5 %collective-permute-start.109 = (f32[8,8192]{1,0:T(8,128)}, f32[8,8192]{1,0:T(8,128)S(1)}, u32[]{:S(2)}, u32[]{:S(2)}) collective-permute-start(f32[8,8192]{1,0:T(8,128)} %get-tuple-element.236), channel_id=1, source_target_pairs={{0,2},{1,3},{2,0},{3,1},{4,6},{5,7},{6,4},{7,5},{8,10},{9,11},{10,... | collective-permute-start | bytes 786440 | tf_op jit(solution)/shard_map/ppermute | solution.py:225
  572.5 18.6 %collective-permute-start.110 = (f32[8,8192]{1,0:T(8,128)}, f32[8,8192]{1,0:T(8,128)S(1)}, u32[]{:S(2)}, u32[]{:S(2)}) collective-permute-start(f32[8,8192]{1,0:T(8,128)} %get-tuple-element.237), channel_id=1, source_target_pairs={{0,2},{1,3},{2,0},{3,1},{4,6},{5,7},{6,4},{7,5},{8,10},{9,11},{10,... | collective-permute-start | bytes 786440 | tf_op jit(solution)/shard_map/ppermute | solution.py:225
  573.0 23.0 %collective-permute-start.111 = (f32[8,8192]{1,0:T(8,128)}, f32[8,8192]{1,0:T(8,128)S(1)}, u32[]{:S(2)}, u32[]{:S(2)}) collective-permute-start(f32[8,8192]{1,0:T(8,128)} %get-tuple-element.238), channel_id=1, source_target_pairs={{0,2},{1,3},{2,0},{3,1},{4,6},{5,7},{6,4},{7,5},{8,10},{9,11},{10,... | collective-permute-start | bytes 786440 | tf_op jit(solution)/shard_map/ppermute | solution.py:225
  (198 other events, 844.0 us)
